TPU v7x, 32 devices: a whole 2x2x4 slice. The times are simulated.
32 devices in a mesh: ctx: 16 (over z, y, x), round: 2 (over core).
Axes of the slice: x: 2, y: 2, z: 4, core: 2. Of those that a mesh axis runs over, the one named last changes fastest.
Arguments:
- x2: bfloat16 [4096, 1024], P('ctx'), may hold values from -16 to 16
- out_grad: bfloat16 [4096, 1024], P('ctx'), may hold values from -6 to 6
- w_qk: bfloat16 [1024, 1024], replicated, may hold values from -0.3125 to 0.3125
- w_v: bfloat16 [1024, 1024], replicated, may hold values from -0.1875 to 0.1875
- sort_slot: int32 [2, 4096], P(None, 'ctx'), may hold values from 0 to 4095, as said below
- source_pos: int32 [2, 4096], P('round', 'ctx'), may hold values from 0 to 4095, as said below
Outputs:
- grad_x2: bfloat16 [4096, 1024], P(('ctx', 'round'))
- grad_w_qk: float32 [1024, 1024], P(('ctx', 'round'))
- grad_w_v: float32 [1024, 1024], P(('ctx', 'round'))
Inputs may be any that keep to these rules, and one draw needn't show every extreme that they name: `sort_slot`: for each round a permutation of the positions. Of the 256 positions k * 256 to (k + 1) * 256 - 1, at most 32 have sorted positions in any one range j * 256 to (j + 1) * 256 - 1 in one round, and in every round some pair of ranges reaches 32. For each round the inverse permutation of sort_slot: sort_slot[r, source_pos[r, s]] = s.
All inputs are finite; a program needn't handle non-finite values.
Results may differ from a plain program's by a relative error of at most 0.013.
The roundings to bfloat16 on the way count: a program that leaves them out, or rounds other values in their place, can miss the bound.
Values may be sent and summed in bfloat16 or wider, within the bound.
No kernel may reach another device: no remote copies, remote signals or barrier semaphores. Data moves between devices by JAX's collectives and lax.ppermute only.
A program may use at most 128 MiB of HBM per device.

v0:
```python
import jax
import jax.numpy as jnp
from jax import lax
from jax.sharding import PartitionSpec as P

HEADS = 16
SPAN = 256


masked_score = -1000000000.0


def from_behind(block, axis, distance):
    devices = range(lax.axis_size(axis))
    route = [((i - distance) % len(devices), i) for i in devices]
    return lax.ppermute(block, axis, route)


def ordinal(group, order):
    same = group[:, None] == group[None, :]
    before = order[None, :] < order[:, None]
    return jnp.sum((same & before).astype(jnp.int32), axis=1)


def token_routes(slots, tdev, cap, paired, hround):
    owner = slots // tdev
    target = owner * 2 + hround if paired else owner
    return target * cap + ordinal(owner, jnp.arange(slots.shape[0], dtype=jnp.int32))


def slot_routes(sources, tdev, cap, paired):
    if paired:
        group = sources // tdev * 2 + sources % tdev // (tdev // 2)
    else:
        group = sources // tdev
    return group * cap + ordinal(group, sources)


def place_rows(rows, index, total):
    return jnp.zeros((total,) + rows.shape[1:], rows.dtype).at[index].set(rows)


def per_device(x2, out_grad, w_qk, w_v, sort_slot, source_pos):
    tdev, width = x2.shape
    half = tdev // 2
    peers = lax.axis_size("ctx")
    cap = 2 * tdev // peers
    head_dim = width // HEADS
    scale = head_dim ** (-0.5)
    nblocks = tdev // SPAN
    hround = lax.axis_index("round")
    sources = source_pos[0]
    own_slots = lax.dynamic_index_in_dim(sort_slot, hround, 0, keepdims=False)
    half_slots = lax.dynamic_slice_in_dim(sort_slot, hround * half, half, 1)
    back_index = [
        token_routes(half_slots[0], tdev, cap, True, 0),
        token_routes(half_slots[1], tdev, cap, True, 1),
    ]
    slot_index = slot_routes(sources, tdev, cap, True)
    send_index = token_routes(own_slots, tdev, cap, False, 0)
    recv_index = slot_routes(sources, tdev, cap, False)
    x_half = lax.dynamic_slice_in_dim(x2, hround * half, half, 0)
    grad_half = lax.dynamic_slice_in_dim(out_grad, hround * half, half, 0)
    paired_rows = 2 * peers * cap
    qk = jnp.dot(x2, w_qk, preferred_element_type=jnp.float32).astype(jnp.bfloat16)
    val = jnp.dot(x2, w_v, preferred_element_type=jnp.float32).astype(jnp.bfloat16)
    sent_q = place_rows(qk, send_index, peers * cap)
    sent_v = place_rows(val, send_index, peers * cap)
    sent_g = place_rows(out_grad, send_index, peers * cap)
    got_q, got_v, got_g = (
        lax.all_to_all(sent_q, "ctx", split_axis=0, concat_axis=0, tiled=True),
        lax.all_to_all(sent_v, "ctx", split_axis=0, concat_axis=0, tiled=True),
        lax.all_to_all(sent_g, "ctx", split_axis=0, concat_axis=0, tiled=True),
    )
    q_sorted = got_q[recv_index]
    v_sorted = got_v[recv_index]
    g_sorted = got_g[recv_index]
    prev_q, prev_v = from_behind((q_sorted, v_sorted), "ctx", 1)

    def blocks_of(rows):
        return rows.reshape(rows.shape[0] // SPAN, SPAN, HEADS, head_dim)

    q_blocks = blocks_of(q_sorted)
    g_blocks = blocks_of(g_sorted)
    q_ext = blocks_of(jnp.concatenate([prev_q, q_sorted], axis=0))
    v_ext = blocks_of(jnp.concatenate([prev_v, v_sorted], axis=0))
    k_blocks = jnp.concatenate([q_ext[:-1], q_ext[1:]], axis=1)
    v_blocks = jnp.concatenate([v_ext[:-1], v_ext[1:]], axis=1)
    scores = (
        jnp.einsum("mqhd,mkhd->mhqk", q_blocks, k_blocks, preferred_element_type=jnp.float32)
        * scale
    )
    selfpos = jnp.arange(2 * SPAN)[None, :] == jnp.arange(SPAN)[:, None] + SPAN
    scores = jnp.where(selfpos[None, None], masked_score, scores)
    top = jnp.max(scores, axis=3, keepdims=True)
    lse = top + jnp.log(jnp.sum(jnp.exp(scores - top), axis=3, keepdims=True))
    probs = jnp.exp(scores - lse).astype(jnp.bfloat16)
    out_sorted = jnp.einsum(
        "mhqk,mkhd->mqhd", probs, v_blocks, preferred_element_type=jnp.float32
    ).reshape(tdev, width)
    lse_sorted = jnp.transpose(lse[..., 0], (0, 2, 1)).reshape(tdev, HEADS)
    sent_out = place_rows(out_sorted, slot_index, paired_rows)
    sent_lse = place_rows(lse_sorted, slot_index, paired_rows)
    got_out, got_lse = (
        lax.all_to_all(sent_out, ("ctx", "round"), split_axis=0, concat_axis=0, tiled=True),
        lax.all_to_all(sent_lse, ("ctx", "round"), split_axis=0, concat_axis=0, tiled=True),
    )
    lse_zero = got_lse[back_index[0]]
    lse_one = got_lse[back_index[1]]
    peak = jnp.maximum(lse_zero, lse_one)
    total = peak + jnp.log(jnp.exp(lse_zero - peak) + jnp.exp(lse_one - peak))
    attended = jnp.exp(lse_zero - total)[:, :, None] * got_out[back_index[0]].reshape(
        half, HEADS, head_dim
    )
    attended = attended + jnp.exp(lse_one - total)[:, :, None] * got_out[back_index[1]].reshape(
        half, HEADS, head_dim
    )
    delta = jnp.sum(grad_half.astype(jnp.float32).reshape(half, HEADS, head_dim) * attended, axis=2)
    total_buf = place_rows(total, back_index[0], paired_rows).at[back_index[1]].set(total)
    delta_buf = place_rows(delta, back_index[0], paired_rows).at[back_index[1]].set(delta)
    got_total, got_delta = (
        lax.all_to_all(total_buf, ("ctx", "round"), split_axis=0, concat_axis=0, tiled=True),
        lax.all_to_all(delta_buf, ("ctx", "round"), split_axis=0, concat_axis=0, tiled=True),
    )
    total_blocks = jnp.transpose(got_total[slot_index].reshape(nblocks, SPAN, HEADS), (0, 2, 1))[
        ..., None
    ]
    delta_blocks = jnp.transpose(got_delta[slot_index].reshape(nblocks, SPAN, HEADS), (0, 2, 1))[
        ..., None
    ]
    weights = jnp.exp(scores - total_blocks)
    grad_val = jnp.einsum(
        "mhqk,mqhd->mkhd",
        weights.astype(jnp.bfloat16),
        g_blocks,
        preferred_element_type=jnp.float32,
    )
    inner = jnp.einsum("mqhd,mkhd->mhqk", g_blocks, v_blocks, preferred_element_type=jnp.float32)
    dscore = (weights * (inner - delta_blocks)).astype(jnp.bfloat16)
    grad_q = (
        jnp.einsum("mhqk,mkhd->mqhd", dscore, k_blocks, preferred_element_type=jnp.float32) * scale
    )
    grad_k = (
        jnp.einsum("mhqk,mqhd->mkhd", dscore, q_blocks, preferred_element_type=jnp.float32) * scale
    )
    empty = jnp.zeros((nblocks + 1, SPAN, HEADS, head_dim), jnp.float32)
    key_grad = empty.at[:-1].add(grad_k[:, :SPAN]).at[1:].add(grad_k[:, SPAN:])
    val_grad = empty.at[:-1].add(grad_val[:, :SPAN]).at[1:].add(grad_val[:, SPAN:])
    back_k, back_v = (
        from_behind(key_grad[0].astype(jnp.bfloat16), "ctx", -1).astype(jnp.float32),
        from_behind(val_grad[0].astype(jnp.bfloat16), "ctx", -1).astype(jnp.float32),
    )
    key_rest = key_grad[1:].reshape(tdev, width).at[-SPAN:].add(back_k.reshape(SPAN, width))
    val_rest = val_grad[1:].reshape(tdev, width).at[-SPAN:].add(back_v.reshape(SPAN, width))
    dqk_sorted = (grad_q.reshape(tdev, width) + key_rest).astype(jnp.bfloat16)
    dv_sorted = val_rest.astype(jnp.bfloat16)
    sent_dq = place_rows(dqk_sorted, slot_index, paired_rows)
    sent_dv = place_rows(dv_sorted, slot_index, paired_rows)
    got_dq, got_dv = (
        lax.all_to_all(sent_dq, ("ctx", "round"), split_axis=0, concat_axis=0, tiled=True),
        lax.all_to_all(sent_dv, ("ctx", "round"), split_axis=0, concat_axis=0, tiled=True),
    )
    grad_pairs = [
        (got_dq[back_index[0]], got_dv[back_index[0]]),
        (got_dq[back_index[1]], got_dv[back_index[1]]),
    ]
    grad_sum = jnp.zeros((half, width), jnp.float32)
    for grad_qk_r, grad_v_r in grad_pairs:
        grad_sum = grad_sum + jnp.dot(grad_qk_r, w_qk.T, preferred_element_type=jnp.float32)
        grad_sum = grad_sum + jnp.dot(grad_v_r, w_v.T, preferred_element_type=jnp.float32)
    grad_x = grad_sum.astype(jnp.bfloat16)
    rows_each = width // (2 * peers)
    qk_part = jnp.zeros((rows_each * lax.axis_size(("ctx", "round")), width), jnp.float32)
    v_part = jnp.zeros((rows_each * lax.axis_size(("ctx", "round")), width), jnp.float32)
    for grad_qk_r, grad_v_r in grad_pairs:
        qk_part = qk_part + lax.dot_general(
            x_half, grad_qk_r, (((0,), (0,)), ((), ())), preferred_element_type=jnp.float32
        )
        v_part = v_part + lax.dot_general(
            x_half, grad_v_r, (((0,), (0,)), ((), ())), preferred_element_type=jnp.float32
        )
    summed = lax.psum_scatter(
        jnp.concatenate([qk_part, v_part], axis=1),
        ("ctx", "round"),
        scatter_dimension=0,
        tiled=True,
    )
    weight_scale = (tdev * peers) ** (-0.5)
    return (grad_x, summed[:, :width] * weight_scale, summed[:, width:] * weight_scale)


def solution(mesh):
    placed = (P("ctx", None), P("ctx", None), P(), P(), P(None, "ctx"), P("round", "ctx"))
    return jax.shard_map(
        per_device,
        mesh=mesh,
        in_specs=placed,
        out_specs=(P(("ctx", "round"), None), P(("ctx", "round"), None), P(("ctx", "round"), None)),
        check_vma=False,
    )
```

profile of v0, /device:TPU:0, one launch (start us, length us, event | category | flops | bytes accessed | tf_op | source)
XLA Modules:
  0.0 633.2 jit_solution(2025844279390918794)
XLA Ops:
  11.4 1.8 convolution_convert_fusion.1
  13.2 2.6 scatter_custom_fusion
  15.8 8.3 %all-to-all-start = ((bf16[16,32,1024]{2,1,0:T(8,128)(2,1)}), bf16[16,32,1024]{2,1,0:T(8,128)(2,1)S(1)}, u32[]{:S(2)}, u32[]{:S(2)}) async-start(bf16[16,32,1024]{2,1,0:T(8,128)(2,1)} %bitcast.222), calls=%async_computation | async-start | bytes 2097152 | tf_op jit(solution)/shard_map/all_to_all | solution.py:71
  24.1 3.3 convolution_convert_fusion
  27.4 3.2 scatter_custom_fusion.5
  30.6 17.9 %all-to-all-done = bf16[16,32,1024]{2,1,0:T(8,128)(2,1)S(1)} async-done(((bf16[16,32,1024]{2,1,0:T(8,128)(2,1)}), bf16[16,32,1024]{2,1,0:T(8,128)(2,1)S(1)}, u32[]{:S(2)}, u32[]{:S(2)}) %all-to-all-start) | async-done | bytes 1048608 | tf_op jit(solution)/shard_map/all_to_all | solution.py:71
  49.5 5.8 all-to-all-start.4
  55.4 3.7 gather_fusion
  59.1 1.9 collective-permute-start
  61.2 2.1 copy.139
  63.3 24.9 %collective-permute-done = bf16[256,1024]{1,0:T(8,128)(2,1)} collective-permute-done((bf16[256,1024]{1,0:T(8,128)(2,1)}, bf16[256,1024]{1,0:T(8,128)(2,1)}, u32[]{:S(2)}, u32[]{:S(2)}) %collective-permute-start) | collective-permute-done | bytes 524320 | tf_op jit(solution)/shard_map/ppermute | solution.py:16
  88.1 2.1 copy.138
  90.2 3.1 fusion.1
  93.3 2.1 exponential_reduce_fusion
  96.6 1.9 scatter_custom_fusion.1
  100.6 5.7 all-to-all-start.1
  106.3 3.2 scatter_custom_fusion.4
  109.6 4.2 all-to-all-done.1
  113.7 3.7 all-to-all-start.3
  118.1 3.9 gather_fusion.5
  122.0 1.8 collective-permute-start.1
  125.2 2.0 copy.155
  127.2 25.0 %collective-permute-done.1 = bf16[256,1024]{1,0:T(8,128)(2,1)} collective-permute-done((bf16[256,1024]{1,0:T(8,128)(2,1)}, bf16[256,1024]{1,0:T(8,128)(2,1)}, u32[]{:S(2)}, u32[]{:S(2)}) %collective-permute-start.1) | collective-permute-done | bytes 524320 | tf_op jit(solution)/shard_map/ppermute | solution.py:16
  152.2 2.0 copy.154
  158.2 1.8 gather_fusion.1
  160.0 1.8 gather_fusion.2
  162.7 1.8 scatter_custom_fusion.2
  164.5 2.8 scatter_fusion
  169.3 5.7 all-to-all-start.2
  174.9 6.8 %fusion.7 = f32[16,64,256]{2,1,0:T(8,128)} fusion(f32[16,256,512]{2,1,0:T(8,128)} %copy-done.5, f32[16,256]{1,0:T(8,128)S(1)} %log_add_fusion, pred[256,512]{1,0:T(8,128)(4,1)S(1)} %iota_compare_fusion, bf16[1,256,16,64]{1,3,2,0:T(8,128)(2,1)} %bitcast.236, bf16[1,256,16,64]{1,3,2,0:T(8,128)(2,1)} %bitcast.238), kind=kOutput, calls=%fused_computation.36 | convolution fusion | flops 278921216 | bytes 10633216 | tf_op jit(solution)/shard_map/mhqk,mkhd->mqhd/dot_general | solution.py:98
  181.8 2.6 copy.158
  184.4 4.3 scatter_custom_fusion.6
  189.3 6.0 all-to-all-start.5
  195.3 2.1 gather_fusion.4
  198.7 1.6 reduce.20
  201.4 4.7 fusion.12
  208.4 5.6 collective-permute-start.3
  216.8 72.8 %all-to-all-done.5 = f32[32,32,1024]{2,1,0:T(8,128)} async-done(((f32[32,32,1024]{2,1,0:T(8,128)}), f32[32,32,1024]{2,1,0:T(8,128)}, u32[]{:S(2)}, u32[]{:S(2)}) %all-to-all-start.5) | async-done | bytes 4194336 | tf_op jit(solution)/shard_map/all_to_all | solution.py:105
  289.7 3.4 gather_fusion.6
  293.0 3.4 gather_fusion.7
  302.3 14.9 %all-to-all-start.6 = ((f32[32,1,512]{2,1,0:T(1,128)}), f32[32,1,512]{2,1,0:T(1,128)}, u32[]{:S(2)}, u32[]{:S(2)}) async-start(f32[32,1,512]{2,1,0:T(1,128)} %reshape.1161), calls=%async_computation.6 | async-start | bytes 131072 | tf_op jit(solution)/shard_map/all_to_all | solution.py:123
  317.3 2.1 bitcast_convert_fusion
  319.3 2.6 copy.171
  322.0 4.0 scatter_custom_fusion.10
  325.9 5.9 all-to-all-start.8
  334.7 5.6 multiply_convert_fusion
  342.1 5.4 collective-permute-start.2
  348.6 2.6 copy.167
  351.1 4.5 convolution_multiply_fusion
  355.7 2.6 copy.169
  358.3 20.5 %collective-permute-done.2 = bf16[256,16,64]{0,2,1:T(8,128)(2,1)} collective-permute-done((bf16[256,16,64]{0,2,1:T(8,128)(2,1)}, bf16[256,16,64]{0,2,1:T(8,128)(2,1)}, u32[]{:S(2)}, u32[]{:S(2)}) %collective-permute-start.2) | collective-permute-done | bytes 524320 | tf_op jit(solution)/shard_map/ppermute | solution.py:16
  381.2 4.9 scatter_custom_fusion.9
  386.1 16.1 %all-to-all-start.7 = ((bf16[32,32,1024]{2,1,0:T(8,128)(2,1)}), bf16[32,32,1024]{2,1,0:T(8,128)(2,1)}, u32[]{:S(2)}, u32[]{:S(2)}) async-start(bf16[32,32,1024]{2,1,0:T(8,128)(2,1)} %bitcast.209), calls=%async_computation.7 | async-start | bytes 4194304 | tf_op jit(solution)/shard_map/all_to_all | solution.py:160
  402.2 3.0 gather_fusion.10
  405.2 3.0 gather_fusion.12
  409.0 2.7 convolution_add_fusion
  411.7 39.3 %all-to-all-done.7 = bf16[32,32,1024]{2,1,0:T(8,128)(2,1)} async-done(((bf16[32,32,1024]{2,1,0:T(8,128)(2,1)}), bf16[32,32,1024]{2,1,0:T(8,128)(2,1)}, u32[]{:S(2)}, u32[]{:S(2)}) %all-to-all-start.7) | async-done | bytes 2097184 | tf_op jit(solution)/shard_map/all_to_all | solution.py:160
  451.0 3.0 gather_fusion.9
  454.0 3.0 gather_fusion.11
  457.1 1.8 fusion.41
  461.0 4.1 pad_maximum_fusion
  465.1 9.2 %copy.174 = f32[1024,2048]{1,0:T(8,128)} copy(f32[1024,2048]{0,1:T(8,128)} %pad_maximum_fusion) | data formatting | bytes 16777216
  475.2 2.4 convolution_add_fusion.4
  480.0 142.7 %reduce-scatter.4.cloned.1.call-done = f32[32,2048]{1,0:T(8,128)} async-done(((f32[1024,2048]{1,0:T(8,128)}), f32[32,2048]{1,0:T(8,128)}) %reduce-scatter.4.cloned.1.call-update) | async-done | bytes 262160
  (139 shorter events, 48.9 us)
Async XLA Ops:
  7.2 4.2 copy-start
  11.4 16.0 %copy-start.28 = (s32[256,1]{0,1:T(1,128)}, s32[256,1]{0,1:T(1,128)S(1)}, u32[]{:S(2)}) copy-start(s32[256,1]{0,1:T(1,128)S(1)} %get-tuple-element.132) | copy-start | bytes 3076
  15.8 32.8 %all-to-all-start = ((bf16[16,32,1024]{2,1,0:T(8,128)(2,1)}), bf16[16,32,1024]{2,1,0:T(8,128)(2,1)S(1)}, u32[]{:S(2)}, u32[]{:S(2)}) async-start(bf16[16,32,1024]{2,1,0:T(8,128)(2,1)} %bitcast.222), calls=%async_computation | async-start | bytes 2097152 | tf_op jit(solution)/shard_map/all_to_all | solution.py:71
  27.4 33.6 %copy-start.17 = (s32[1,256]{1,0:T(1,128)S(1)}, s32[1,256]{1,0:T(1,128)}, u32[]{:S(2)}) copy-start(s32[1,256]{1,0:T(1,128)} %param.27) | copy-start | bytes 3076
  48.6 1.0 copy-start.2
  49.5 51.1 %all-to-all-start.4 = ((bf16[16,32,1024]{2,1,0:T(8,128)(2,1)}), bf16[16,32,1024]{2,1,0:T(8,128)(2,1)S(1)}, u32[]{:S(2)}, u32[]{:S(2)}) async-start(bf16[16,32,1024]{2,1,0:T(8,128)(2,1)} %bitcast.221), calls=%async_computation.4 | async-start | bytes 2097152 | tf_op jit(solution)/shard_map/all_to_all | solution.py:72
  55.4 34.8 %copy-start.22 = (s32[1024]{0:T(1024)}, s32[1024]{0:T(1024)S(1)}, u32[]{:S(2)}) copy-start(s32[1024]{0:T(1024)S(1)} %pad_clamp_fusion.3) | copy-start | bytes 12292
  59.1 29.0 %collective-permute-start = (bf16[256,1024]{1,0:T(8,128)(2,1)}, bf16[256,1024]{1,0:T(8,128)(2,1)}, u32[]{:S(2)}, u32[]{:S(2)}) collective-permute-start(bf16[256,1024]{1,0:T(8,128)(2,1)} %gather_fusion), channel_id=1, source_target_pairs={{30,0},{0,2},{2,4},{4,6},{6,8},{8,10},{10,12},{12,14},{14,16},{16,... | collective-permute-start | bytes 1572872 | tf_op jit(solution)/shard_map/ppermute | solution.py:16
  61.1 35.6 %copy-start.25 = (s32[256,1]{0,1:T(1,128)}, s32[256,1]{0,1:T(1,128)S(1)}, u32[]{:S(2)}) copy-start(s32[256,1]{0,1:T(1,128)S(1)} %compare_select_fusion.2) | copy-start | bytes 3076
  93.3 3.2 copy-start.5
  100.6 13.1 %copy-start.1 = (bf16[16,32,1024]{2,1,0:T(8,128)(2,1)}, bf16[16,32,1024]{2,1,0:T(8,128)(2,1)S(1)}, u32[]{:S(2)}) copy-start(bf16[16,32,1024]{2,1,0:T(8,128)(2,1)S(1)} %all-to-all-done.4) | copy-start | bytes 3145732
  100.6 13.1 %all-to-all-start.1 = ((f32[32,1,512]{2,1,0:T(1,128)}), f32[32,1,512]{2,1,0:T(1,128)S(1)}, u32[]{:S(2)}, u32[]{:S(2)}) async-start(f32[32,1,512]{2,1,0:T(1,128)} %reshape.1159), calls=%async_computation.1 | async-start | bytes 131072 | tf_op jit(solution)/shard_map/all_to_all | solution.py:106
  113.7 55.5 %all-to-all-start.3 = ((bf16[16,32,1024]{2,1,0:T(8,128)(2,1)}), bf16[16,32,1024]{2,1,0:T(8,128)(2,1)S(1)}, u32[]{:S(2)}, u32[]{:S(2)}) async-start(bf16[16,32,1024]{2,1,0:T(8,128)(2,1)} %bitcast.220), calls=%async_computation.3 | async-start | bytes 2097152 | tf_op jit(solution)/shard_map/all_to_all | solution.py:73
  122.0 30.3 %collective-permute-start.1 = (bf16[256,1024]{1,0:T(8,128)(2,1)}, bf16[256,1024]{1,0:T(8,128)(2,1)}, u32[]{:S(2)}, u32[]{:S(2)}) collective-permute-start(bf16[256,1024]{1,0:T(8,128)(2,1)} %gather_fusion.5), channel_id=1, source_target_pairs={{30,0},{0,2},{2,4},{4,6},{6,8},{8,10},{10,12},{12,14},{14,16},{16,... | collective-permute-start | bytes 1572872 | tf_op jit(solution)/shard_map/ppermute | solution.py:16
  124.0 30.8 %copy-start.24 = (s32[128]{0:T(128)}, s32[128]{0:T(128)S(1)}, u32[]{:S(2)}) copy-start(s32[128]{0:T(128)S(1)} %get-tuple-element.124) | copy-start | bytes 1540
  124.0 30.8 %copy-start.27 = (s32[128]{0:T(128)}, s32[128]{0:T(128)S(1)}, u32[]{:S(2)}) copy-start(s32[128]{0:T(128)S(1)} %get-tuple-element.125) | copy-start | bytes 1540
  169.3 19.4 %all-to-all-start.2 = ((f32[32,1,512]{2,1,0:T(1,128)}), f32[32,1,512]{2,1,0:T(1,128)S(1)}, u32[]{:S(2)}, u32[]{:S(2)}) async-start(f32[32,1,512]{2,1,0:T(1,128)} %reshape.1163), calls=%async_computation.2 | async-start | bytes 131072 | tf_op jit(solution)/shard_map/all_to_all | solution.py:122
  174.9 9.4 %copy-start.26 = (s32[256,1]{0,1:T(1,128)S(1)}, s32[256,1]{0,1:T(1,128)}, u32[]{:S(2)}) copy-start(s32[256,1]{0,1:T(1,128)} %copy-done.25) | copy-start | bytes 3076
  188.7 0.6 copy-start.15
  189.3 100.4 %all-to-all-start.5 = ((f32[32,32,1024]{2,1,0:T(8,128)}), f32[32,32,1024]{2,1,0:T(8,128)}, u32[]{:S(2)}, u32[]{:S(2)}) async-start(f32[32,32,1024]{2,1,0:T(8,128)} %bitcast.207), calls=%async_computation.5 | async-start | bytes 8388608 | tf_op jit(solution)/shard_map/all_to_all | solution.py:105
  195.3 10.8 %copy-start.23 = (s32[1024]{0:T(1024)}, s32[1024]{0:T(1024)S(1)}, u32[]{:S(2)}) copy-start(s32[1024]{0:T(1024)S(1)} %pad_clamp_fusion) | copy-start | bytes 12292
  198.7 7.5 %copy-start.14 = (bf16[256,1024]{0,1:T(8,128)(2,1)}, bf16[256,1024]{0,1:T(8,128)(2,1)S(1)}, u32[]{:S(2)}) copy-start(bf16[256,1024]{0,1:T(8,128)(2,1)S(1)} %copy.153) | copy-start | bytes 1572868
  201.4 4.7 copy-start.20
  201.4 12.6 %copy-start.16 = (bf16[256,1024]{1,0:T(8,128)(2,1)S(1)}, bf16[256,1024]{1,0:T(8,128)(2,1)}, u32[]{:S(2)}) copy-start(bf16[256,1024]{1,0:T(8,128)(2,1)} %param.23) | copy-start | bytes 1572868
  206.1 1.3 copy-start.12
  208.4 108.9 %collective-permute-start.3 = (bf16[256,16,64]{0,2,1:T(8,128)(2,1)}, bf16[256,16,64]{0,2,1:T(8,128)(2,1)}, u32[]{:S(2)}, u32[]{:S(2)}) collective-permute-start(bf16[256,16,64]{0,2,1:T(8,128)(2,1)} %fusion.22), channel_id=1, source_target_pairs={{2,0},{4,2},{6,4},{8,6},{10,8},{12,10},{14,12},{16,14},{18,16},{20... | collective-permute-start | bytes 1572872 | tf_op jit(solution)/shard_map/ppermute | solution.py:16
  293.0 4.6 copy-start.18
  293.0 4.6 copy-start.19
  301.5 20.5 %copy-start.8 = (f32[256,1024]{1,0:T(8,128)S(1)}, f32[256,1024]{1,0:T(8,128)}, u32[]{:S(2)}) copy-start(f32[256,1024]{1,0:T(8,128)} %copy.170) | copy-start | bytes 3145732
  302.3 23.6 %all-to-all-start.6 = ((f32[32,1,512]{2,1,0:T(1,128)}), f32[32,1,512]{2,1,0:T(1,128)}, u32[]{:S(2)}, u32[]{:S(2)}) async-start(f32[32,1,512]{2,1,0:T(1,128)} %reshape.1161), calls=%async_computation.6 | async-start | bytes 131072 | tf_op jit(solution)/shard_map/all_to_all | solution.py:123
  325.9 8.8 %copy-start.13 = (bf16[256,1024]{0,1:T(8,128)(2,1)S(1)}, bf16[256,1024]{0,1:T(8,128)(2,1)}, u32[]{:S(2)}) copy-start(bf16[256,1024]{0,1:T(8,128)(2,1)} %copy.155) | copy-start | bytes 1572868
  325.9 8.8 %copy-start.21 = (f32[16,256]{1,0:T(8,128)S(1)}, f32[16,256]{1,0:T(8,128)}, u32[]{:S(2)}) copy-start(f32[16,256]{1,0:T(8,128)} %copy-done.20) | copy-start | bytes 49156
  325.9 60.1 %all-to-all-start.8 = ((bf16[32,32,1024]{2,1,0:T(8,128)(2,1)}), bf16[32,32,1024]{2,1,0:T(8,128)(2,1)}, u32[]{:S(2)}, u32[]{:S(2)}) async-start(bf16[32,32,1024]{2,1,0:T(8,128)(2,1)} %bitcast.208), calls=%async_computation.8 | async-start | bytes 4194304 | tf_op jit(solution)/shard_map/all_to_all | solution.py:161
  334.7 5.6 copy-start.7
  340.3 8.3 %copy-start.3 = (bf16[16,256,512]{2,1,0:T(8,128)(2,1)}, bf16[16,256,512]{2,1,0:T(8,128)(2,1)S(1)}, u32[]{:S(2)}) copy-start(bf16[16,256,512]{2,1,0:T(8,128)(2,1)S(1)} %multiply_convert_fusion) | copy-start | bytes 12582916
  341.1 10.0 %copy-start.11 = (bf16[256,1024]{0,1:T(8,128)(2,1)S(1)}, bf16[256,1024]{0,1:T(8,128)(2,1)}, u32[]{:S(2)}) copy-start(bf16[256,1024]{0,1:T(8,128)(2,1)} %copy.138) | copy-start | bytes 1572868
  342.1 36.7 %collective-permute-start.2 = (bf16[256,16,64]{0,2,1:T(8,128)(2,1)}, bf16[256,16,64]{0,2,1:T(8,128)(2,1)}, u32[]{:S(2)}, u32[]{:S(2)}) collective-permute-start(bf16[256,16,64]{0,2,1:T(8,128)(2,1)} %fusion.21), channel_id=1, source_target_pairs={{2,0},{4,2},{6,4},{8,6},{10,8},{12,10},{14,12},{16,14},{18,16},{20... | collective-permute-start | bytes 1572872 | tf_op jit(solution)/shard_map/ppermute | solution.py:16
  386.0 22.2 %copy-start.9 = (bf16[256,1024]{1,0:T(8,128)(2,1)S(1)}, bf16[256,1024]{1,0:T(8,128)(2,1)}, u32[]{:S(2)}) copy-start(bf16[256,1024]{1,0:T(8,128)(2,1)} %param.22) | copy-start | bytes 1572868
  386.1 64.9 %all-to-all-start.7 = ((bf16[32,32,1024]{2,1,0:T(8,128)(2,1)}), bf16[32,32,1024]{2,1,0:T(8,128)(2,1)}, u32[]{:S(2)}, u32[]{:S(2)}) async-start(bf16[32,32,1024]{2,1,0:T(8,128)(2,1)} %bitcast.209), calls=%async_computation.7 | async-start | bytes 4194304 | tf_op jit(solution)/shard_map/all_to_all | solution.py:160
  402.1 220.6 %reduce-scatter.4.cloned.1.call-start = ((), (), s32[]{:S(2)}) async-start(), calls=%async_computation.10 | async-start | bytes 8650752
  457.1 1.8 copy-start.10
  458.9 2.2 copy-start.4
  474.4 4.1 copy-start.6
Sparse Core Ops, SparseCore 0:
  474.5 148.2 reduce-scatter.3
where the time goes:
time: 644 us; the launch traced here: 633 us
  waiting for transfers between devices  347 us (54%)
  local copies, waits for them, and re-layouts  111 us (17%)
  starting transfers between devices  86.8 us (13%)
  matrix products  42.2 us (7%)
  other arithmetic  30.5 us (5%)
  between operations  15.2 us (2%)
    unnamed x2, waiting for transfers between devices  143 us
    all_to_all x1, waiting for transfers between devices, per_device(): lax.all_to_all(sent_out, ('ctx', 'round'), split_axis=0, concat_axis=0, t...  72.8 us
    ppermute x4, waiting for transfers between devices, from_behind(): return lax.ppermute(block, axis, route)  70.3 us
    all_to_all x1, waiting for transfers between devices, per_device(): lax.all_to_all(sent_dq, ('ctx', 'round'), split_axis=0, concat_axis=0, ti...  39.3 us
    unnamed x70, local copies, waits for them, and re-layouts  20.5 us
    scatter x7, local copies, waits for them, and re-layouts, place_rows(): return jnp.zeros((total,) + rows.shape[1:], rows.dtype).at[index].set(rows)  18.2 us
    all_to_all x1, waiting for transfers between devices, per_device(): lax.all_to_all(sent_q, 'ctx', split_axis=0, concat_axis=0, tiled=True)  17.9 us
    all_to_all x1, starting transfers between devices, per_device(): lax.all_to_all(sent_dq, ('ctx', 'round'), split_axis=0, concat_axis=0, ti...  16.1 us
  transfers between devices with their start and end apart: 14, of which 8 were waited for; matrix products, arithmetic and copies ran while one was open for 23% of the time, Pallas kernels for 0%

commit v1 on v0

v1 whole, which is shorter than its diff:
```python
import functools
import math

import jax
import jax.numpy as jnp
from jax import lax
from jax.experimental import pallas as pl
from jax.experimental.pallas import tpu as pltpu
from jax.sharding import PartitionSpec as P

HEADS = 16
SPAN = 256
LAYERS = 4
PAIR = 128
BLOCK = 256
VMEM_LIMIT = 56 * 2**20
CHUNK = 64

masked_score = -1000000000.0
NT = (((1,), (1,)), ((), ()))
TN = (((0,), (0,)), ((), ()))
f32 = jnp.float32
bf16 = jnp.bfloat16


def span_ring(peers):
    side = math.isqrt(peers // LAYERS)
    if side * side * LAYERS != peers or side % 2:
        return list(range(peers))
    columns = [(0, x) for x in range(side)]
    for y in range(1, side):
        xs = range(side - 1, 0, -1) if y % 2 else range(1, side)
        columns += [(y, x) for x in xs]
    columns += [(y, 0) for y in range(side - 1, 0, -1)]
    span_of = [0] * peers
    for k, (y, x) in enumerate(columns):
        for step in range(LAYERS):
            z = step if k % 2 == 0 else LAYERS - 1 - step
            span_of[(z * side + y) * side + x] = k * LAYERS + step
    return span_of


def ordinal(group, order):
    same = group[:, None] == group[None, :]
    before = order[None, :] < order[:, None]
    return jnp.sum((same & before).astype(jnp.int32), axis=1)


def one_hot(index, total):
    return (index[:, None] == jnp.arange(total, dtype=jnp.int32)[None, :]).astype(bf16)


def mm(a, b, dims=(((1,), (0,)), ((), ()))):
    return lax.dot_general(a, b, dims, preferred_element_type=f32)


def head_masks(block):
    lane = lax.broadcasted_iota(jnp.int32, block.shape, 1)
    zero = jnp.zeros_like(block)
    low = lane < PAIR // 2
    return jnp.where(low, block, zero), jnp.where(low, zero, block)


def half_rows(block_t, h):
    row = lax.broadcasted_iota(jnp.int32, block_t.shape, 0)
    return jnp.where((row < PAIR // 2) == (h == 0), block_t, jnp.zeros_like(block_t))


def chunks():
    return [slice(k, k + CHUNK) for k in range(0, 2 * SPAN, CHUNK)]


def lanes_of(pair):
    return pl.ds(pl.multiple_of(pair * PAIR, PAIR), PAIR)


def whole_of(array):
    zeros = (0,) * len(array.shape)
    return pl.BlockSpec(array.shape, lambda i: zeros)


def params():
    return pltpu.CompilerParams(vmem_limit_bytes=VMEM_LIMIT)


def forward_kernel(scale, k_own, v_own, k_prev, v_prev, lse, inverse, out_t, kept, scores):
    step = pl.program_id(0)
    half = PAIR // 2
    rows = lax.broadcasted_iota(jnp.int32, (SPAN, SPAN), 0)
    cols = lax.broadcasted_iota(jnp.int32, (SPAN, SPAN), 1)
    for p in range(BLOCK // PAIR):
        pair = (BLOCK // PAIR) * step + p
        lanes = lanes_of(pair)
        own = k_own[:, lanes]
        vals_t = jnp.concatenate([v_prev[:, lanes].T, v_own[:, lanes].T], axis=1)
        query_t = (own.T.astype(f32) * scale).astype(bf16)
        for h in range(2):
            mine = half_rows(query_t, h)
            scores[h, :SPAN] = mm(k_prev[:, lanes], mine)
            scores[h, SPAN:] = jnp.where(rows == cols, masked_score, mm(own, mine))
        for h in range(2):
            head = pl.ds(2 * pair + h, 1)
            top = jnp.max(scores[h], axis=0, keepdims=True)
            total = jnp.zeros((8, SPAN), f32)
            for part in chunks():
                probs = jnp.exp(scores[h, part] - top)
                total += jnp.sum(probs.reshape(CHUNK // 8, 8, SPAN), axis=0)
                kept[2 * p + h, part] = probs.astype(bf16)
            total = jnp.sum(total, axis=0, keepdims=True)
            lse[head, :] = top + jnp.log(total)
            inverse[head, :] = 1.0 / total
            first = p * PAIR + h * half
            out = mm(vals_t[h * half : (h + 1) * half], kept[2 * p + h])
            out_t[first : first + half, :] = out * (1.0 / total)


def forward(k_own, v_own, k_prev, v_prev, scale):
    width = k_own.shape[1]
    heads = HEADS * BLOCK // width
    rows = pl.BlockSpec((HEADS, SPAN), lambda i: (0, 0))
    return pl.pallas_call(
        functools.partial(forward_kernel, scale),
        grid=(width // BLOCK,),
        in_specs=[whole_of(k_own)] * 4,
        out_specs=[
            rows,
            rows,
            pl.BlockSpec((BLOCK, SPAN), lambda i: (i, 0)),
            pl.BlockSpec((heads, 2 * SPAN, SPAN), lambda i: (i, 0, 0)),
        ],
        out_shape=[
            jax.ShapeDtypeStruct((HEADS, SPAN), f32),
            jax.ShapeDtypeStruct((HEADS, SPAN), f32),
            jax.ShapeDtypeStruct((width, SPAN), f32),
            jax.ShapeDtypeStruct((HEADS, 2 * SPAN, SPAN), bf16),
        ],
        scratch_shapes=[pltpu.VMEM((2, 2 * SPAN, SPAN), f32)],
        compiler_params=params(),
        name="forward",
    )(k_own, v_own, k_prev, v_prev)


def cotangent_kernel(got, pick, out_t, lse, ids, g_out, g_t, stats):
    rows = mm(pick[...], got[...])
    g_out[...] = rows.astype(bf16)
    rows_t = rows.T
    g_t[...] = rows_t.astype(bf16)
    terms = (rows_t * out_t[...]).reshape(HEADS, PAIR // 2, SPAN)
    stats[:HEADS, :] = lse[...]
    stats[HEADS : 2 * HEADS, :] = jnp.sum(terms, axis=1)
    stats[2 * HEADS :, :] = jnp.broadcast_to(ids[...], (8, SPAN))


def cotangent(got, pick, out_t, lse, ids):
    width = got.shape[1]
    whole = pl.BlockSpec(memory_space=pltpu.VMEM)
    return pl.pallas_call(
        cotangent_kernel,
        in_specs=[whole] * 5,
        out_specs=[whole] * 3,
        out_shape=[
            jax.ShapeDtypeStruct((SPAN, width), bf16),
            jax.ShapeDtypeStruct((width, SPAN), bf16),
            jax.ShapeDtypeStruct((2 * HEADS + 8, SPAN), f32),
        ],
        compiler_params=params(),
        name="cotangent",
    )(got, pick, out_t, lse, ids)


def pick_other(stats, wanted):
    group = 4
    rows = 2 * HEADS

    def body(k, acc):
        spans = [stats[group * k + j] for j in range(group)]
        values = jnp.concatenate([span[:rows] for span in spans], axis=1)
        ids = jnp.concatenate([span[rows : rows + 1] for span in spans], axis=1)
        high = values.astype(bf16)
        rest = values - high.astype(f32)
        middle = rest.astype(bf16)
        low = (rest - middle.astype(f32)).astype(bf16)
        hits = jnp.where(wanted == ids, 1.0, 0.0).astype(bf16)
        return acc + mm(jnp.concatenate([high, middle, low], axis=0), hits, NT)

    acc = lax.fori_loop(0, stats.shape[0] // group, body, jnp.zeros((3 * rows, SPAN), f32))
    return acc[:rows] + (acc[rows : 2 * rows] + acc[2 * rows :])


def backward_kernel(
    scale, stats, wanted, mine, inverse, probs, k_own, k_prev, v_own, v_prev, g_own, g_t,
    grads, factor_s, delta_s, inner_s, weight_s, dscore_s, dq_s,
):
    pair = pl.program_id(0)

    @pl.when(pair == 0)
    def _():
        other = pick_other(stats, wanted[...])
        lse_a, d_a = mine[:HEADS, :], mine[HEADS : 2 * HEADS, :]
        lse_b, d_b = other[:HEADS], other[HEADS:]
        peak = jnp.maximum(lse_a, lse_b)
        total = peak + jnp.log(jnp.exp(lse_a - peak) + jnp.exp(lse_b - peak))
        share = jnp.exp(lse_a - total)
        factor_s[...] = share * inverse[...]
        delta_s[...] = share * d_a + jnp.exp(lse_b - total) * d_b

    half = PAIR // 2
    lanes = lanes_of(pair)
    own = k_own[:, lanes]
    keys_t = jnp.concatenate([k_prev[:, lanes].T, own.T], axis=1)
    queries = head_masks((own.astype(f32) * scale).astype(bf16))
    cotangents = head_masks(g_own[:, lanes])
    for h in range(2):
        cotangent_t = half_rows(g_t[...], h)
        inner_s[h, :SPAN] = mm(v_prev[:, lanes], cotangent_t)
        inner_s[h, SPAN:] = mm(v_own[:, lanes], cotangent_t)
    for h in range(2):
        factor = factor_s[pl.ds(2 * pair + h, 1), :]
        delta = delta_s[pl.ds(2 * pair + h, 1), :]
        queried = slice(h * SPAN, (h + 1) * SPAN)
        for part in chunks():
            weight = probs[h, part].astype(f32) * factor
            weight_s[part, queried] = weight.astype(bf16)
            dscore_s[part, queried] = (weight * (inner_s[h, part] - delta)).astype(bf16)
    for h in range(2):
        part = slice(h * half, (h + 1) * half)
        dq_s[part, :] = mm(keys_t[part], dscore_s[:, h * SPAN : (h + 1) * SPAN])
    dv = mm(weight_s[...], jnp.concatenate(cotangents, axis=0))
    grads[1, :, lanes] = dv.astype(bf16)
    dk = mm(dscore_s[...], jnp.concatenate(queries, axis=0))
    grads[0, :SPAN, lanes] = dk[:SPAN].astype(bf16)
    grads[0, SPAN:, lanes] = (dk[SPAN:] + dq_s[...].T * scale).astype(bf16)


def backward(stats, wanted, mine, inverse, probs, k_own, k_prev, v_own, v_prev, g_own, g_t, scale):
    width = k_own.shape[1]
    square = pl.BlockSpec((HEADS * PAIR // width, 2 * SPAN, SPAN), lambda i: (i, 0, 0))
    out = jax.ShapeDtypeStruct((2, 2 * SPAN, width), bf16)
    return pl.pallas_call(
        functools.partial(backward_kernel, scale),
        grid=(width // PAIR,),
        in_specs=[whole_of(a) for a in (stats, wanted, mine, inverse)]
        + [square]
        + [whole_of(k_own)] * 5
        + [pl.BlockSpec((PAIR, SPAN), lambda i: (i, 0))],
        out_specs=whole_of(out),
        out_shape=out,
        scratch_shapes=[
            pltpu.VMEM((HEADS, SPAN), f32),
            pltpu.VMEM((HEADS, SPAN), f32),
            pltpu.VMEM((2, 2 * SPAN, SPAN), f32),
            pltpu.VMEM((2 * SPAN, 2 * SPAN), bf16),
            pltpu.VMEM((2 * SPAN, 2 * SPAN), bf16),
            pltpu.VMEM((PAIR, SPAN), f32),
        ],
        compiler_params=params(),
        name="backward",
    )(stats, wanted, mine, inverse, probs, k_own, k_prev, v_own, v_prev, g_own, g_t)


def combine_kernel(x_t, grads, other_k, other_v, sent):
    near, rows, width = sent.shape
    for k, other in enumerate((other_k, other_v)):
        for start in range(0, width, BLOCK):
            cols = slice(start, start + BLOCK)
            total = mm(x_t[...], grads[k, :, cols]) + other[:, cols].astype(f32)
            sent[:, k * rows // 2 : (k + 1) * rows // 2, cols] = total.reshape(
                near, rows // 2, BLOCK
            ).astype(bf16)


def combine(x_t, grads, other_k, other_v, near):
    rows, width = x_t.shape[0], grads.shape[2]
    whole = pl.BlockSpec(memory_space=pltpu.VMEM)
    return pl.pallas_call(
        combine_kernel,
        in_specs=[whole] * 4,
        out_specs=whole,
        out_shape=jax.ShapeDtypeStruct((near, 2 * rows // near, width), bf16),
        compiler_params=pltpu.CompilerParams(vmem_limit_bytes=VMEM_LIMIT // 2),
        name="combine",
    )(x_t, grads, other_k, other_v)


def place_kernel(pick_t, y_own, y_next, sent):
    rows = y_own[...].astype(f32) + y_next[...].astype(f32)
    sent[...] = mm(pick_t[...], rows.astype(bf16)).astype(bf16)


def place_rows(pick_t, y_own, y_next):
    whole = pl.BlockSpec(memory_space=pltpu.VMEM)
    return pl.pallas_call(
        place_kernel,
        in_specs=[whole] * 3,
        out_specs=whole,
        out_shape=jax.ShapeDtypeStruct((pick_t.shape[0], y_own.shape[1]), bf16),
        compiler_params=params(),
        name="place_rows",
    )(pick_t, y_own, y_next)


def per_device(x2, out_grad, w_qk, w_v, sort_slot, source_pos):
    tdev, width = x2.shape
    part_rows = tdev // 2
    peers = lax.axis_size("ctx")
    near = peers // 2
    cap = 2 * tdev // peers
    slots = 2 * near * cap
    scale = (width // HEADS) ** (-0.5)
    chip = lax.axis_index("ctx")
    hround = lax.axis_index("round")
    side = chip // near
    both = ("ctx", "round")

    ring = span_ring(peers)
    span_of = [ring, [(peers - m) % peers for m in ring]]
    holder = [[spans.index(m) for m in range(peers)] for spans in span_of]

    def flat(c, r):
        return 2 * c + r

    every = [(c, r) for c in range(peers) for r in range(2)]
    onward = [
        (flat(holder[r][m], r), flat(holder[r][(m + 1) % peers], r))
        for m in range(peers)
        for r in range(2)
    ]
    backward_way = [(b, a) for a, b in onward]
    fetch = [(flat(span_of[r][c], r), flat(c, r)) for c, r in every]
    mirror = [(flat(c, r), flat((c + near) % peers, r)) for c, r in every]
    swap = [(flat(c, r), flat(c, 1 - r)) for c, r in every]
    swap_mirror = [(flat(c, r), flat((c + near) % peers, 1 - r)) for c, r in every]
    halves = [list(range(near)), list(range(near, peers))]

    def move(rows, route):
        return lax.ppermute(rows, both, route)

    def exchange(blocks):
        return lax.all_to_all(blocks, "ctx", 0, 0, axis_index_groups=halves, tiled=True)

    def my_part(rows):
        return lax.dynamic_slice_in_dim(rows, hround * part_rows, part_rows, 0)

    def their_part(rows):
        return lax.dynamic_slice_in_dim(rows, (1 - hround) * part_rows, part_rows, 0)

    own_spans = lax.dynamic_index_in_dim(sort_slot, hround, 0, keepdims=False) // SPAN
    spare = jnp.zeros((16, width - tdev), bf16)
    label = jnp.broadcast_to(own_spans.astype(bf16)[None, :], (16, tdev))
    label = jnp.concatenate([label, spare], axis=1)
    far_x = move(jnp.concatenate([my_part(x2), label], axis=0), mirror)
    far_x, half_g = lax.optimization_barrier((far_x, my_part(out_grad)))
    far_g = move(half_g, mirror)
    far_spans = far_x[part_rows, :tdev].astype(jnp.int32)
    far_x = far_x[:part_rows]

    def send_index(spans):
        tables = jnp.where(
            hround == 0, jnp.array(span_of[0], jnp.int32), jnp.array(span_of[1], jnp.int32)
        )
        held = spans[:, None] == tables[None, :]
        owner = jnp.sum(jnp.where(held, jnp.arange(peers, dtype=jnp.int32)[None, :], 0), axis=1)
        order = ordinal(owner, jnp.arange(tdev, dtype=jnp.int32))
        return jnp.where(owner // near == side, owner % near, peers) * 2 * cap + order

    near_index = send_index(own_spans)
    far_index = send_index(far_spans) + cap
    rolled = jnp.where(hround == 0, far_index, jnp.roll(far_index, part_rows, axis=0))
    send = one_hot(near_index, slots)
    send_far = one_hot(far_index, slots)
    send_far_rolled = one_hot(rolled, slots)
    sources = move(source_pos[0], fetch)
    group = sources // tdev
    is_near = group // near == side
    place = 2 * (group % near) * cap + jnp.where(is_near, 0, cap) + ordinal(group, sources)
    pick = one_hot(place, slots)

    def in_slots(rows, far_rows):
        far_rows = jnp.concatenate([far_rows, move(far_rows, swap)], axis=0)
        sent = mm(send, rows, TN) + mm(send_far_rolled, far_rows, TN)
        return sent.astype(bf16).reshape(near, 2 * cap, width)

    sent_x, sources = lax.optimization_barrier((in_slots(x2, far_x), sources))
    got_x = exchange(sent_x).reshape(slots, width)
    x_own = mm(pick, got_x).astype(bf16)
    x_prev = move(x_own, onward)
    far_g, _ = lax.optimization_barrier((far_g, x_own))
    k_own = mm(x_own, w_qk).astype(bf16)
    v_own = mm(x_own, w_v).astype(bf16)

    sent_g = in_slots(out_grad, far_g)
    x_prev, k_own, v_own, sent_g = lax.optimization_barrier((x_prev, k_own, v_own, sent_g))
    got_g = exchange(sent_g).reshape(slots, width)
    k_prev = mm(x_prev, w_qk).astype(bf16)
    v_prev = mm(x_prev, w_v).astype(bf16)
    lse, inverse, out_t, probs = forward(k_own, v_own, k_prev, v_prev, scale)
    ids = sources.astype(f32)
    g_own, g_t, mine = cotangent(got_g, pick, out_t, lse, ids[None, :])

    told = jnp.stack([move(mine, swap), move(mine, swap_mirror)])
    stats = exchange(jnp.broadcast_to(told[None], (near,) + told.shape))
    stats = stats.reshape((peers,) + mine.shape)
    grads = backward(
        stats, ids[:, None], mine, inverse, probs, k_own, k_prev, v_own, v_prev, g_own, g_t, scale
    )

    y_prev = (mm(grads[0, :SPAN], w_qk, NT) + mm(grads[1, :SPAN], w_v, NT)).astype(bf16)
    y_next = move(y_prev, backward_way)

    each = width // (2 * peers)
    spot = jnp.arange(near * each, dtype=jnp.int32)
    x_both = jnp.concatenate([x_prev, x_own], axis=0)

    def columns_for(core, half):
        column = (half * near + spot // each) * (2 * each) + core * each + spot % each
        ordered = jnp.arange(width, dtype=jnp.int32)[None, :] == column[:, None]
        return mm(ordered.astype(bf16), x_both, NT).astype(bf16)

    def weight_terms(half, after):
        x_ours, x_theirs = columns_for(hround, half), columns_for(1 - hround, half)
        x_theirs, _ = lax.optimization_barrier((x_theirs, after))
        theirs = [move(mm(x_theirs, grads[k]).astype(bf16), swap) for k in range(2)]
        return combine(x_ours, grads, theirs[0], theirs[1], near)

    y_own = (mm(grads[0, SPAN:], w_qk, NT) + mm(grads[1, SPAN:], w_v, NT)).astype(bf16)
    sent_y = place_rows(jnp.transpose(pick), y_own, y_next).reshape(near, 2 * cap, width)
    got_y = exchange(sent_y)
    terms, got_y = lax.optimization_barrier((weight_terms(1 - side, y_prev), got_y))
    got_far_w = exchange(terms)
    terms, got_far_w = lax.optimization_barrier((weight_terms(side, sent_y), got_far_w))
    got_w = exchange(terms)

    got_y = got_y.reshape(slots, width)
    rows_far = mm(send_far, got_y)
    rows_near = mm(send, got_y)
    from_core = jnp.concatenate([their_part(rows_far), their_part(rows_near)], axis=0)
    from_core = move(from_core.astype(bf16), swap).astype(f32)
    crossing = move((my_part(rows_far) + from_core[:part_rows]).astype(bf16), mirror)
    grad_x = (my_part(rows_near) + from_core[part_rows:] + crossing.astype(f32)).astype(bf16)
    crossing_w = move(jnp.sum(got_far_w.astype(f32), axis=0).astype(bf16), mirror)

    got_w, grad_x, crossing_w = lax.optimization_barrier((got_w, grad_x, crossing_w))
    weight_grads = jnp.sum(got_w.astype(f32), axis=0) + crossing_w.astype(f32)
    weight_grads = weight_grads * (tdev * peers) ** (-0.5)
    return (grad_x, weight_grads[:each], weight_grads[each:])


def solution(mesh):
    placed = (P("ctx", None), P("ctx", None), P(), P(), P(None, "ctx"), P("round", "ctx"))
    return jax.shard_map(
        per_device,
        mesh=mesh,
        in_specs=placed,
        out_specs=(P(("ctx", "round"), None), P(("ctx", "round"), None), P(("ctx", "round"), None)),
        check_vma=False,
    )
```

time: 644 us -> 202 us (0.31); the launches traced: 633 us -> 200 us
  waiting for transfers between devices: 347 us -> 69.5 us
  local copies, waits for them, and re-layouts: 111 us -> 10.2 us
  starting transfers between devices: 86.8 us -> 41.6 us
  Pallas kernels: 0 us -> 29.3 us
  other arithmetic: 30.5 us -> 10.7 us
  between operations: 15.2 us -> 1.09 us
    unnamed x2 -> x0, waiting for transfers between devices: 143 us -> none
    all_to_all x9 -> x6, waiting for transfers between devices: 134 us -> 30.6 us  [exchange(): lax.all_to_all(blocks, 'ctx', 0, 0, axis_index_groups=halves, tiled=True)]
    all_to_all x9 -> x6, starting transfers between devices: 72 us -> 25.9 us  [exchange(): lax.all_to_all(blocks, 'ctx', 0, 0, axis_index_groups=halves, tiled=True)]
    gather x20 -> x0, local copies, waits for them, and re-layouts: 40.4 us -> none  [the longest x2 5.92 us: per_device(): v_sorted = got_v[recv_index]]
    ppermute x4 -> x16, waiting for transfers between devices: 70.3 us -> 38.9 us  [move(): return lax.ppermute(rows, both, route)]
    pallas_call x0 -> x6, Pallas kernels: none -> 29.3 us  [the longest x1 12.5 us: backward(): pl.pallas_call(functools.partial(backward_kernel, scale), grid=(width //...]
    scatter x9 -> x0, local copies, waits for them, and re-layouts: 22.2 us -> none  [the longest x7 18.2 us: place_rows(): return jnp.zeros((total,) + rows.shape[1:], rows.dtype).at[index].set(rows)]
    unnamed x70 -> x42, local copies, waits for them, and re-layouts: 20.5 us -> 4.65 us
  transfers between devices with their start and end apart: 14 -> 22, of which waited for: 8 -> 14; matrix products, arithmetic and copies ran while one was open for 23% -> 23% of each run, Pallas kernels for 0% -> 6%
where the time goes in v1:
time: 202 us; the launch traced here: 200 us
  waiting for transfers between devices  69.5 us (34%)
  starting transfers between devices  41.6 us (21%)
  matrix products  38.1 us (19%)
  Pallas kernels  29.3 us (15%)
  other arithmetic  10.7 us (5%)
  local copies, waits for them, and re-layouts  10.2 us (5%)
    ppermute x16, waiting for transfers between devices, move(): return lax.ppermute(rows, both, route)  38.9 us
    dot_general x23, matrix products, mm(): return lax.dot_general(a, b, dims, preferred_element_type=f32)  38.1 us
    all_to_all x6, waiting for transfers between devices, exchange(): lax.all_to_all(blocks, 'ctx', 0, 0, axis_index_groups=halves, tiled=True)  30.6 us
    all_to_all x6, starting transfers between devices, exchange(): lax.all_to_all(blocks, 'ctx', 0, 0, axis_index_groups=halves, tiled=True)  25.9 us
    ppermute x16, starting transfers between devices, move(): return lax.ppermute(rows, both, route)  15.7 us
    pallas_call x1, Pallas kernels, backward(): pl.pallas_call(functools.partial(backward_kernel, scale), grid=(width //...  12.5 us
    pallas_call x1, Pallas kernels, forward(): pl.pallas_call(functools.partial(forward_kernel, scale), grid=(width // B...  7.63 us
    unnamed x42, local copies, waits for them, and re-layouts  4.65 us
  transfers between devices with their start and end apart: 22, of which 14 were waited for; matrix products, arithmetic and copies ran while one was open for 23% of the time, Pallas kernels for 6%

profile of v1, /device:TPU:0, one launch (start us, length us, event | category | flops | bytes accessed | tf_op | source)
XLA Modules:
  0.0 200.4 jit_solution(7711212776553243138)
XLA Ops:
  0.7 1.1 constant_dynamic-slice_fusion.1
  2.6 4.1 %collective-permute-start.1 = (bf16[144,1024]{1,0:T(8,128)(2,1)S(1)}, bf16[144,1024]{1,0:T(8,128)(2,1)}, u32[]{:S(2)}, u32[]{:S(2)}) collective-permute-start(bf16[144,1024]{1,0:T(8,128)(2,1)S(1)} %pad_maximum_fusion.2), channel_id=1, source_target_pairs={{0,16},{1,17},{2,18},{3,19},{4,20},{5,21},{6,22},{7,23},{8,24},{9,... | collective-permute-start | bytes 884744 | tf_op jit(solution)/shard_map/ppermute | solution.py:336
  6.7 1.3 collective-permute-start
  8.7 1.0 constant_dynamic-slice_fusion
  9.6 10.5 %collective-permute-done.1 = bf16[144,1024]{1,0:T(8,128)(2,1)} collective-permute-done((bf16[144,1024]{1,0:T(8,128)(2,1)S(1)}, bf16[144,1024]{1,0:T(8,128)(2,1)}, u32[]{:S(2)}, u32[]{:S(2)}) %collective-permute-start.1) | collective-permute-done | bytes 294944 | tf_op jit(solution)/shard_map/ppermute | solution.py:336
  20.8 1.0 slice.49
  22.9 0.9 collective-permute-done.2
  23.9 1.5 add_convert_fusion.1
  25.4 3.8 %all-to-all-start = ((bf16[8,64,1024]{2,1,0:T(8,128)(2,1)}), bf16[8,64,1024]{2,1,0:T(8,128)(2,1)S(1)}, u32[]{:S(2)}, u32[]{:S(2)}) async-start(bf16[8,64,1024]{2,1,0:T(8,128)(2,1)} %bitcast.59), calls=%async_computation | async-start | bytes 2097152 | tf_op jit(solution)/shard_map/all_to_all | solution.py:339
  29.4 3.6 %collective-permute-start.4 = (bf16[128,1024]{1,0:T(8,128)(2,1)S(1)}, bf16[128,1024]{1,0:T(8,128)(2,1)}, u32[]{:S(2)}, u32[]{:S(2)}) collective-permute-start(bf16[128,1024]{1,0:T(8,128)(2,1)S(1)} %constant_dynamic-slice_fusion), channel_id=1, source_target_pairs={{0,16},{1,17},{2,18},{3,19},{4,20},{5,21},{6,22},{7,23},{8,24},{9,... | collective-permute-start | bytes 786440 | tf_op jit(solution)/shard_map/ppermute | solution.py:336
  33.0 3.0 %fusion.17 = f32[512,1024]{1,0:T(8,128)} fusion(bf16[256,1024]{1,0:T(8,128)(2,1)} %param.11, s32[256]{0:T(256)S(1)} %get-tuple-element.62), kind=kOutput, calls=%fused_computation.55 | convolution fusion | flops 268566528 | bytes 2622464 | tf_op jit(solution)/shard_map/dot_general | solution.py:54
  36.0 12.9 %all-to-all-done = bf16[8,64,1024]{2,1,0:T(8,128)(2,1)S(1)} async-done(((bf16[8,64,1024]{2,1,0:T(8,128)(2,1)}), bf16[8,64,1024]{2,1,0:T(8,128)(2,1)S(1)}, u32[]{:S(2)}, u32[]{:S(2)}) %all-to-all-start) | async-done | bytes 1048608 | tf_op jit(solution)/shard_map/all_to_all | solution.py:339
  49.6 3.2 %convolution_convert_fusion.7.v_own = bf16[256,1024]{1,0:T(8,128)(2,1)} fusion(bf16[256,1024]{1,0:T(8,128)(2,1)S(1)} %convolution_convert_fusion.4, bf16[1024,1024]{1,0:T(8,128)(2,1)} %param.13), kind=kOutput, calls=%fused_computation.12 | convolution fusion | flops 537133056 | bytes 3145728 | tf_op jit(solution)/shard_map/dot_general | solution.py:54
  52.7 1.6 convolution_convert_fusion.8.k_own
  54.3 2.5 %add_convert_fusion = bf16[512,1024]{1,0:T(8,128)(2,1)} fusion(f32[512,1024]{1,0:T(8,128)S(1)} %copy-done.7, bf16[128,1024]{1,0:T(8,128)(2,1)S(1)} %collective-permute-done.5, bf16[128,1024]{1,0:T(8,128)(2,1)} %collective-permute-done.4, s32[256]{0:T(256)S(1)} %add_select_fusion), kind=kOutput, calls=%fused_computation.1 | convolution fusion | flops 270663680 | bytes 3671040 | tf_op jit(solution)/shard_map/dot_general | solution.py:54
  56.8 1.7 collective-permute-done.3
  58.6 0.8 copy-done.19
  59.4 4.6 %all-to-all-start.1 = ((bf16[8,64,1024]{2,1,0:T(8,128)(2,1)}), bf16[8,64,1024]{2,1,0:T(8,128)(2,1)S(1)}, u32[]{:S(2)}, u32[]{:S(2)}) async-start(bf16[8,64,1024]{2,1,0:T(8,128)(2,1)} %bitcast.58), calls=%async_computation.1 | async-start | bytes 2097152 | tf_op jit(solution)/shard_map/all_to_all | solution.py:339
  64.0 0.8 fusion.19.pick
  65.4 3.3 %convolution_convert_fusion.5.v_prev = bf16[256,1024]{1,0:T(8,128)(2,1)} fusion(bf16[256,1024]{1,0:T(8,128)(2,1)} %copy-done.19, bf16[1024,1024]{1,0:T(8,128)(2,1)} %param.13), kind=kOutput, calls=%fused_computation.10 | convolution fusion | flops 537133056 | bytes 3145728 | tf_op jit(solution)/shard_map/dot_general | solution.py:54
  68.7 1.5 convolution_convert_fusion.6.k_prev
  70.2 7.6 %forward.1 = (f32[16,256]{1,0:T(8,128)}, f32[16,256]{1,0:T(8,128)}, f32[1024,256]{1,0:T(8,128)}, bf16[16,512,256]{2,1,0:T(8,128)(2,1)}) custom-call(bf16[256,1024]{1,0:T(8,128)(2,1)} %convolution_convert_fusion.8.k_own, bf16[256,1024]{1,0:T(8,128)(2,1)} %convolution_convert_fusion.7.v_own, bf16[256,1024]{1,0:T(8,128)(2,1)} %convolution_convert_fusion.6.k_prev, ...), custom_call_target="tpu_custom_call" | custom-call | tf_op jit(solution)/shard_map/forward/pallas_call | solution.py:121
  77.8 1.4 all-to-all-done.1
  79.3 1.0 copy-done.8
  80.3 3.1 %cotangent.1 = (bf16[256,1024]{1,0:T(8,128)(2,1)}, bf16[1024,256]{1,0:T(8,128)(2,1)}, f32[40,256]{1,0:T(8,128)}) custom-call(bf16[512,1024]{1,0:T(8,128)(2,1)} %bitcast.56, bf16[256,512]{1,0:T(8,128)(2,1)} %fusion.19.pick, f32[1024,256]{1,0:T(8,128)} %get-tuple-element.36.out_t, f32[16,256]{1,0:T(8,128)} %get-tuple-element.37.lse, f32[1,256]{1,0:T(1,128)} %bitcast.63), custom_call_target="tpu_custom_call" | custom-call | tf_op jit(solution)/shard_map/cotangent/pallas_call | solution.py:157
  83.4 1.5 collective-permute-start.7
  84.9 3.0 %collective-permute-done.7 = f32[40,256]{1,0:T(8,128)S(1)} collective-permute-done((f32[40,256]{1,0:T(8,128)}, f32[40,256]{1,0:T(8,128)S(1)}, u32[]{:S(2)}, u32[]{:S(2)}) %collective-permute-start.7) | collective-permute-done | bytes 40992 | tf_op jit(solution)/shard_map/ppermute | solution.py:336
  87.9 0.9 broadcast_in_dim.41
  88.8 4.7 %all-to-all-start.2 = ((f32[8,2,40,256]{3,2,1,0:T(8,128)}), f32[8,2,40,256]{3,2,1,0:T(8,128)S(1)}, u32[]{:S(2)}, u32[]{:S(2)}) async-start(f32[8,2,40,256]{3,2,1,0:T(8,128)} %broadcast_in_dim.41), calls=%async_computation.2 | async-start | bytes 1310720 | tf_op jit(solution)/shard_map/all_to_all | solution.py:339
  93.5 0.8 fusion.21.pick_t
  94.3 0.8 copy.14.wanted
  95.1 9.3 %all-to-all-done.2 = f32[8,2,40,256]{3,2,1,0:T(8,128)S(1)} async-done(((f32[8,2,40,256]{3,2,1,0:T(8,128)}), f32[8,2,40,256]{3,2,1,0:T(8,128)S(1)}, u32[]{:S(2)}, u32[]{:S(2)}) %all-to-all-start.2) | async-done | bytes 655392 | tf_op jit(solution)/shard_map/all_to_all | solution.py:339
  104.4 0.8 copy-done.12
  105.2 12.5 %backward.1.grads = bf16[2,512,1024]{2,1,0:T(8,128)(2,1)} custom-call(f32[16,40,256]{2,1,0:T(8,128)} %bitcast.60, f32[256,1]{1,0:T(8,128)} %copy.14.wanted, f32[40,256]{1,0:T(8,128)} %get-tuple-element.39.mine, f32[16,256]{1,0:T(8,128)} %get-tuple-element.40.inverse, bf16[16,512,256]{2,1,0:T(8,128)(2,1)} %get-tuple-element.41.probs, ...), custom_call_target="tpu_custom_call" | custom-call | tf_op jit(solution)/shard_map/backward/pallas_call | solution.py:239
  117.7 1.9 fusion.5
  120.5 0.8 collective-permute-start.8
  122.0 1.6 fusion.y_own
  123.6 6.3 %collective-permute-done.8.y_next = bf16[256,1024]{1,0:T(8,128)(2,1)S(1)} collective-permute-done((bf16[256,1024]{1,0:T(8,128)(2,1)S(1)}, bf16[256,1024]{1,0:T(8,128)(2,1)S(1)}, u32[]{:S(2)}, u32[]{:S(2)}) %collective-permute-start.8) | collective-permute-done | bytes 524320 | tf_op jit(solution)/shard_map/ppermute | solution.py:336
  129.9 0.8 copy-done.17
  130.7 2.7 %place_rows.1 = bf16[512,1024]{1,0:T(8,128)(2,1)} custom-call(bf16[512,256]{1,0:T(8,128)(2,1)} %fusion.21.pick_t, bf16[256,1024]{1,0:T(8,128)(2,1)} %fusion.y_own, bf16[256,1024]{1,0:T(8,128)(2,1)} %copy-done.17), custom_call_target="tpu_custom_call" | custom-call | tf_op jit(solution)/shard_map/place_rows/pallas_call | solution.py:292
  133.4 4.2 %all-to-all-start.3 = ((bf16[8,64,1024]{2,1,0:T(8,128)(2,1)}), bf16[8,64,1024]{2,1,0:T(8,128)(2,1)}, u32[]{:S(2)}, u32[]{:S(2)}) async-start(bf16[8,64,1024]{2,1,0:T(8,128)(2,1)} %bitcast.55), calls=%async_computation.3 | async-start | bytes 2097152 | tf_op jit(solution)/shard_map/all_to_all | solution.py:339
  137.7 1.7 convolution_convert_fusion.9
  139.4 1.3 convolution_convert_fusion
  140.7 1.3 convolution_convert_fusion.1
  142.5 1.8 convolution_convert_fusion.10.x_t
  144.8 1.7 combine.3
  146.6 4.3 %all-to-all-done.3 = bf16[8,64,1024]{2,1,0:T(8,128)(2,1)} async-done(((bf16[8,64,1024]{2,1,0:T(8,128)(2,1)}), bf16[8,64,1024]{2,1,0:T(8,128)(2,1)}, u32[]{:S(2)}, u32[]{:S(2)}) %all-to-all-start.3) | async-done | bytes 1048608 | tf_op jit(solution)/shard_map/all_to_all | solution.py:339
  150.9 4.2 %all-to-all-start.4 = ((bf16[8,64,1024]{2,1,0:T(8,128)(2,1)}), bf16[8,64,1024]{2,1,0:T(8,128)(2,1)}, u32[]{:S(2)}, u32[]{:S(2)}) async-start(bf16[8,64,1024]{2,1,0:T(8,128)(2,1)} %combine.3), calls=%async_computation.4 | async-start | bytes 2097152 | tf_op jit(solution)/shard_map/all_to_all | solution.py:339
  155.1 1.7 convolution_convert_fusion.11
  156.9 1.3 convolution_convert_fusion.2
  158.1 1.3 convolution_convert_fusion.3
  159.9 1.8 convolution_convert_fusion.12.x_t
  162.3 1.7 combine.2
  164.0 1.7 fusion.22
  165.7 2.7 %all-to-all-done.4 = bf16[8,64,1024]{2,1,0:T(8,128)(2,1)} async-done(((bf16[8,64,1024]{2,1,0:T(8,128)(2,1)}), bf16[8,64,1024]{2,1,0:T(8,128)(2,1)}, u32[]{:S(2)}, u32[]{:S(2)}) %all-to-all-start.4) | async-done | bytes 1048608 | tf_op jit(solution)/shard_map/all_to_all | solution.py:339
  168.4 4.2 %all-to-all-start.5 = ((bf16[8,64,1024]{2,1,0:T(8,128)(2,1)}), bf16[8,64,1024]{2,1,0:T(8,128)(2,1)}, u32[]{:S(2)}, u32[]{:S(2)}) async-start(bf16[8,64,1024]{2,1,0:T(8,128)(2,1)} %combine.2), calls=%async_computation.5 | async-start | bytes 2097152 | tf_op jit(solution)/shard_map/all_to_all | solution.py:339
  172.7 1.7 fusion.16
  174.4 1.0 copy-done.11
  175.5 1.9 collective-permute-done.13
  177.6 2.3 %collective-permute-start.14 = (bf16[128,1024]{1,0:T(8,128)(2,1)S(1)}, bf16[128,1024]{1,0:T(8,128)(2,1)}, u32[]{:S(2)}, u32[]{:S(2)}) collective-permute-start(bf16[128,1024]{1,0:T(8,128)(2,1)S(1)} %fusion.2), channel_id=1, source_target_pairs={{0,16},{1,17},{2,18},{3,19},{4,20},{5,21},{6,22},{7,23},{8,24},{9,... | collective-permute-start | bytes 786440 | tf_op jit(solution)/shard_map/ppermute | solution.py:336
  179.9 2.1 %reduce_sum.71 = bf16[64,1024]{1,0:T(8,128)(2,1)} reduce(bf16[8,64,1024]{2,1,0:T(8,128)(2,1)} %all-to-all-done.4, bf16[]{:T(256)} %constant.159.clone.1), dimensions={0}, to_apply=%region_5.6 | reduce | flops 458752 | bytes 1179650 | tf_op jit(solution)/shard_map/reduce_sum | solution.py:440
  182.7 13.6 %collective-permute-done.14 = bf16[128,1024]{1,0:T(8,128)(2,1)} collective-permute-done((bf16[128,1024]{1,0:T(8,128)(2,1)S(1)}, bf16[128,1024]{1,0:T(8,128)(2,1)}, u32[]{:S(2)}, u32[]{:S(2)}) %collective-permute-start.14) | collective-permute-done | bytes 262176 | tf_op jit(solution)/shard_map/ppermute | solution.py:336
  196.3 1.9 fusion.4
  198.2 1.4 convert_reduce_fusion
  (90 shorter events, 10.3 us)
Async XLA Ops:
  0.6 52.1 %copy-start = (bf16[1024,1024]{1,0:T(8,128)(2,1)S(1)}, bf16[1024,1024]{1,0:T(8,128)(2,1)}, u32[]{:S(2)}) copy-start(bf16[1024,1024]{1,0:T(8,128)(2,1)} %param.12) | copy-start | bytes 6291460
  0.6 21.7 %copy-start.13 = (bf16[256,1024]{1,0:T(8,128)(2,1)S(1)}, bf16[256,1024]{1,0:T(8,128)(2,1)}, u32[]{:S(2)}) copy-start(bf16[256,1024]{1,0:T(8,128)(2,1)} %param.10) | copy-start | bytes 1572868
  2.6 17.5 %collective-permute-start.1 = (bf16[144,1024]{1,0:T(8,128)(2,1)S(1)}, bf16[144,1024]{1,0:T(8,128)(2,1)}, u32[]{:S(2)}, u32[]{:S(2)}) collective-permute-start(bf16[144,1024]{1,0:T(8,128)(2,1)S(1)} %pad_maximum_fusion.2), channel_id=1, source_target_pairs={{0,16},{1,17},{2,18},{3,19},{4,20},{5,21},{6,22},{7,23},{8,24},{9,... | collective-permute-start | bytes 884744 | tf_op jit(solution)/shard_map/ppermute | solution.py:336
  6.7 18.7 %collective-permute-start = (s32[256]{0:T(256)}, s32[256]{0:T(256)S(1)}, u32[]{:S(2)}, u32[]{:S(2)}) collective-permute-start(s32[256]{0:T(256)} %bitcast.67), channel_id=1, source_target_pairs={{0,0},{1,1},{14,2},{19,3},{30,4},{3,5},{16,6},{17,7},{2,8},{31,9},... | collective-permute-start | bytes 3080 | tf_op jit(solution)/shard_map/ppermute | solution.py:336
  22.3 1.6 collective-permute-start.2
  25.4 23.4 %all-to-all-start = ((bf16[8,64,1024]{2,1,0:T(8,128)(2,1)}), bf16[8,64,1024]{2,1,0:T(8,128)(2,1)S(1)}, u32[]{:S(2)}, u32[]{:S(2)}) async-start(bf16[8,64,1024]{2,1,0:T(8,128)(2,1)} %bitcast.59), calls=%async_computation | async-start | bytes 2097152 | tf_op jit(solution)/shard_map/all_to_all | solution.py:339
  29.4 19.9 %collective-permute-start.4 = (bf16[128,1024]{1,0:T(8,128)(2,1)S(1)}, bf16[128,1024]{1,0:T(8,128)(2,1)}, u32[]{:S(2)}, u32[]{:S(2)}) collective-permute-start(bf16[128,1024]{1,0:T(8,128)(2,1)S(1)} %constant_dynamic-slice_fusion), channel_id=1, source_target_pairs={{0,16},{1,17},{2,18},{3,19},{4,20},{5,21},{6,22},{7,23},{8,24},{9,... | collective-permute-start | bytes 786440 | tf_op jit(solution)/shard_map/ppermute | solution.py:336
  49.3 5.0 %copy-start.14 = (bf16[256,1024]{1,0:T(8,128)(2,1)}, bf16[256,1024]{1,0:T(8,128)(2,1)S(1)}, u32[]{:S(2)}) copy-start(bf16[256,1024]{1,0:T(8,128)(2,1)S(1)} %convolution_convert_fusion.4) | copy-start | bytes 1572868
  49.3 9.2 %collective-permute-start.3 = (bf16[256,1024]{1,0:T(8,128)(2,1)S(1)}, bf16[256,1024]{1,0:T(8,128)(2,1)S(1)}, u32[]{:S(2)}, u32[]{:S(2)}) collective-permute-start(bf16[256,1024]{1,0:T(8,128)(2,1)S(1)} %convolution_convert_fusion.4), channel_id=1, source_target_pairs={{0,8},{1,5},{8,16},{5,13},{16,24},{13,21},{24,26},{21,29},{26,18},... | collective-permute-start | bytes 1572872 | tf_op jit(solution)/shard_map/ppermute | solution.py:336
  49.4 4.9 %collective-permute-start.5 = (bf16[128,1024]{1,0:T(8,128)(2,1)}, bf16[128,1024]{1,0:T(8,128)(2,1)S(1)}, u32[]{:S(2)}, u32[]{:S(2)}) collective-permute-start(bf16[128,1024]{1,0:T(8,128)(2,1)} %collective-permute-done.4), channel_id=1, source_target_pairs={{0,1},{1,0},{2,3},{3,2},{4,5},{5,4},{6,7},{7,6},{8,9},{9,8},{10,11... | collective-permute-start | bytes 786440 | tf_op jit(solution)/shard_map/ppermute | solution.py:336
  52.7 1.6 copy-start.7
  58.5 0.9 copy-start.19
  59.4 19.9 %all-to-all-start.1 = ((bf16[8,64,1024]{2,1,0:T(8,128)(2,1)}), bf16[8,64,1024]{2,1,0:T(8,128)(2,1)S(1)}, u32[]{:S(2)}, u32[]{:S(2)}) async-start(bf16[8,64,1024]{2,1,0:T(8,128)(2,1)} %bitcast.58), calls=%async_computation.1 | async-start | bytes 2097152 | tf_op jit(solution)/shard_map/all_to_all | solution.py:339
  64.0 4.7 %copy-start.20 = (bf16[256,1024]{1,0:T(8,128)(2,1)S(1)}, bf16[256,1024]{1,0:T(8,128)(2,1)}, u32[]{:S(2)}) copy-start(bf16[256,1024]{1,0:T(8,128)(2,1)} %copy-done.19) | copy-start | bytes 1572868
  79.3 1.0 copy-start.8
  80.3 14.0 %copy-start.18 = (f32[256]{0:T(256)S(1)}, f32[256]{0:T(256)}, u32[]{:S(2)}) copy-start(f32[256]{0:T(256)} %convert_element_type.125) | copy-start | bytes 3076
  83.4 1.5 collective-permute-start.6
  83.4 4.5 %collective-permute-start.7 = (f32[40,256]{1,0:T(8,128)}, f32[40,256]{1,0:T(8,128)S(1)}, u32[]{:S(2)}, u32[]{:S(2)}) collective-permute-start(f32[40,256]{1,0:T(8,128)} %get-tuple-element.39.mine), channel_id=1, source_target_pairs={{0,17},{1,16},{2,19},{3,18},{4,21},{5,20},{6,23},{7,22},{8,25},{9,... | collective-permute-start | bytes 122888 | tf_op jit(solution)/shard_map/ppermute | solution.py:336
  88.8 15.6 %all-to-all-start.2 = ((f32[8,2,40,256]{3,2,1,0:T(8,128)}), f32[8,2,40,256]{3,2,1,0:T(8,128)S(1)}, u32[]{:S(2)}, u32[]{:S(2)}) async-start(f32[8,2,40,256]{3,2,1,0:T(8,128)} %broadcast_in_dim.41), calls=%async_computation.2 | async-start | bytes 1310720 | tf_op jit(solution)/shard_map/all_to_all | solution.py:339
  104.4 0.8 copy-start.12
  105.2 14.4 %copy-start.6 = (bf16[1024,1024]{1,0:T(8,128)(2,1)S(1)}, bf16[1024,1024]{1,0:T(8,128)(2,1)}, u32[]{:S(2)}) copy-start(bf16[1024,1024]{1,0:T(8,128)(2,1)} %param.13) | copy-start | bytes 6291460
  117.7 2.0 copy-start.1
  120.5 9.4 %collective-permute-start.8 = (bf16[256,1024]{1,0:T(8,128)(2,1)S(1)}, bf16[256,1024]{1,0:T(8,128)(2,1)S(1)}, u32[]{:S(2)}, u32[]{:S(2)}) collective-permute-start(bf16[256,1024]{1,0:T(8,128)(2,1)S(1)} %fusion.1), channel_id=1, source_target_pairs={{8,0},{5,1},{16,8},{13,5},{24,16},{21,13},{26,24},{29,21},{18,26},... | collective-permute-start | bytes 1572872 | tf_op jit(solution)/shard_map/ppermute | solution.py:336
  123.6 14.1 %copy-start.15 = (bf16[256,1024]{1,0:T(8,128)(2,1)S(1)}, bf16[256,1024]{1,0:T(8,128)(2,1)}, u32[]{:S(2)}) copy-start(bf16[256,1024]{1,0:T(8,128)(2,1)} %copy-done.14) | copy-start | bytes 1572868
  129.9 0.8 copy-start.17
  133.4 17.5 %all-to-all-start.3 = ((bf16[8,64,1024]{2,1,0:T(8,128)(2,1)}), bf16[8,64,1024]{2,1,0:T(8,128)(2,1)}, u32[]{:S(2)}, u32[]{:S(2)}) async-start(bf16[8,64,1024]{2,1,0:T(8,128)(2,1)} %bitcast.55), calls=%async_computation.3 | async-start | bytes 2097152 | tf_op jit(solution)/shard_map/all_to_all | solution.py:339
  137.7 1.7 copy-start.2
  142.0 2.4 %collective-permute-start.12 = (bf16[256,1024]{1,0:T(8,128)(2,1)}, bf16[256,1024]{1,0:T(8,128)(2,1)S(1)}, u32[]{:S(2)}, u32[]{:S(2)}) collective-permute-start(bf16[256,1024]{1,0:T(8,128)(2,1)} %convolution_convert_fusion), channel_id=1, source_target_pairs={{0,1},{1,0},{2,3},{3,2},{4,5},{5,4},{6,7},{7,6},{8,9},{9,8},{10,11... | collective-permute-start | bytes 1572872 | tf_op jit(solution)/shard_map/ppermute | solution.py:336
  142.0 2.9 %collective-permute-start.11 = (bf16[256,1024]{1,0:T(8,128)(2,1)}, bf16[256,1024]{1,0:T(8,128)(2,1)S(1)}, u32[]{:S(2)}, u32[]{:S(2)}) collective-permute-start(bf16[256,1024]{1,0:T(8,128)(2,1)} %convolution_convert_fusion.1), channel_id=1, source_target_pairs={{0,1},{1,0},{2,3},{3,2},{4,5},{5,4},{6,7},{7,6},{8,9},{9,8},{10,11... | collective-permute-start | bytes 1572872 | tf_op jit(solution)/shard_map/ppermute | solution.py:336
  142.5 2.4 %copy-start.3 = (bf16[2,512,1024]{2,1,0:T(8,128)(2,1)S(1)}, bf16[2,512,1024]{2,1,0:T(8,128)(2,1)}, u32[]{:S(2)}) copy-start(bf16[2,512,1024]{2,1,0:T(8,128)(2,1)} %backward.1.grads) | copy-start | bytes 6291460
  146.6 8.6 %copy-start.16 = (bf16[256,1024]{1,0:T(8,128)(2,1)S(1)}, bf16[256,1024]{1,0:T(8,128)(2,1)}, u32[]{:S(2)}) copy-start(bf16[256,1024]{1,0:T(8,128)(2,1)} %copy-done.14) | copy-start | bytes 1572868
  150.9 17.5 %all-to-all-start.4 = ((bf16[8,64,1024]{2,1,0:T(8,128)(2,1)}), bf16[8,64,1024]{2,1,0:T(8,128)(2,1)}, u32[]{:S(2)}, u32[]{:S(2)}) async-start(bf16[8,64,1024]{2,1,0:T(8,128)(2,1)} %combine.3), calls=%async_computation.4 | async-start | bytes 2097152 | tf_op jit(solution)/shard_map/all_to_all | solution.py:339
  155.1 1.7 copy-start.4
  159.4 2.4 %collective-permute-start.10 = (bf16[256,1024]{1,0:T(8,128)(2,1)}, bf16[256,1024]{1,0:T(8,128)(2,1)S(1)}, u32[]{:S(2)}, u32[]{:S(2)}) collective-permute-start(bf16[256,1024]{1,0:T(8,128)(2,1)} %convolution_convert_fusion.2), channel_id=1, source_target_pairs={{0,1},{1,0},{2,3},{3,2},{4,5},{5,4},{6,7},{7,6},{8,9},{9,8},{10,11... | collective-permute-start | bytes 1572872 | tf_op jit(solution)/shard_map/ppermute | solution.py:336
  159.4 2.9 %collective-permute-start.9 = (bf16[256,1024]{1,0:T(8,128)(2,1)}, bf16[256,1024]{1,0:T(8,128)(2,1)S(1)}, u32[]{:S(2)}, u32[]{:S(2)}) collective-permute-start(bf16[256,1024]{1,0:T(8,128)(2,1)} %convolution_convert_fusion.3), channel_id=1, source_target_pairs={{0,1},{1,0},{2,3},{3,2},{4,5},{5,4},{6,7},{7,6},{8,9},{9,8},{10,11... | collective-permute-start | bytes 1572872 | tf_op jit(solution)/shard_map/ppermute | solution.py:336
  159.9 2.4 %copy-start.5 = (bf16[2,512,1024]{2,1,0:T(8,128)(2,1)S(1)}, bf16[2,512,1024]{2,1,0:T(8,128)(2,1)}, u32[]{:S(2)}) copy-start(bf16[2,512,1024]{2,1,0:T(8,128)(2,1)} %backward.1.grads) | copy-start | bytes 6291460
  165.7 8.7 %copy-start.9 = (f32[256,1024]{1,0:T(8,128)}, f32[256,1024]{1,0:T(8,128)S(1)}, u32[]{:S(2)}) copy-start(f32[256,1024]{1,0:T(8,128)S(1)} %fusion.22) | copy-start | bytes 3145732
  168.4 29.9 %all-to-all-start.5 = ((bf16[8,64,1024]{2,1,0:T(8,128)(2,1)}), bf16[8,64,1024]{2,1,0:T(8,128)(2,1)}, u32[]{:S(2)}, u32[]{:S(2)}) async-start(bf16[8,64,1024]{2,1,0:T(8,128)(2,1)} %combine.2), calls=%async_computation.5 | async-start | bytes 2097152 | tf_op jit(solution)/shard_map/all_to_all | solution.py:339
  174.4 1.0 copy-start.11
  175.4 2.1 %copy-start.10 = (f32[256,1024]{1,0:T(8,128)S(1)}, f32[256,1024]{1,0:T(8,128)}, u32[]{:S(2)}) copy-start(f32[256,1024]{1,0:T(8,128)} %copy-done.9) | copy-start | bytes 3145732
  175.5 2.0 collective-permute-start.13
  177.6 18.7 %collective-permute-start.14 = (bf16[128,1024]{1,0:T(8,128)(2,1)S(1)}, bf16[128,1024]{1,0:T(8,128)(2,1)}, u32[]{:S(2)}, u32[]{:S(2)}) collective-permute-start(bf16[128,1024]{1,0:T(8,128)(2,1)S(1)} %fusion.2), channel_id=1, source_target_pairs={{0,16},{1,17},{2,18},{3,19},{4,20},{5,21},{6,22},{7,23},{8,24},{9,... | collective-permute-start | bytes 786440 | tf_op jit(solution)/shard_map/ppermute | solution.py:336
  182.0 16.3 %collective-permute-start.15 = (bf16[64,1024]{1,0:T(8,128)(2,1)}, bf16[64,1024]{1,0:T(8,128)(2,1)S(1)}, u32[]{:S(2)}, u32[]{:S(2)}) collective-permute-start(bf16[64,1024]{1,0:T(8,128)(2,1)} %reduce_sum.71), channel_id=1, source_target_pairs={{0,16},{1,17},{2,18},{3,19},{4,20},{5,21},{6,22},{7,23},{8,24},{9,... | collective-permute-start | bytes 393224 | tf_op jit(solution)/shard_map/ppermute | solution.py:336

commit v2 on v1

--- a/solution.py
+++ b/solution.py
@@ -191,9 +191,9 @@
     scale, stats, wanted, mine, inverse, probs, k_own, k_prev, v_own, v_prev, g_own, g_t,
     grads, factor_s, delta_s, inner_s, weight_s, dscore_s, dq_s,
 ):
-    pair = pl.program_id(0)
-
-    @pl.when(pair == 0)
+    step = pl.program_id(0)
+
+    @pl.when(step == 0)
     def _():
         other = pick_other(stats, wanted[...])
         lse_a, d_a = mine[:HEADS, :], mine[HEADS : 2 * HEADS, :]
@@ -205,81 +205,102 @@
         delta_s[...] = share * d_a + jnp.exp(lse_b - total) * d_b
 
     half = PAIR // 2
-    lanes = lanes_of(pair)
-    own = k_own[:, lanes]
-    keys_t = jnp.concatenate([k_prev[:, lanes].T, own.T], axis=1)
-    queries = head_masks((own.astype(f32) * scale).astype(bf16))
-    cotangents = head_masks(g_own[:, lanes])
-    for h in range(2):
-        cotangent_t = half_rows(g_t[...], h)
-        inner_s[h, :SPAN] = mm(v_prev[:, lanes], cotangent_t)
-        inner_s[h, SPAN:] = mm(v_own[:, lanes], cotangent_t)
-    for h in range(2):
-        factor = factor_s[pl.ds(2 * pair + h, 1), :]
-        delta = delta_s[pl.ds(2 * pair + h, 1), :]
-        queried = slice(h * SPAN, (h + 1) * SPAN)
-        for part in chunks():
-            weight = probs[h, part].astype(f32) * factor
-            weight_s[part, queried] = weight.astype(bf16)
-            dscore_s[part, queried] = (weight * (inner_s[h, part] - delta)).astype(bf16)
-    for h in range(2):
-        part = slice(h * half, (h + 1) * half)
-        dq_s[part, :] = mm(keys_t[part], dscore_s[:, h * SPAN : (h + 1) * SPAN])
-    dv = mm(weight_s[...], jnp.concatenate(cotangents, axis=0))
-    grads[1, :, lanes] = dv.astype(bf16)
-    dk = mm(dscore_s[...], jnp.concatenate(queries, axis=0))
-    grads[0, :SPAN, lanes] = dk[:SPAN].astype(bf16)
-    grads[0, SPAN:, lanes] = (dk[SPAN:] + dq_s[...].T * scale).astype(bf16)
+    for p in range(BLOCK // PAIR):
+        pair = (BLOCK // PAIR) * step + p
+        lanes = lanes_of(pair)
+        own = k_own[:, lanes]
+        keys_t = jnp.concatenate([k_prev[:, lanes].T, own.T], axis=1)
+        queries = head_masks((own.astype(f32) * scale).astype(bf16))
+        cotangents = head_masks(g_own[:, lanes])
+        for h in range(2):
+            cotangent_t = half_rows(g_t[p * PAIR : (p + 1) * PAIR, :], h)
+            inner_s[p, h, :SPAN] = mm(v_prev[:, lanes], cotangent_t)
+            inner_s[p, h, SPAN:] = mm(v_own[:, lanes], cotangent_t)
+        for h in range(2):
+            factor = factor_s[pl.ds(2 * pair + h, 1), :]
+            delta = delta_s[pl.ds(2 * pair + h, 1), :]
+            queried = slice(h * SPAN, (h + 1) * SPAN)
+            for part in chunks():
+                weight = probs[2 * p + h, part].astype(f32) * factor
+                weight_s[p, part, queried] = weight.astype(bf16)
+                dscore_s[p, part, queried] = (weight * (inner_s[p, h, part] - delta)).astype(bf16)
+        for h in range(2):
+            part = slice(h * half, (h + 1) * half)
+            dq_s[p, part, :] = mm(keys_t[part], dscore_s[p, :, h * SPAN : (h + 1) * SPAN])
+        dv = mm(weight_s[p], jnp.concatenate(cotangents, axis=0))
+        grads[1, :, lanes] = dv.astype(bf16)
+        dk = mm(dscore_s[p], jnp.concatenate(queries, axis=0))
+        grads[0, :SPAN, lanes] = dk[:SPAN].astype(bf16)
+        grads[0, SPAN:, lanes] = (dk[SPAN:] + dq_s[p].T * scale).astype(bf16)
 
 
 def backward(stats, wanted, mine, inverse, probs, k_own, k_prev, v_own, v_prev, g_own, g_t, scale):
     width = k_own.shape[1]
-    square = pl.BlockSpec((HEADS * PAIR // width, 2 * SPAN, SPAN), lambda i: (i, 0, 0))
+    square = pl.BlockSpec((HEADS * BLOCK // width, 2 * SPAN, SPAN), lambda i: (i, 0, 0))
     out = jax.ShapeDtypeStruct((2, 2 * SPAN, width), bf16)
     return pl.pallas_call(
         functools.partial(backward_kernel, scale),
-        grid=(width // PAIR,),
+        grid=(width // BLOCK,),
         in_specs=[whole_of(a) for a in (stats, wanted, mine, inverse)]
         + [square]
         + [whole_of(k_own)] * 5
-        + [pl.BlockSpec((PAIR, SPAN), lambda i: (i, 0))],
+        + [pl.BlockSpec((BLOCK, SPAN), lambda i: (i, 0))],
         out_specs=whole_of(out),
         out_shape=out,
         scratch_shapes=[
             pltpu.VMEM((HEADS, SPAN), f32),
             pltpu.VMEM((HEADS, SPAN), f32),
-            pltpu.VMEM((2, 2 * SPAN, SPAN), f32),
-            pltpu.VMEM((2 * SPAN, 2 * SPAN), bf16),
-            pltpu.VMEM((2 * SPAN, 2 * SPAN), bf16),
-            pltpu.VMEM((PAIR, SPAN), f32),
+            pltpu.VMEM((BLOCK // PAIR, 2, 2 * SPAN, SPAN), f32),
+            pltpu.VMEM((BLOCK // PAIR, 2 * SPAN, 2 * SPAN), bf16),
+            pltpu.VMEM((BLOCK // PAIR, 2 * SPAN, 2 * SPAN), bf16),
+            pltpu.VMEM((BLOCK // PAIR, PAIR, SPAN), f32),
         ],
         compiler_params=params(),
         name="backward",
     )(stats, wanted, mine, inverse, probs, k_own, k_prev, v_own, v_prev, g_own, g_t)
 
 
-def combine_kernel(x_t, grads, other_k, other_v, sent):
-    near, rows, width = sent.shape
-    for k, other in enumerate((other_k, other_v)):
-        for start in range(0, width, BLOCK):
-            cols = slice(start, start + BLOCK)
-            total = mm(x_t[...], grads[k, :, cols]) + other[:, cols].astype(f32)
-            sent[:, k * rows // 2 : (k + 1) * rows // 2, cols] = total.reshape(
-                near, rows // 2, BLOCK
-            ).astype(bf16)
-
-
-def combine(x_t, grads, other_k, other_v, near):
-    rows, width = x_t.shape[0], grads.shape[2]
+def small_params():
+    return pltpu.CompilerParams(vmem_limit_bytes=VMEM_LIMIT // 4)
+
+
+def cut_rows(total, low, leave, keep, cols):
+    rows, width = total.shape
+    cut = total.reshape(rows // (2 * low), 2, low, width)
+    leave[:, cols] = cut[:, 1].reshape(rows // 2, width).astype(bf16)
+    keep[:, cols] = cut[:, 0].reshape(rows // 2, width).astype(bf16)
+
+
+def first_fold_kernel(edges, lows, x_t, grads, other_k, other_v, *outs):
+    width = grads.shape[2]
+    for part, low in enumerate(lows):
+        for start in range(edges[part], edges[part + 1], BLOCK):
+            kind, cols = start // width, slice(start % width, start % width + BLOCK)
+            other = (other_k, other_v)[kind]
+            total = mm(x_t[...], grads[kind, :, cols]) + other[:, cols].astype(f32)
+            inside = slice(start - edges[part], start - edges[part] + BLOCK)
+            cut_rows(total, low, outs[2 * part], outs[2 * part + 1], inside)
+
+
+def fold_kernel(lows, *refs):
+    outs = refs[2 * len(lows) :]
+    for k, low in enumerate(lows):
+        total = refs[2 * k][...].astype(f32) + refs[2 * k + 1][...].astype(f32)
+        cut_rows(total, low, outs[2 * k], outs[2 * k + 1], slice(0, total.shape[1]))
+
+
+def call_fold(kernel, operands, rows, widths, name):
+    shapes = [jax.ShapeDtypeStruct((rows, w), bf16) for w in widths for _ in range(2)]
     whole = pl.BlockSpec(memory_space=pltpu.VMEM)
-    return pl.pallas_call(
-        combine_kernel,
-        in_specs=[whole] * 4,
-        out_specs=whole,
-        out_shape=jax.ShapeDtypeStruct((near, 2 * rows // near, width), bf16),
-        compiler_params=pltpu.CompilerParams(vmem_limit_bytes=VMEM_LIMIT // 2),
-        name="combine",
-    )(x_t, grads, other_k, other_v)
+    outs = pl.pallas_call(
+        kernel,
+        in_specs=[whole] * len(operands),
+        out_specs=[whole] * len(shapes),
+        out_shape=shapes,
+        compiler_params=small_params(),
+        name=name,
+    )(*operands)
+    return [(outs[2 * k], outs[2 * k + 1]) for k in range(len(widths))]
 
 
 def place_kernel(pick_t, y_own, y_next, sent):
@@ -294,7 +315,7 @@
         in_specs=[whole] * 3,
         out_specs=whole,
         out_shape=jax.ShapeDtypeStruct((pick_t.shape[0], y_own.shape[1]), bf16),
-        compiler_params=params(),
+        compiler_params=small_params(),
         name="place_rows",
     )(pick_t, y_own, y_next)
 
@@ -400,6 +421,18 @@
     told = jnp.stack([move(mine, swap), move(mine, swap_mirror)])
     stats = exchange(jnp.broadcast_to(told[None], (near,) + told.shape))
     stats = stats.reshape((peers,) + mine.shape)
+
+    each = width // (2 * peers)
+    spot = jnp.arange(width // 2, dtype=jnp.int32)
+    column = ((spot // each) ^ chip) * (2 * each) + spot % each
+    x_both = jnp.concatenate([x_prev, x_own], axis=0)
+
+    def columns_for(core):
+        ordered = jnp.arange(width, dtype=jnp.int32)[None, :] == (column + core * each)[:, None]
+        return mm(ordered.astype(bf16), x_both, NT).astype(bf16)
+
+    x_ours, x_theirs = columns_for(hround), columns_for(1 - hround)
+    stats, x_ours, x_theirs = lax.optimization_barrier((stats, x_ours, x_theirs))
     grads = backward(
         stats, ids[:, None], mine, inverse, probs, k_own, k_prev, v_own, v_prev, g_own, g_t, scale
     )
@@ -407,42 +440,53 @@
     y_prev = (mm(grads[0, :SPAN], w_qk, NT) + mm(grads[1, :SPAN], w_v, NT)).astype(bf16)
     y_next = move(y_prev, backward_way)
 
-    each = width // (2 * peers)
-    spot = jnp.arange(near * each, dtype=jnp.int32)
-    x_both = jnp.concatenate([x_prev, x_own], axis=0)
-
-    def columns_for(core, half):
-        column = (half * near + spot // each) * (2 * each) + core * each + spot % each
-        ordered = jnp.arange(width, dtype=jnp.int32)[None, :] == column[:, None]
-        return mm(ordered.astype(bf16), x_both, NT).astype(bf16)
-
-    def weight_terms(half, after):
-        x_ours, x_theirs = columns_for(hround, half), columns_for(1 - hround, half)
-        x_theirs, _ = lax.optimization_barrier((x_theirs, after))
-        theirs = [move(mm(x_theirs, grads[k]).astype(bf16), swap) for k in range(2)]
-        return combine(x_ours, grads, theirs[0], theirs[1], near)
-
+    x_theirs, _ = lax.optimization_barrier((x_theirs, y_prev))
+    theirs = [move(mm(x_theirs, grads[k]).astype(bf16), swap) for k in range(2)]
     y_own = (mm(grads[0, SPAN:], w_qk, NT) + mm(grads[1, SPAN:], w_v, NT)).astype(bf16)
-    sent_y = place_rows(jnp.transpose(pick), y_own, y_next).reshape(near, 2 * cap, width)
-    got_y = exchange(sent_y)
-    terms, got_y = lax.optimization_barrier((weight_terms(1 - side, y_prev), got_y))
-    got_far_w = exchange(terms)
-    terms, got_far_w = lax.optimization_barrier((weight_terms(side, sent_y), got_far_w))
-    got_w = exchange(terms)
-
-    got_y = got_y.reshape(slots, width)
-    rows_far = mm(send_far, got_y)
-    rows_near = mm(send, got_y)
-    from_core = jnp.concatenate([their_part(rows_far), their_part(rows_near)], axis=0)
-    from_core = move(from_core.astype(bf16), swap).astype(f32)
-    crossing = move((my_part(rows_far) + from_core[:part_rows]).astype(bf16), mirror)
-    grad_x = (my_part(rows_near) + from_core[part_rows:] + crossing.astype(f32)).astype(bf16)
-    crossing_w = move(jnp.sum(got_far_w.astype(f32), axis=0).astype(bf16), mirror)
-
-    got_w, grad_x, crossing_w = lax.optimization_barrier((got_w, grad_x, crossing_w))
-    weight_grads = jnp.sum(got_w.astype(f32), axis=0) + crossing_w.astype(f32)
-    weight_grads = weight_grads * (tdev * peers) ** (-0.5)
-    return (grad_x, weight_grads[:each], weight_grads[each:])
+
+    bits = near.bit_length() - 1
+    blocks = 2 * width // BLOCK
+    edges = [BLOCK * ((blocks * k + 2) // 3) for k in range(4)]
+    widths = [edges[k + 1] - edges[k] for k in range(3)]
+    left = [list(range(bits + 1)) for _ in range(3)]
+    pairs = None
+    for turn in range(bits):
+        turn_bits = [(k * bits // 3 + turn) % bits for k in range(3)]
+        lows = [each << left[k].index(bit) for k, bit in enumerate(turn_bits)]
+        if turn == 0:
+            kernel = functools.partial(first_fold_kernel, edges, lows)
+            operands = [x_ours, grads, theirs[0], theirs[1]]
+        else:
+            kernel = functools.partial(fold_kernel, lows)
+            operands = [array for pair in pairs for array in pair]
+        cuts = call_fold(kernel, operands, (width // 2) >> (turn + 1), widths, "fold")
+        if turn == 0:
+            y_next, cuts = lax.optimization_barrier((y_next, cuts))
+            sent_y = place_rows(jnp.transpose(pick), y_own, y_next)
+            got_y = exchange(sent_y.reshape(near, 2 * cap, width)).reshape(slots, width)
+        if turn == 1:
+            got_y, cuts = lax.optimization_barrier((got_y, cuts))
+            rows_far = mm(send_far, got_y)
+            rows_near = mm(send, got_y)
+            from_core = jnp.concatenate([their_part(rows_far), their_part(rows_near)], axis=0)
+            from_core = move(from_core.astype(bf16), swap)
+        pairs = []
+        for k, (leave, keep) in enumerate(cuts):
+            left[k].remove(turn_bits[k])
+            route = [(flat(c, r), flat(c ^ (1 << turn_bits[k]), r)) for c, r in every]
+            pairs.append((keep, move(leave, route)))
+        if turn == 1:
+            pairs, from_core = lax.optimization_barrier((pairs, from_core))
+            from_core = from_core.astype(f32)
+            crossing = move((my_part(rows_far) + from_core[:part_rows]).astype(bf16), mirror)
+            grad_x = my_part(rows_near) + from_core[part_rows:] + crossing.astype(f32)
+            grad_x = grad_x.astype(bf16)
+
+    pairs, grad_x = lax.optimization_barrier((pairs, grad_x))
+    summed = jnp.concatenate([a.astype(f32) + b.astype(f32) for a, b in pairs], axis=1)
+    leaving = move(summed[each:].astype(bf16), mirror).astype(f32)
+    weight_grads = (summed[:each] + leaving) * (tdev * peers) ** (-0.5)
+    return (grad_x, weight_grads[:, :width], weight_grads[:, width:])
 
 
 def solution(mesh):

time: 202 us -> 201 us (level)
  waiting for transfers between devices: 69.5 us -> 80.5 us
  matrix products: 38.1 us -> 30.1 us
  other arithmetic: 10.7 us -> 5.43 us
  Pallas kernels: 29.3 us -> 26 us
  starting transfers between devices: 41.6 us -> 44.3 us
  local copies, waits for them, and re-layouts: 10.2 us -> 12.4 us
    ppermute x16 -> x23, waiting for transfers between devices: 38.9 us -> 59.7 us  [move(): return lax.ppermute(rows, both, route)]
    ppermute x16 -> x23, starting transfers between devices: 15.7 us -> 26.9 us  [move(): return lax.ppermute(rows, both, route)]
    all_to_all x6 -> x4, waiting for transfers between devices: 30.6 us -> 20.8 us  [exchange(): lax.all_to_all(blocks, 'ctx', 0, 0, axis_index_groups=halves, tiled=True)]
    all_to_all x6 -> x4, starting transfers between devices: 25.9 us -> 17.4 us  [exchange(): lax.all_to_all(blocks, 'ctx', 0, 0, axis_index_groups=halves, tiled=True)]
    dot_general x23 -> x19, matrix products: 38.1 us -> 30.1 us  [mm(): return lax.dot_general(a, b, dims, preferred_element_type=f32)]
    reduce_sum x2 -> x0, other arithmetic: 3.52 us -> none  [the longest x1 2.09 us: per_device(): jnp.sum(got_far_w.astype(f32), axis=0).astype(bf16)]
    unnamed x42 -> x56, local copies, waits for them, and re-layouts: 4.65 us -> 6.76 us
  transfers between devices with their start and end apart: 22 -> 27, of which waited for: 14 -> 15; matrix products, arithmetic and copies ran while one was open for 23% -> 15% of each run, Pallas kernels for 6% -> 5%
where the time goes in v2:
time: 201 us; the launch traced here: 200 us
  waiting for transfers between devices  80.5 us (40%)
  starting transfers between devices  44.3 us (22%)
  matrix products  30.1 us (15%)
  Pallas kernels  26 us (13%)
  local copies, waits for them, and re-layouts  12.4 us (6%)
  other arithmetic  5.43 us (3%)
    ppermute x23, waiting for transfers between devices, move(): return lax.ppermute(rows, both, route)  59.7 us
    dot_general x19, matrix products, mm(): return lax.dot_general(a, b, dims, preferred_element_type=f32)  30.1 us
    ppermute x23, starting transfers between devices, move(): return lax.ppermute(rows, both, route)  26.9 us
    all_to_all x4, waiting for transfers between devices, exchange(): lax.all_to_all(blocks, 'ctx', 0, 0, axis_index_groups=halves, tiled=True)  20.8 us
    all_to_all x4, starting transfers between devices, exchange(): lax.all_to_all(blocks, 'ctx', 0, 0, axis_index_groups=halves, tiled=True)  17.4 us
    pallas_call x1, Pallas kernels, backward(): pl.pallas_call(functools.partial(backward_kernel, scale), grid=(width //...  11.1 us
    pallas_call x1, Pallas kernels, forward(): pl.pallas_call(functools.partial(forward_kernel, scale), grid=(width // B...  7.63 us
    unnamed x56, local copies, waits for them, and re-layouts  6.76 us
  transfers between devices with their start and end apart: 27, of which 15 were waited for; matrix products, arithmetic and copies ran while one was open for 15% of the time, Pallas kernels for 5%

profile of v2, /device:TPU:0, one launch (start us, length us, event | category | flops | bytes accessed | tf_op | source)
XLA Modules:
  0.0 199.8 jit_solution(1865255265342889846)
XLA Ops:
  0.7 1.1 constant_dynamic-slice_fusion.1
  2.6 4.1 %collective-permute-start.1 = (bf16[144,1024]{1,0:T(8,128)(2,1)S(1)}, bf16[144,1024]{1,0:T(8,128)(2,1)}, u32[]{:S(2)}, u32[]{:S(2)}) collective-permute-start(bf16[144,1024]{1,0:T(8,128)(2,1)S(1)} %pad_maximum_fusion.5), channel_id=1, source_target_pairs={{0,16},{1,17},{2,18},{3,19},{4,20},{5,21},{6,22},{7,23},{8,24},{9,... | collective-permute-start | bytes 884744 | tf_op jit(solution)/shard_map/ppermute | solution.py:357
  6.7 1.3 collective-permute-start
  8.7 1.0 constant_dynamic-slice_fusion
  9.6 10.5 %collective-permute-done.1 = bf16[144,1024]{1,0:T(8,128)(2,1)} collective-permute-done((bf16[144,1024]{1,0:T(8,128)(2,1)S(1)}, bf16[144,1024]{1,0:T(8,128)(2,1)}, u32[]{:S(2)}, u32[]{:S(2)}) %collective-permute-start.1) | collective-permute-done | bytes 294944 | tf_op jit(solution)/shard_map/ppermute | solution.py:357
  20.8 1.0 slice.54
  22.9 0.9 collective-permute-done.2
  23.9 1.5 add_convert_fusion.1
  25.4 3.8 %all-to-all-start = ((bf16[8,64,1024]{2,1,0:T(8,128)(2,1)}), bf16[8,64,1024]{2,1,0:T(8,128)(2,1)S(1)}, u32[]{:S(2)}, u32[]{:S(2)}) async-start(bf16[8,64,1024]{2,1,0:T(8,128)(2,1)} %bitcast.53), calls=%async_computation | async-start | bytes 2097152 | tf_op jit(solution)/shard_map/all_to_all | solution.py:360
  29.4 3.6 %collective-permute-start.4 = (bf16[128,1024]{1,0:T(8,128)(2,1)S(1)}, bf16[128,1024]{1,0:T(8,128)(2,1)}, u32[]{:S(2)}, u32[]{:S(2)}) collective-permute-start(bf16[128,1024]{1,0:T(8,128)(2,1)S(1)} %constant_dynamic-slice_fusion), channel_id=1, source_target_pairs={{0,16},{1,17},{2,18},{3,19},{4,20},{5,21},{6,22},{7,23},{8,24},{9,... | collective-permute-start | bytes 786440 | tf_op jit(solution)/shard_map/ppermute | solution.py:357
  33.0 2.9 %fusion.20 = f32[512,1024]{1,0:T(8,128)} fusion(bf16[256,1024]{1,0:T(8,128)(2,1)} %param.11, s32[256]{0:T(256)S(1)} %get-tuple-element.146), kind=kOutput, calls=%fused_computation.49 | convolution fusion | flops 268566528 | bytes 2622464 | tf_op jit(solution)/shard_map/dot_general | solution.py:54
  35.9 12.9 %all-to-all-done = bf16[8,64,1024]{2,1,0:T(8,128)(2,1)S(1)} async-done(((bf16[8,64,1024]{2,1,0:T(8,128)(2,1)}), bf16[8,64,1024]{2,1,0:T(8,128)(2,1)S(1)}, u32[]{:S(2)}, u32[]{:S(2)}) %all-to-all-start) | async-done | bytes 1048608 | tf_op jit(solution)/shard_map/all_to_all | solution.py:360
  49.5 3.2 %convolution_convert_fusion.5.v_own = bf16[256,1024]{1,0:T(8,128)(2,1)} fusion(bf16[256,1024]{1,0:T(8,128)(2,1)S(1)} %convolution_convert_fusion.2, bf16[1024,1024]{1,0:T(8,128)(2,1)} %param.13), kind=kOutput, calls=%fused_computation.15 | convolution fusion | flops 537133056 | bytes 3145728 | tf_op jit(solution)/shard_map/dot_general | solution.py:54
  52.7 1.6 convolution_convert_fusion.6.k_own
  54.3 2.5 %add_convert_fusion = bf16[512,1024]{1,0:T(8,128)(2,1)} fusion(f32[512,1024]{1,0:T(8,128)S(1)} %copy-done.16, bf16[128,1024]{1,0:T(8,128)(2,1)S(1)} %collective-permute-done.5, bf16[128,1024]{1,0:T(8,128)(2,1)} %collective-permute-done.4, s32[256]{0:T(256)S(1)} %add_select_fusion.1), kind=kOutput, calls=%fused_computation.2 | convolution fusion | flops 270663680 | bytes 3671040 | tf_op jit(solution)/shard_map/dot_general | solution.py:54
  56.8 1.7 collective-permute-done.3
  58.5 0.8 copy-done.24
  59.4 4.6 %all-to-all-start.1 = ((bf16[8,64,1024]{2,1,0:T(8,128)(2,1)}), bf16[8,64,1024]{2,1,0:T(8,128)(2,1)S(1)}, u32[]{:S(2)}, u32[]{:S(2)}) async-start(bf16[8,64,1024]{2,1,0:T(8,128)(2,1)} %bitcast.54), calls=%async_computation.1 | async-start | bytes 2097152 | tf_op jit(solution)/shard_map/all_to_all | solution.py:360
  64.0 0.8 fusion.22.pick
  65.4 3.3 %convolution_convert_fusion.3.v_prev = bf16[256,1024]{1,0:T(8,128)(2,1)} fusion(bf16[256,1024]{1,0:T(8,128)(2,1)} %copy-done.24, bf16[1024,1024]{1,0:T(8,128)(2,1)} %param.13), kind=kOutput, calls=%fused_computation.13 | convolution fusion | flops 537133056 | bytes 3145728 | tf_op jit(solution)/shard_map/dot_general | solution.py:54
  68.7 1.6 convolution_convert_fusion.4.k_prev
  70.3 7.6 %forward.1 = (f32[16,256]{1,0:T(8,128)}, f32[16,256]{1,0:T(8,128)}, f32[1024,256]{1,0:T(8,128)}, bf16[16,512,256]{2,1,0:T(8,128)(2,1)}) custom-call(bf16[256,1024]{1,0:T(8,128)(2,1)} %convolution_convert_fusion.6.k_own, bf16[256,1024]{1,0:T(8,128)(2,1)} %convolution_convert_fusion.5.v_own, bf16[256,1024]{1,0:T(8,128)(2,1)} %convolution_convert_fusion.4.k_prev, ...), custom_call_target="tpu_custom_call" | custom-call | tf_op jit(solution)/shard_map/forward/pallas_call | solution.py:121
  77.9 1.4 all-to-all-done.1
  79.3 1.0 copy-done.17
  80.3 3.1 %cotangent.1 = (bf16[256,1024]{1,0:T(8,128)(2,1)}, bf16[1024,256]{1,0:T(8,128)(2,1)}, f32[40,256]{1,0:T(8,128)}) custom-call(bf16[512,1024]{1,0:T(8,128)(2,1)} %bitcast.51, bf16[256,512]{1,0:T(8,128)(2,1)} %fusion.22.pick, f32[1024,256]{1,0:T(8,128)} %get-tuple-element.77.out_t, f32[16,256]{1,0:T(8,128)} %get-tuple-element.78.lse, f32[1,256]{1,0:T(1,128)} %bitcast.58), custom_call_target="tpu_custom_call" | custom-call | tf_op jit(solution)/shard_map/cotangent/pallas_call | solution.py:157
  83.4 1.5 collective-permute-start.7
  84.9 3.0 %collective-permute-done.7 = f32[40,256]{1,0:T(8,128)S(1)} collective-permute-done((f32[40,256]{1,0:T(8,128)}, f32[40,256]{1,0:T(8,128)S(1)}, u32[]{:S(2)}, u32[]{:S(2)}) %collective-permute-start.7) | collective-permute-done | bytes 40992 | tf_op jit(solution)/shard_map/ppermute | solution.py:357
  87.9 0.9 broadcast_in_dim.41
  88.8 4.7 %all-to-all-start.2 = ((f32[8,2,40,256]{3,2,1,0:T(8,128)}), f32[8,2,40,256]{3,2,1,0:T(8,128)S(1)}, u32[]{:S(2)}, u32[]{:S(2)}) async-start(f32[8,2,40,256]{3,2,1,0:T(8,128)} %broadcast_in_dim.41), calls=%async_computation.2 | async-start | bytes 1310720 | tf_op jit(solution)/shard_map/all_to_all | solution.py:360
  93.6 0.8 copy.14.wanted
  94.4 2.7 %fusion.2 = bf16[512,512]{1,0:T(8,128)(2,1)} fusion(s32[512]{0:T(512)S(1)} %get-tuple-element.143, bf16[256,1024]{1,0:T(8,128)(2,1)S(1)} %copy-done.21, bf16[256,1024]{1,0:T(8,128)(2,1)} %copy-done.24), kind=kOutput, calls=%fused_computation.10 | convolution fusion | flops 539754496 | bytes 1574912 | tf_op jit(solution)/shard_map/dot_general | solution.py:54
  97.1 0.8 fusion.3.x_t
  97.8 6.6 %all-to-all-done.2 = f32[8,2,40,256]{3,2,1,0:T(8,128)S(1)} async-done(((f32[8,2,40,256]{3,2,1,0:T(8,128)}), f32[8,2,40,256]{3,2,1,0:T(8,128)S(1)}, u32[]{:S(2)}, u32[]{:S(2)}) %all-to-all-start.2) | async-done | bytes 655392 | tf_op jit(solution)/shard_map/all_to_all | solution.py:360
  104.4 0.8 copy-done.18
  105.2 11.1 %backward.1.grads = bf16[2,512,1024]{2,1,0:T(8,128)(2,1)} custom-call(f32[16,40,256]{2,1,0:T(8,128)} %bitcast.55, f32[256,1]{1,0:T(8,128)} %copy.14.wanted, f32[40,256]{1,0:T(8,128)} %get-tuple-element.80.mine, f32[16,256]{1,0:T(8,128)} %get-tuple-element.82.inverse, bf16[16,512,256]{2,1,0:T(8,128)(2,1)} %get-tuple-element.83.probs, ...), custom_call_target="tpu_custom_call" | custom-call | tf_op jit(solution)/shard_map/backward/pallas_call | solution.py:241
  116.3 1.9 fusion.11
  118.3 0.7 fusion.5
  122.0 0.7 fusion.12
  122.8 0.7 fusion.4.y_own
  123.6 1.4 collective-permute-done.9.other_k
  125.0 1.3 fold.3
  126.3 4.3 %collective-permute-done.8.y_next = bf16[256,1024]{1,0:T(8,128)(2,1)S(1)} collective-permute-done((bf16[256,1024]{1,0:T(8,128)(2,1)S(1)}, bf16[256,1024]{1,0:T(8,128)(2,1)S(1)}, u32[]{:S(2)}, u32[]{:S(2)}) %collective-permute-start.8) | collective-permute-done | bytes 524320 | tf_op jit(solution)/shard_map/ppermute | solution.py:357
  130.6 1.5 place_rows.1
  132.1 4.3 %all-to-all-start.3 = ((bf16[8,64,1024]{2,1,0:T(8,128)(2,1)}), bf16[8,64,1024]{2,1,0:T(8,128)(2,1)}, u32[]{:S(2)}, u32[]{:S(2)}) async-start(bf16[8,64,1024]{2,1,0:T(8,128)(2,1)} %bitcast.18), calls=%async_computation.3 | async-start | bytes 2097152 | tf_op jit(solution)/shard_map/all_to_all | solution.py:360
  136.4 1.9 collective-permute-start.11
  138.3 1.5 collective-permute-start.12
  139.7 1.5 collective-permute-start.13
  141.2 14.1 %collective-permute-done.13.refs_5_ = bf16[256,512]{1,0:T(8,128)(2,1)} collective-permute-done((bf16[256,512]{1,0:T(8,128)(2,1)}, bf16[256,512]{1,0:T(8,128)(2,1)}, u32[]{:S(2)}, u32[]{:S(2)}) %collective-permute-start.13) | collective-permute-done | bytes 262176 | tf_op jit(solution)/shard_map/ppermute | solution.py:357
  155.3 2.8 %collective-permute-done.11.refs_1_ = bf16[256,768]{1,0:T(8,128)(2,1)S(1)} collective-permute-done((bf16[256,768]{1,0:T(8,128)(2,1)}, bf16[256,768]{1,0:T(8,128)(2,1)S(1)}, u32[]{:S(2)}, u32[]{:S(2)}) %collective-permute-start.11) | collective-permute-done | bytes 393248 | tf_op jit(solution)/shard_map/ppermute | solution.py:357
  158.1 0.9 copy-done.3
  159.1 1.3 fold.4
  163.1 1.7 fusion.24
  164.9 1.8 fusion.19
  166.9 1.5 collective-permute-start.14
  168.4 1.3 collective-permute-start.15
  169.7 1.3 collective-permute-start.16
  171.0 3.9 %collective-permute-done.16.refs_5_ = bf16[128,512]{1,0:T(8,128)(2,1)S(1)} collective-permute-done((bf16[128,512]{1,0:T(8,128)(2,1)S(1)}, bf16[128,512]{1,0:T(8,128)(2,1)S(1)}, u32[]{:S(2)}, u32[]{:S(2)}) %collective-permute-start.16) | collective-permute-done | bytes 131104 | tf_op jit(solution)/shard_map/ppermute | solution.py:357
  175.6 2.3 %collective-permute-start.21 = (bf16[128,1024]{1,0:T(8,128)(2,1)S(1)}, bf16[128,1024]{1,0:T(8,128)(2,1)S(1)}, u32[]{:S(2)}, u32[]{:S(2)}) collective-permute-start(bf16[128,1024]{1,0:T(8,128)(2,1)S(1)} %fusion.8), channel_id=1, source_target_pairs={{0,16},{1,17},{2,18},{3,19},{4,20},{5,21},{6,22},{7,23},{8,24},{9,... | collective-permute-start | bytes 786440 | tf_op jit(solution)/shard_map/ppermute | solution.py:357
  178.0 1.4 collective-permute-start.18
  179.3 1.3 collective-permute-start.19
  180.6 0.8 collective-permute-start.20
  181.5 8.2 %collective-permute-done.21 = bf16[128,1024]{1,0:T(8,128)(2,1)S(1)} collective-permute-done((bf16[128,1024]{1,0:T(8,128)(2,1)S(1)}, bf16[128,1024]{1,0:T(8,128)(2,1)S(1)}, u32[]{:S(2)}, u32[]{:S(2)}) %collective-permute-start.21) | collective-permute-done | bytes 262176 | tf_op jit(solution)/shard_map/ppermute | solution.py:357
  189.7 0.8 fusion.10
  190.7 8.3 %collective-permute-done.22 = bf16[32,2048]{1,0:T(8,128)(2,1)S(1)} collective-permute-done((bf16[32,2048]{1,0:T(8,128)(2,1)S(1)}, bf16[32,2048]{1,0:T(8,128)(2,1)S(1)}, u32[]{:S(2)}, u32[]{:S(2)}) %collective-permute-start.22) | collective-permute-done | bytes 131104 | tf_op jit(solution)/shard_map/ppermute | solution.py:357
  (111 shorter events, 12.5 us)
Async XLA Ops:
  0.6 52.1 %copy-start = (bf16[1024,1024]{1,0:T(8,128)(2,1)S(1)}, bf16[1024,1024]{1,0:T(8,128)(2,1)}, u32[]{:S(2)}) copy-start(bf16[1024,1024]{1,0:T(8,128)(2,1)} %param.12) | copy-start | bytes 6291460
  0.6 21.7 %copy-start.19 = (bf16[256,1024]{1,0:T(8,128)(2,1)S(1)}, bf16[256,1024]{1,0:T(8,128)(2,1)}, u32[]{:S(2)}) copy-start(bf16[256,1024]{1,0:T(8,128)(2,1)} %param.10) | copy-start | bytes 1572868
  2.6 17.5 %collective-permute-start.1 = (bf16[144,1024]{1,0:T(8,128)(2,1)S(1)}, bf16[144,1024]{1,0:T(8,128)(2,1)}, u32[]{:S(2)}, u32[]{:S(2)}) collective-permute-start(bf16[144,1024]{1,0:T(8,128)(2,1)S(1)} %pad_maximum_fusion.5), channel_id=1, source_target_pairs={{0,16},{1,17},{2,18},{3,19},{4,20},{5,21},{6,22},{7,23},{8,24},{9,... | collective-permute-start | bytes 884744 | tf_op jit(solution)/shard_map/ppermute | solution.py:357
  6.7 18.7 %collective-permute-start = (s32[256]{0:T(256)}, s32[256]{0:T(256)S(1)}, u32[]{:S(2)}, u32[]{:S(2)}) collective-permute-start(s32[256]{0:T(256)} %bitcast.62), channel_id=1, source_target_pairs={{0,0},{1,1},{14,2},{19,3},{30,4},{3,5},{16,6},{17,7},{2,8},{31,9},... | collective-permute-start | bytes 3080 | tf_op jit(solution)/shard_map/ppermute | solution.py:357
  22.3 1.6 collective-permute-start.2
  25.4 23.4 %all-to-all-start = ((bf16[8,64,1024]{2,1,0:T(8,128)(2,1)}), bf16[8,64,1024]{2,1,0:T(8,128)(2,1)S(1)}, u32[]{:S(2)}, u32[]{:S(2)}) async-start(bf16[8,64,1024]{2,1,0:T(8,128)(2,1)} %bitcast.53), calls=%async_computation | async-start | bytes 2097152 | tf_op jit(solution)/shard_map/all_to_all | solution.py:360
  29.4 19.9 %collective-permute-start.4 = (bf16[128,1024]{1,0:T(8,128)(2,1)S(1)}, bf16[128,1024]{1,0:T(8,128)(2,1)}, u32[]{:S(2)}, u32[]{:S(2)}) collective-permute-start(bf16[128,1024]{1,0:T(8,128)(2,1)S(1)} %constant_dynamic-slice_fusion), channel_id=1, source_target_pairs={{0,16},{1,17},{2,18},{3,19},{4,20},{5,21},{6,22},{7,23},{8,24},{9,... | collective-permute-start | bytes 786440 | tf_op jit(solution)/shard_map/ppermute | solution.py:357
  49.3 5.0 %copy-start.20 = (bf16[256,1024]{1,0:T(8,128)(2,1)}, bf16[256,1024]{1,0:T(8,128)(2,1)S(1)}, u32[]{:S(2)}) copy-start(bf16[256,1024]{1,0:T(8,128)(2,1)S(1)} %convolution_convert_fusion.2) | copy-start | bytes 1572868
  49.3 9.2 %collective-permute-start.3 = (bf16[256,1024]{1,0:T(8,128)(2,1)S(1)}, bf16[256,1024]{1,0:T(8,128)(2,1)S(1)}, u32[]{:S(2)}, u32[]{:S(2)}) collective-permute-start(bf16[256,1024]{1,0:T(8,128)(2,1)S(1)} %convolution_convert_fusion.2), channel_id=1, source_target_pairs={{0,8},{1,5},{8,16},{5,13},{16,24},{13,21},{24,26},{21,29},{26,18},... | collective-permute-start | bytes 1572872 | tf_op jit(solution)/shard_map/ppermute | solution.py:357
  49.4 4.9 %collective-permute-start.5 = (bf16[128,1024]{1,0:T(8,128)(2,1)}, bf16[128,1024]{1,0:T(8,128)(2,1)S(1)}, u32[]{:S(2)}, u32[]{:S(2)}) collective-permute-start(bf16[128,1024]{1,0:T(8,128)(2,1)} %collective-permute-done.4), channel_id=1, source_target_pairs={{0,1},{1,0},{2,3},{3,2},{4,5},{5,4},{6,7},{7,6},{8,9},{9,8},{10,11... | collective-permute-start | bytes 786440 | tf_op jit(solution)/shard_map/ppermute | solution.py:357
  52.7 1.6 copy-start.16
  58.5 0.8 copy-start.24
  59.4 19.9 %all-to-all-start.1 = ((bf16[8,64,1024]{2,1,0:T(8,128)(2,1)}), bf16[8,64,1024]{2,1,0:T(8,128)(2,1)S(1)}, u32[]{:S(2)}, u32[]{:S(2)}) async-start(bf16[8,64,1024]{2,1,0:T(8,128)(2,1)} %bitcast.54), calls=%async_computation.1 | async-start | bytes 2097152 | tf_op jit(solution)/shard_map/all_to_all | solution.py:360
  64.0 4.7 %copy-start.25 = (bf16[256,1024]{1,0:T(8,128)(2,1)S(1)}, bf16[256,1024]{1,0:T(8,128)(2,1)}, u32[]{:S(2)}) copy-start(bf16[256,1024]{1,0:T(8,128)(2,1)} %copy-done.24) | copy-start | bytes 1572868
  79.2 1.0 copy-start.17
  80.3 13.3 %copy-start.23 = (f32[256]{0:T(256)S(1)}, f32[256]{0:T(256)}, u32[]{:S(2)}) copy-start(f32[256]{0:T(256)} %convert_element_type.125) | copy-start | bytes 3076
  83.3 11.0 %copy-start.21 = (bf16[256,1024]{1,0:T(8,128)(2,1)S(1)}, bf16[256,1024]{1,0:T(8,128)(2,1)}, u32[]{:S(2)}) copy-start(bf16[256,1024]{1,0:T(8,128)(2,1)} %copy-done.20) | copy-start | bytes 1572868
  83.3 1.5 collective-permute-start.6
  83.4 4.5 %collective-permute-start.7 = (f32[40,256]{1,0:T(8,128)}, f32[40,256]{1,0:T(8,128)S(1)}, u32[]{:S(2)}, u32[]{:S(2)}) collective-permute-start(f32[40,256]{1,0:T(8,128)} %get-tuple-element.80.mine), channel_id=1, source_target_pairs={{0,17},{1,16},{2,19},{3,18},{4,21},{5,20},{6,23},{7,22},{8,25},{9,... | collective-permute-start | bytes 122888 | tf_op jit(solution)/shard_map/ppermute | solution.py:357
  88.8 15.6 %all-to-all-start.2 = ((f32[8,2,40,256]{3,2,1,0:T(8,128)}), f32[8,2,40,256]{3,2,1,0:T(8,128)S(1)}, u32[]{:S(2)}, u32[]{:S(2)}) async-start(f32[8,2,40,256]{3,2,1,0:T(8,128)} %broadcast_in_dim.41), calls=%async_computation.2 | async-start | bytes 1310720 | tf_op jit(solution)/shard_map/all_to_all | solution.py:360
  94.4 2.7 %copy-start.22 = (bf16[256,1024]{1,0:T(8,128)(2,1)S(1)}, bf16[256,1024]{1,0:T(8,128)(2,1)}, u32[]{:S(2)}) copy-start(bf16[256,1024]{1,0:T(8,128)(2,1)} %copy-done.20) | copy-start | bytes 1572868
  94.4 2.7 %copy-start.26 = (bf16[256,1024]{1,0:T(8,128)(2,1)S(1)}, bf16[256,1024]{1,0:T(8,128)(2,1)}, u32[]{:S(2)}) copy-start(bf16[256,1024]{1,0:T(8,128)(2,1)} %copy-done.24) | copy-start | bytes 1572868
  104.4 0.8 copy-start.18
  105.2 13.0 %copy-start.15 = (bf16[1024,1024]{1,0:T(8,128)(2,1)S(1)}, bf16[1024,1024]{1,0:T(8,128)(2,1)}, u32[]{:S(2)}) copy-start(bf16[1024,1024]{1,0:T(8,128)(2,1)} %param.13) | copy-start | bytes 6291460
  116.3 2.0 copy-start.1
  118.3 1.0 copy-start.27
  120.7 2.8 %collective-permute-start.10 = (bf16[512,1024]{1,0:T(8,128)(2,1)S(1)}, bf16[512,1024]{1,0:T(8,128)(2,1)S(1)}, u32[]{:S(2)}, u32[]{:S(2)}) collective-permute-start(bf16[512,1024]{1,0:T(8,128)(2,1)S(1)} %convolution_convert_fusion), channel_id=1, source_target_pairs={{0,1},{1,0},{2,3},{3,2},{4,5},{5,4},{6,7},{7,6},{8,9},{9,8},{10,11... | collective-permute-start | bytes 3145736 | tf_op jit(solution)/shard_map/ppermute | solution.py:357
  120.8 4.1 %collective-permute-start.9 = (bf16[512,1024]{1,0:T(8,128)(2,1)S(1)}, bf16[512,1024]{1,0:T(8,128)(2,1)S(1)}, u32[]{:S(2)}, u32[]{:S(2)}) collective-permute-start(bf16[512,1024]{1,0:T(8,128)(2,1)S(1)} %convolution_convert_fusion.1), channel_id=1, source_target_pairs={{0,1},{1,0},{2,3},{3,2},{4,5},{5,4},{6,7},{7,6},{8,9},{9,8},{10,11... | collective-permute-start | bytes 3145736 | tf_op jit(solution)/shard_map/ppermute | solution.py:357
  121.4 9.2 %collective-permute-start.8 = (bf16[256,1024]{1,0:T(8,128)(2,1)S(1)}, bf16[256,1024]{1,0:T(8,128)(2,1)S(1)}, u32[]{:S(2)}, u32[]{:S(2)}) collective-permute-start(bf16[256,1024]{1,0:T(8,128)(2,1)S(1)} %fusion.5), channel_id=1, source_target_pairs={{8,0},{5,1},{16,8},{13,5},{24,16},{21,13},{26,24},{29,21},{18,26},... | collective-permute-start | bytes 1572872 | tf_op jit(solution)/shard_map/ppermute | solution.py:357
  126.2 5.9 %copy-start.2 = (bf16[256,512]{1,0:T(8,128)(2,1)}, bf16[256,512]{1,0:T(8,128)(2,1)S(1)}, u32[]{:S(2)}) copy-start(bf16[256,512]{1,0:T(8,128)(2,1)S(1)} %get-tuple-element.100.refs_4_) | copy-start | bytes 786436
  126.3 5.8 %copy-start.8 = (bf16[256,768]{1,0:T(8,128)(2,1)}, bf16[256,768]{1,0:T(8,128)(2,1)S(1)}, u32[]{:S(2)}) copy-start(bf16[256,768]{1,0:T(8,128)(2,1)S(1)} %get-tuple-element.99) | copy-start | bytes 1179652
  126.3 5.8 %copy-start.9 = (bf16[256,768]{1,0:T(8,128)(2,1)}, bf16[256,768]{1,0:T(8,128)(2,1)S(1)}, u32[]{:S(2)}) copy-start(bf16[256,768]{1,0:T(8,128)(2,1)S(1)} %get-tuple-element.97) | copy-start | bytes 1179652
  126.3 5.8 %copy-start.10 = (bf16[256,512]{1,0:T(8,128)(2,1)}, bf16[256,512]{1,0:T(8,128)(2,1)S(1)}, u32[]{:S(2)}) copy-start(bf16[256,512]{1,0:T(8,128)(2,1)S(1)} %get-tuple-element.101) | copy-start | bytes 786436
  132.1 31.0 %all-to-all-start.3 = ((bf16[8,64,1024]{2,1,0:T(8,128)(2,1)}), bf16[8,64,1024]{2,1,0:T(8,128)(2,1)}, u32[]{:S(2)}, u32[]{:S(2)}) async-start(bf16[8,64,1024]{2,1,0:T(8,128)(2,1)} %bitcast.18), calls=%async_computation.3 | async-start | bytes 2097152 | tf_op jit(solution)/shard_map/all_to_all | solution.py:360
  136.4 21.7 %collective-permute-start.11 = (bf16[256,768]{1,0:T(8,128)(2,1)}, bf16[256,768]{1,0:T(8,128)(2,1)S(1)}, u32[]{:S(2)}, u32[]{:S(2)}) collective-permute-start(bf16[256,768]{1,0:T(8,128)(2,1)} %copy-done.9), channel_id=1, source_target_pairs={{0,2},{1,3},{2,0},{3,1},{4,6},{5,7},{6,4},{7,5},{8,10},{9,11},{10,... | collective-permute-start | bytes 1179656 | tf_op jit(solution)/shard_map/ppermute | solution.py:357
  138.3 19.8 %collective-permute-start.12 = (bf16[256,768]{1,0:T(8,128)(2,1)}, bf16[256,768]{1,0:T(8,128)(2,1)}, u32[]{:S(2)}, u32[]{:S(2)}) collective-permute-start(bf16[256,768]{1,0:T(8,128)(2,1)} %copy-done.8), channel_id=1, source_target_pairs={{0,4},{1,5},{2,6},{3,7},{4,0},{5,1},{6,2},{7,3},{8,12},{9,13},{10,... | collective-permute-start | bytes 1179656 | tf_op jit(solution)/shard_map/ppermute | solution.py:357
  139.7 15.5 %collective-permute-start.13 = (bf16[256,512]{1,0:T(8,128)(2,1)}, bf16[256,512]{1,0:T(8,128)(2,1)}, u32[]{:S(2)}, u32[]{:S(2)}) collective-permute-start(bf16[256,512]{1,0:T(8,128)(2,1)} %copy-done.10), channel_id=1, source_target_pairs={{0,8},{1,9},{2,10},{3,11},{4,12},{5,13},{6,14},{7,15},{8,0},{9,1},... | collective-permute-start | bytes 786440 | tf_op jit(solution)/shard_map/ppermute | solution.py:357
  158.1 1.0 copy-start.3
  160.4 0.7 copy-start.4
  161.0 0.7 copy-start.6
  161.7 0.7 copy-start.11
  162.4 0.7 copy-start.13
  164.8 2.0 %copy-start.14 = (bf16[128,768]{1,0:T(8,128)(2,1)S(1)}, bf16[128,768]{1,0:T(8,128)(2,1)}, u32[]{:S(2)}) copy-start(bf16[128,768]{1,0:T(8,128)(2,1)} %copy-done.13) | copy-start | bytes 589828
  164.9 3.6 %copy-start.12 = (bf16[128,768]{1,0:T(8,128)(2,1)S(1)}, bf16[128,768]{1,0:T(8,128)(2,1)}, u32[]{:S(2)}) copy-start(bf16[128,768]{1,0:T(8,128)(2,1)} %copy-done.11) | copy-start | bytes 589828
  166.7 11.1 %copy-start.5 = (bf16[128,768]{1,0:T(8,128)(2,1)S(1)}, bf16[128,768]{1,0:T(8,128)(2,1)}, u32[]{:S(2)}) copy-start(bf16[128,768]{1,0:T(8,128)(2,1)} %copy-done.4) | copy-start | bytes 589828
  166.7 11.1 %copy-start.7 = (bf16[128,768]{1,0:T(8,128)(2,1)S(1)}, bf16[128,768]{1,0:T(8,128)(2,1)}, u32[]{:S(2)}) copy-start(bf16[128,768]{1,0:T(8,128)(2,1)} %copy-done.6) | copy-start | bytes 589828
  166.8 8.6 %collective-permute-start.17 = (bf16[256,1024]{1,0:T(8,128)(2,1)S(1)}, bf16[256,1024]{1,0:T(8,128)(2,1)S(1)}, u32[]{:S(2)}, u32[]{:S(2)}) collective-permute-start(bf16[256,1024]{1,0:T(8,128)(2,1)S(1)} %pad_maximum_fusion.3), channel_id=1, source_target_pairs={{0,1},{1,0},{2,3},{3,2},{4,5},{5,4},{6,7},{7,6},{8,9},{9,8},{10,11... | collective-permute-start | bytes 1572872 | tf_op jit(solution)/shard_map/ppermute | solution.py:357
  166.9 8.1 %collective-permute-start.14 = (bf16[128,768]{1,0:T(8,128)(2,1)S(1)}, bf16[128,768]{1,0:T(8,128)(2,1)S(1)}, u32[]{:S(2)}, u32[]{:S(2)}) collective-permute-start(bf16[128,768]{1,0:T(8,128)(2,1)S(1)} %copy-done.14), channel_id=1, source_target_pairs={{0,4},{1,5},{2,6},{3,7},{4,0},{5,1},{6,2},{7,3},{8,12},{9,13},{10,... | collective-permute-start | bytes 589832 | tf_op jit(solution)/shard_map/ppermute | solution.py:357
  168.4 7.0 %collective-permute-start.15 = (bf16[128,768]{1,0:T(8,128)(2,1)S(1)}, bf16[128,768]{1,0:T(8,128)(2,1)S(1)}, u32[]{:S(2)}, u32[]{:S(2)}) collective-permute-start(bf16[128,768]{1,0:T(8,128)(2,1)S(1)} %copy-done.12), channel_id=1, source_target_pairs={{0,8},{1,9},{2,10},{3,11},{4,12},{5,13},{6,14},{7,15},{8,0},{9,1},... | collective-permute-start | bytes 589832 | tf_op jit(solution)/shard_map/ppermute | solution.py:357
  169.7 5.3 %collective-permute-start.16 = (bf16[128,512]{1,0:T(8,128)(2,1)S(1)}, bf16[128,512]{1,0:T(8,128)(2,1)S(1)}, u32[]{:S(2)}, u32[]{:S(2)}) collective-permute-start(bf16[128,512]{1,0:T(8,128)(2,1)S(1)} %get-tuple-element.113), channel_id=1, source_target_pairs={{0,2},{1,3},{2,0},{3,1},{4,6},{5,7},{6,4},{7,5},{8,10},{9,11},{10,... | collective-permute-start | bytes 393224 | tf_op jit(solution)/shard_map/ppermute | solution.py:357
  175.6 14.1 %collective-permute-start.21 = (bf16[128,1024]{1,0:T(8,128)(2,1)S(1)}, bf16[128,1024]{1,0:T(8,128)(2,1)S(1)}, u32[]{:S(2)}, u32[]{:S(2)}) collective-permute-start(bf16[128,1024]{1,0:T(8,128)(2,1)S(1)} %fusion.8), channel_id=1, source_target_pairs={{0,16},{1,17},{2,18},{3,19},{4,20},{5,21},{6,22},{7,23},{8,24},{9,... | collective-permute-start | bytes 786440 | tf_op jit(solution)/shard_map/ppermute | solution.py:357
  178.0 12.5 %collective-permute-start.18 = (bf16[64,768]{1,0:T(8,128)(2,1)S(1)}, bf16[64,768]{1,0:T(8,128)(2,1)S(1)}, u32[]{:S(2)}, u32[]{:S(2)}) collective-permute-start(bf16[64,768]{1,0:T(8,128)(2,1)S(1)} %get-tuple-element.122), channel_id=1, source_target_pairs={{0,8},{1,9},{2,10},{3,11},{4,12},{5,13},{6,14},{7,15},{8,0},{9,1},... | collective-permute-start | bytes 294920 | tf_op jit(solution)/shard_map/ppermute | solution.py:357
  179.3 11.2 %collective-permute-start.19 = (bf16[64,768]{1,0:T(8,128)(2,1)S(1)}, bf16[64,768]{1,0:T(8,128)(2,1)S(1)}, u32[]{:S(2)}, u32[]{:S(2)}) collective-permute-start(bf16[64,768]{1,0:T(8,128)(2,1)S(1)} %get-tuple-element.124), channel_id=1, source_target_pairs={{0,2},{1,3},{2,0},{3,1},{4,6},{5,7},{6,4},{7,5},{8,10},{9,11},{10,... | collective-permute-start | bytes 294920 | tf_op jit(solution)/shard_map/ppermute | solution.py:357
  180.6 9.9 %collective-permute-start.20 = (bf16[64,512]{1,0:T(8,128)(2,1)S(1)}, bf16[64,512]{1,0:T(8,128)(2,1)S(1)}, u32[]{:S(2)}, u32[]{:S(2)}) collective-permute-start(bf16[64,512]{1,0:T(8,128)(2,1)S(1)} %get-tuple-element.126), channel_id=1, source_target_pairs={{0,4},{1,5},{2,6},{3,7},{4,0},{5,1},{6,2},{7,3},{8,12},{9,13},{10,... | collective-permute-start | bytes 196616 | tf_op jit(solution)/shard_map/ppermute | solution.py:357
  190.7 8.4 %collective-permute-start.22 = (bf16[32,2048]{1,0:T(8,128)(2,1)S(1)}, bf16[32,2048]{1,0:T(8,128)(2,1)S(1)}, u32[]{:S(2)}, u32[]{:S(2)}) collective-permute-start(bf16[32,2048]{1,0:T(8,128)(2,1)S(1)} %slice.104), channel_id=1, source_target_pairs={{0,16},{1,17},{2,18},{3,19},{4,20},{5,21},{6,22},{7,23},{8,24},{9,... | collective-permute-start | bytes 393224 | tf_op jit(solution)/shard_map/ppermute | solution.py:357

commit v3 on v2

--- a/solution.py
+++ b/solution.py
@@ -463,19 +463,20 @@
         if turn == 0:
             y_next, cuts = lax.optimization_barrier((y_next, cuts))
             sent_y = place_rows(jnp.transpose(pick), y_own, y_next)
-            got_y = exchange(sent_y.reshape(near, 2 * cap, width)).reshape(slots, width)
-        if turn == 1:
-            got_y, cuts = lax.optimization_barrier((got_y, cuts))
-            rows_far = mm(send_far, got_y)
-            rows_near = mm(send, got_y)
-            from_core = jnp.concatenate([their_part(rows_far), their_part(rows_near)], axis=0)
-            from_core = move(from_core.astype(bf16), swap)
         pairs = []
         for k, (leave, keep) in enumerate(cuts):
             left[k].remove(turn_bits[k])
             route = [(flat(c, r), flat(c ^ (1 << turn_bits[k]), r)) for c, r in every]
             pairs.append((keep, move(leave, route)))
+        if turn == 0:
+            sent_y, pairs = lax.optimization_barrier((sent_y, pairs))
+            got_y = exchange(sent_y.reshape(near, 2 * cap, width)).reshape(slots, width)
         if turn == 1:
+            got_y, pairs = lax.optimization_barrier((got_y, pairs))
+            rows_far = mm(send_far, got_y)
+            rows_near = mm(send, got_y)
+            from_core = jnp.concatenate([their_part(rows_far), their_part(rows_near)], axis=0)
+            from_core = move(from_core.astype(bf16), swap)
             pairs, from_core = lax.optimization_barrier((pairs, from_core))
             from_core = from_core.astype(f32)
             crossing = move((my_part(rows_far) + from_core[:part_rows]).astype(bf16), mirror)

time: 201 us -> 195 us (0.970)
  waiting for transfers between devices: 80.5 us -> 75 us
    ppermute x23, waiting for transfers between devices: 59.7 us -> 54.2 us  [move(): return lax.ppermute(rows, both, route)]
    unnamed x56 -> x50, local copies, waits for them, and re-layouts: 6.76 us -> 8.77 us
  transfers between devices with their start and end apart: 27 -> 27, of which waited for: 15 -> 17; matrix products, arithmetic and copies ran while one was open for 15% -> 15% of each run, Pallas kernels for 5% -> 6%
where the time goes in v3:
time: 195 us; the launch traced here: 194 us
  waiting for transfers between devices  75 us (38%)
  starting transfers between devices  42.5 us (22%)
  matrix products  30 us (15%)
  Pallas kernels  25.6 us (13%)
  local copies, waits for them, and re-layouts  14.4 us (7%)
  other arithmetic  5.38 us (3%)
    ppermute x23, waiting for transfers between devices, move(): return lax.ppermute(rows, both, route)  54.2 us
    dot_general x19, matrix products, mm(): return lax.dot_general(a, b, dims, preferred_element_type=f32)  30 us
    ppermute x23, starting transfers between devices, move(): return lax.ppermute(rows, both, route)  25.1 us
    all_to_all x4, waiting for transfers between devices, exchange(): lax.all_to_all(blocks, 'ctx', 0, 0, axis_index_groups=halves, tiled=True)  20.8 us
    all_to_all x4, starting transfers between devices, exchange(): lax.all_to_all(blocks, 'ctx', 0, 0, axis_index_groups=halves, tiled=True)  17.4 us
    pallas_call x1, Pallas kernels, backward(): pl.pallas_call(functools.partial(backward_kernel, scale), grid=(width //...  11.1 us
    unnamed x50, local copies, waits for them, and re-layouts  8.77 us
    pallas_call x1, Pallas kernels, forward(): pl.pallas_call(functools.partial(forward_kernel, scale), grid=(width // B...  7.66 us
  transfers between devices with their start and end apart: 27, of which 17 were waited for; matrix products, arithmetic and copies ran while one was open for 15% of the time, Pallas kernels for 6%

profile of v3, /device:TPU:0, one launch (start us, length us, event | category | flops | bytes accessed | tf_op | source)
XLA Modules:
  0.0 193.9 jit_solution(18321130696971045327)
XLA Ops:
  0.7 1.1 constant_dynamic-slice_fusion.1
  2.6 4.1 %collective-permute-start.1 = (bf16[144,1024]{1,0:T(8,128)(2,1)S(1)}, bf16[144,1024]{1,0:T(8,128)(2,1)}, u32[]{:S(2)}, u32[]{:S(2)}) collective-permute-start(bf16[144,1024]{1,0:T(8,128)(2,1)S(1)} %pad_maximum_fusion.5), channel_id=1, source_target_pairs={{0,16},{1,17},{2,18},{3,19},{4,20},{5,21},{6,22},{7,23},{8,24},{9,... | collective-permute-start | bytes 884744 | tf_op jit(solution)/shard_map/ppermute | solution.py:357
  6.7 1.3 collective-permute-start
  8.7 1.0 constant_dynamic-slice_fusion
  9.6 10.5 %collective-permute-done.1 = bf16[144,1024]{1,0:T(8,128)(2,1)} collective-permute-done((bf16[144,1024]{1,0:T(8,128)(2,1)S(1)}, bf16[144,1024]{1,0:T(8,128)(2,1)}, u32[]{:S(2)}, u32[]{:S(2)}) %collective-permute-start.1) | collective-permute-done | bytes 294944 | tf_op jit(solution)/shard_map/ppermute | solution.py:357
  20.8 1.0 slice.54
  22.9 0.9 collective-permute-done.2
  23.9 1.5 add_convert_fusion.1
  25.4 3.8 %all-to-all-start = ((bf16[8,64,1024]{2,1,0:T(8,128)(2,1)}), bf16[8,64,1024]{2,1,0:T(8,128)(2,1)S(1)}, u32[]{:S(2)}, u32[]{:S(2)}) async-start(bf16[8,64,1024]{2,1,0:T(8,128)(2,1)} %bitcast.53), calls=%async_computation | async-start | bytes 2097152 | tf_op jit(solution)/shard_map/all_to_all | solution.py:360
  29.4 3.6 %collective-permute-start.4 = (bf16[128,1024]{1,0:T(8,128)(2,1)S(1)}, bf16[128,1024]{1,0:T(8,128)(2,1)}, u32[]{:S(2)}, u32[]{:S(2)}) collective-permute-start(bf16[128,1024]{1,0:T(8,128)(2,1)S(1)} %constant_dynamic-slice_fusion), channel_id=1, source_target_pairs={{0,16},{1,17},{2,18},{3,19},{4,20},{5,21},{6,22},{7,23},{8,24},{9,... | collective-permute-start | bytes 786440 | tf_op jit(solution)/shard_map/ppermute | solution.py:357
  33.0 2.9 %fusion.20 = f32[512,1024]{1,0:T(8,128)} fusion(bf16[256,1024]{1,0:T(8,128)(2,1)} %param.11, s32[256]{0:T(256)S(1)} %get-tuple-element.160), kind=kOutput, calls=%fused_computation.49 | convolution fusion | flops 268566528 | bytes 2622464 | tf_op jit(solution)/shard_map/dot_general | solution.py:54
  35.9 12.9 %all-to-all-done = bf16[8,64,1024]{2,1,0:T(8,128)(2,1)S(1)} async-done(((bf16[8,64,1024]{2,1,0:T(8,128)(2,1)}), bf16[8,64,1024]{2,1,0:T(8,128)(2,1)S(1)}, u32[]{:S(2)}, u32[]{:S(2)}) %all-to-all-start) | async-done | bytes 1048608 | tf_op jit(solution)/shard_map/all_to_all | solution.py:360
  49.5 3.2 %convolution_convert_fusion.5.v_own = bf16[256,1024]{1,0:T(8,128)(2,1)} fusion(bf16[256,1024]{1,0:T(8,128)(2,1)S(1)} %convolution_convert_fusion.2, bf16[1024,1024]{1,0:T(8,128)(2,1)} %param.13), kind=kOutput, calls=%fused_computation.15 | convolution fusion | flops 537133056 | bytes 3145728 | tf_op jit(solution)/shard_map/dot_general | solution.py:54
  52.7 1.5 convolution_convert_fusion.6.k_own
  54.3 2.5 %add_convert_fusion = bf16[512,1024]{1,0:T(8,128)(2,1)} fusion(f32[512,1024]{1,0:T(8,128)S(1)} %copy-done.13, bf16[128,1024]{1,0:T(8,128)(2,1)S(1)} %collective-permute-done.5, bf16[128,1024]{1,0:T(8,128)(2,1)} %collective-permute-done.4, s32[256]{0:T(256)S(1)} %add_select_fusion.1), kind=kOutput, calls=%fused_computation.2 | convolution fusion | flops 270663680 | bytes 3671040 | tf_op jit(solution)/shard_map/dot_general | solution.py:54
  56.8 1.7 collective-permute-done.3
  58.5 0.8 copy-done.21
  59.3 4.6 %all-to-all-start.1 = ((bf16[8,64,1024]{2,1,0:T(8,128)(2,1)}), bf16[8,64,1024]{2,1,0:T(8,128)(2,1)S(1)}, u32[]{:S(2)}, u32[]{:S(2)}) async-start(bf16[8,64,1024]{2,1,0:T(8,128)(2,1)} %bitcast.54), calls=%async_computation.1 | async-start | bytes 2097152 | tf_op jit(solution)/shard_map/all_to_all | solution.py:360
  64.0 0.8 fusion.22.pick
  65.3 3.3 %convolution_convert_fusion.3.v_prev = bf16[256,1024]{1,0:T(8,128)(2,1)} fusion(bf16[256,1024]{1,0:T(8,128)(2,1)} %copy-done.21, bf16[1024,1024]{1,0:T(8,128)(2,1)} %param.13), kind=kOutput, calls=%fused_computation.13 | convolution fusion | flops 537133056 | bytes 3145728 | tf_op jit(solution)/shard_map/dot_general | solution.py:54
  68.6 1.6 convolution_convert_fusion.4.k_prev
  70.2 7.7 %forward.1 = (f32[16,256]{1,0:T(8,128)}, f32[16,256]{1,0:T(8,128)}, f32[1024,256]{1,0:T(8,128)}, bf16[16,512,256]{2,1,0:T(8,128)(2,1)}) custom-call(bf16[256,1024]{1,0:T(8,128)(2,1)} %convolution_convert_fusion.6.k_own, bf16[256,1024]{1,0:T(8,128)(2,1)} %convolution_convert_fusion.5.v_own, bf16[256,1024]{1,0:T(8,128)(2,1)} %convolution_convert_fusion.4.k_prev, ...), custom_call_target="tpu_custom_call" | custom-call | tf_op jit(solution)/shard_map/forward/pallas_call | solution.py:121
  77.8 1.4 all-to-all-done.1
  79.2 1.0 copy-done.14
  80.2 3.1 %cotangent.1 = (bf16[256,1024]{1,0:T(8,128)(2,1)}, bf16[1024,256]{1,0:T(8,128)(2,1)}, f32[40,256]{1,0:T(8,128)}) custom-call(bf16[512,1024]{1,0:T(8,128)(2,1)} %bitcast.51, bf16[256,512]{1,0:T(8,128)(2,1)} %fusion.22.pick, f32[1024,256]{1,0:T(8,128)} %get-tuple-element.84.out_t, f32[16,256]{1,0:T(8,128)} %get-tuple-element.85.lse, f32[1,256]{1,0:T(1,128)} %bitcast.58), custom_call_target="tpu_custom_call" | custom-call | tf_op jit(solution)/shard_map/cotangent/pallas_call | solution.py:157
  83.3 1.5 collective-permute-start.7
  84.8 3.0 %collective-permute-done.7 = f32[40,256]{1,0:T(8,128)S(1)} collective-permute-done((f32[40,256]{1,0:T(8,128)}, f32[40,256]{1,0:T(8,128)S(1)}, u32[]{:S(2)}, u32[]{:S(2)}) %collective-permute-start.7) | collective-permute-done | bytes 40992 | tf_op jit(solution)/shard_map/ppermute | solution.py:357
  87.9 0.9 broadcast_in_dim.41
  88.8 4.7 %all-to-all-start.2 = ((f32[8,2,40,256]{3,2,1,0:T(8,128)}), f32[8,2,40,256]{3,2,1,0:T(8,128)S(1)}, u32[]{:S(2)}, u32[]{:S(2)}) async-start(f32[8,2,40,256]{3,2,1,0:T(8,128)} %broadcast_in_dim.41), calls=%async_computation.2 | async-start | bytes 1310720 | tf_op jit(solution)/shard_map/all_to_all | solution.py:360
  93.5 0.8 copy.14.wanted
  94.3 2.7 %fusion.2 = bf16[512,512]{1,0:T(8,128)(2,1)} fusion(s32[512]{0:T(512)S(1)} %get-tuple-element.157, bf16[256,1024]{1,0:T(8,128)(2,1)S(1)} %copy-done.18, bf16[256,1024]{1,0:T(8,128)(2,1)} %copy-done.21), kind=kOutput, calls=%fused_computation.10 | convolution fusion | flops 539754496 | bytes 1574912 | tf_op jit(solution)/shard_map/dot_general | solution.py:54
  97.8 6.5 %all-to-all-done.2 = f32[8,2,40,256]{3,2,1,0:T(8,128)S(1)} async-done(((f32[8,2,40,256]{3,2,1,0:T(8,128)}), f32[8,2,40,256]{3,2,1,0:T(8,128)S(1)}, u32[]{:S(2)}, u32[]{:S(2)}) %all-to-all-start.2) | async-done | bytes 655392 | tf_op jit(solution)/shard_map/all_to_all | solution.py:360
  104.3 0.8 copy-done.15
  105.2 11.1 %backward.1.grads = bf16[2,512,1024]{2,1,0:T(8,128)(2,1)} custom-call(f32[16,40,256]{2,1,0:T(8,128)} %bitcast.55, f32[256,1]{1,0:T(8,128)} %copy.14.wanted, f32[40,256]{1,0:T(8,128)} %get-tuple-element.87.mine, f32[16,256]{1,0:T(8,128)} %get-tuple-element.89.inverse, bf16[16,512,256]{2,1,0:T(8,128)(2,1)} %get-tuple-element.90.probs, ...), custom_call_target="tpu_custom_call" | custom-call | tf_op jit(solution)/shard_map/backward/pallas_call | solution.py:241
  116.3 1.9 fusion.11
  121.9 1.5 collective-permute-done.10.other_v
  123.4 1.5 collective-permute-done.9.other_k
  124.9 1.3 fold.3
  126.2 4.2 %collective-permute-done.8.y_next = bf16[256,1024]{1,0:T(8,128)(2,1)S(1)} collective-permute-done((bf16[256,1024]{1,0:T(8,128)(2,1)S(1)}, bf16[256,1024]{1,0:T(8,128)(2,1)S(1)}, u32[]{:S(2)}, u32[]{:S(2)}) %collective-permute-start.8) | collective-permute-done | bytes 524320 | tf_op jit(solution)/shard_map/ppermute | solution.py:357
  131.0 1.5 collective-permute-start.12
  133.3 0.9 collective-permute-start.13
  134.9 1.5 place_rows.1
  136.4 3.8 %collective-permute-done.13.refs_5_ = bf16[256,512]{1,0:T(8,128)(2,1)S(1)} collective-permute-done((bf16[256,512]{1,0:T(8,128)(2,1)S(1)}, bf16[256,512]{1,0:T(8,128)(2,1)S(1)}, u32[]{:S(2)}, u32[]{:S(2)}) %collective-permute-start.13) | collective-permute-done | bytes 262176 | tf_op jit(solution)/shard_map/ppermute | solution.py:357
  141.0 0.8 copy-done.2
  141.8 4.2 %all-to-all-start.3 = ((bf16[8,64,1024]{2,1,0:T(8,128)(2,1)}), bf16[8,64,1024]{2,1,0:T(8,128)(2,1)}, u32[]{:S(2)}, u32[]{:S(2)}) async-start(bf16[8,64,1024]{2,1,0:T(8,128)(2,1)} %bitcast.18), calls=%async_computation.3 | async-start | bytes 2097152 | tf_op jit(solution)/shard_map/all_to_all | solution.py:360
  146.0 1.0 copy-done.3
  147.0 0.9 copy-done.5
  148.0 0.9 copy-done.7
  148.9 0.9 fold.4
  151.2 1.9 collective-permute-start.14
  153.1 1.5 collective-permute-start.15
  154.6 1.5 collective-permute-start.16
  156.0 4.7 %collective-permute-done.16.refs_5_ = bf16[128,512]{1,0:T(8,128)(2,1)S(1)} collective-permute-done((bf16[128,512]{1,0:T(8,128)(2,1)S(1)}, bf16[128,512]{1,0:T(8,128)(2,1)S(1)}, u32[]{:S(2)}, u32[]{:S(2)}) %collective-permute-start.16) | collective-permute-done | bytes 131104 | tf_op jit(solution)/shard_map/ppermute | solution.py:357
  160.7 2.4 %collective-permute-done.14.refs_1_ = bf16[128,768]{1,0:T(8,128)(2,1)S(1)} collective-permute-done((bf16[128,768]{1,0:T(8,128)(2,1)}, bf16[128,768]{1,0:T(8,128)(2,1)S(1)}, u32[]{:S(2)}, u32[]{:S(2)}) %collective-permute-start.14) | collective-permute-done | bytes 196640 | tf_op jit(solution)/shard_map/ppermute | solution.py:357
  163.1 1.7 fusion.24
  164.8 1.7 fusion.19
  166.8 1.9 collective-permute-done.17
  168.9 2.3 %collective-permute-start.21 = (bf16[128,1024]{1,0:T(8,128)(2,1)S(1)}, bf16[128,1024]{1,0:T(8,128)(2,1)S(1)}, u32[]{:S(2)}, u32[]{:S(2)}) collective-permute-start(bf16[128,1024]{1,0:T(8,128)(2,1)S(1)} %fusion.8), channel_id=1, source_target_pairs={{0,16},{1,17},{2,18},{3,19},{4,20},{5,21},{6,22},{7,23},{8,24},{9,... | collective-permute-start | bytes 786440 | tf_op jit(solution)/shard_map/ppermute | solution.py:357
  171.3 0.9 collective-permute-start.18
  172.2 1.1 collective-permute-start.19
  173.3 1.0 collective-permute-start.20
  174.3 9.5 %collective-permute-done.21 = bf16[128,1024]{1,0:T(8,128)(2,1)S(1)} collective-permute-done((bf16[128,1024]{1,0:T(8,128)(2,1)S(1)}, bf16[128,1024]{1,0:T(8,128)(2,1)S(1)}, u32[]{:S(2)}, u32[]{:S(2)}) %collective-permute-start.21) | collective-permute-done | bytes 262176 | tf_op jit(solution)/shard_map/ppermute | solution.py:357
  183.8 0.8 fusion.10
  184.9 8.3 %collective-permute-done.22 = bf16[32,2048]{1,0:T(8,128)(2,1)S(1)} collective-permute-done((bf16[32,2048]{1,0:T(8,128)(2,1)S(1)}, bf16[32,2048]{1,0:T(8,128)(2,1)S(1)}, u32[]{:S(2)}, u32[]{:S(2)}) %collective-permute-start.22) | collective-permute-done | bytes 131104 | tf_op jit(solution)/shard_map/ppermute | solution.py:357
  (105 shorter events, 14.9 us)
Async XLA Ops:
  0.6 52.1 %copy-start = (bf16[1024,1024]{1,0:T(8,128)(2,1)S(1)}, bf16[1024,1024]{1,0:T(8,128)(2,1)}, u32[]{:S(2)}) copy-start(bf16[1024,1024]{1,0:T(8,128)(2,1)} %param.12) | copy-start | bytes 6291460
  0.6 21.7 %copy-start.16 = (bf16[256,1024]{1,0:T(8,128)(2,1)S(1)}, bf16[256,1024]{1,0:T(8,128)(2,1)}, u32[]{:S(2)}) copy-start(bf16[256,1024]{1,0:T(8,128)(2,1)} %param.10) | copy-start | bytes 1572868
  2.6 17.5 %collective-permute-start.1 = (bf16[144,1024]{1,0:T(8,128)(2,1)S(1)}, bf16[144,1024]{1,0:T(8,128)(2,1)}, u32[]{:S(2)}, u32[]{:S(2)}) collective-permute-start(bf16[144,1024]{1,0:T(8,128)(2,1)S(1)} %pad_maximum_fusion.5), channel_id=1, source_target_pairs={{0,16},{1,17},{2,18},{3,19},{4,20},{5,21},{6,22},{7,23},{8,24},{9,... | collective-permute-start | bytes 884744 | tf_op jit(solution)/shard_map/ppermute | solution.py:357
  6.7 18.7 %collective-permute-start = (s32[256]{0:T(256)}, s32[256]{0:T(256)S(1)}, u32[]{:S(2)}, u32[]{:S(2)}) collective-permute-start(s32[256]{0:T(256)} %bitcast.62), channel_id=1, source_target_pairs={{0,0},{1,1},{14,2},{19,3},{30,4},{3,5},{16,6},{17,7},{2,8},{31,9},... | collective-permute-start | bytes 3080 | tf_op jit(solution)/shard_map/ppermute | solution.py:357
  22.3 1.6 collective-permute-start.2
  25.4 23.4 %all-to-all-start = ((bf16[8,64,1024]{2,1,0:T(8,128)(2,1)}), bf16[8,64,1024]{2,1,0:T(8,128)(2,1)S(1)}, u32[]{:S(2)}, u32[]{:S(2)}) async-start(bf16[8,64,1024]{2,1,0:T(8,128)(2,1)} %bitcast.53), calls=%async_computation | async-start | bytes 2097152 | tf_op jit(solution)/shard_map/all_to_all | solution.py:360
  29.4 19.9 %collective-permute-start.4 = (bf16[128,1024]{1,0:T(8,128)(2,1)S(1)}, bf16[128,1024]{1,0:T(8,128)(2,1)}, u32[]{:S(2)}, u32[]{:S(2)}) collective-permute-start(bf16[128,1024]{1,0:T(8,128)(2,1)S(1)} %constant_dynamic-slice_fusion), channel_id=1, source_target_pairs={{0,16},{1,17},{2,18},{3,19},{4,20},{5,21},{6,22},{7,23},{8,24},{9,... | collective-permute-start | bytes 786440 | tf_op jit(solution)/shard_map/ppermute | solution.py:357
  49.3 5.0 %copy-start.17 = (bf16[256,1024]{1,0:T(8,128)(2,1)}, bf16[256,1024]{1,0:T(8,128)(2,1)S(1)}, u32[]{:S(2)}) copy-start(bf16[256,1024]{1,0:T(8,128)(2,1)S(1)} %convolution_convert_fusion.2) | copy-start | bytes 1572868
  49.3 9.2 %collective-permute-start.3 = (bf16[256,1024]{1,0:T(8,128)(2,1)S(1)}, bf16[256,1024]{1,0:T(8,128)(2,1)S(1)}, u32[]{:S(2)}, u32[]{:S(2)}) collective-permute-start(bf16[256,1024]{1,0:T(8,128)(2,1)S(1)} %convolution_convert_fusion.2), channel_id=1, source_target_pairs={{0,8},{1,5},{8,16},{5,13},{16,24},{13,21},{24,26},{21,29},{26,18},... | collective-permute-start | bytes 1572872 | tf_op jit(solution)/shard_map/ppermute | solution.py:357
  49.4 4.9 %collective-permute-start.5 = (bf16[128,1024]{1,0:T(8,128)(2,1)}, bf16[128,1024]{1,0:T(8,128)(2,1)S(1)}, u32[]{:S(2)}, u32[]{:S(2)}) collective-permute-start(bf16[128,1024]{1,0:T(8,128)(2,1)} %collective-permute-done.4), channel_id=1, source_target_pairs={{0,1},{1,0},{2,3},{3,2},{4,5},{5,4},{6,7},{7,6},{8,9},{9,8},{10,11... | collective-permute-start | bytes 786440 | tf_op jit(solution)/shard_map/ppermute | solution.py:357
  52.7 1.6 copy-start.13
  58.5 0.8 copy-start.21
  59.3 19.9 %all-to-all-start.1 = ((bf16[8,64,1024]{2,1,0:T(8,128)(2,1)}), bf16[8,64,1024]{2,1,0:T(8,128)(2,1)S(1)}, u32[]{:S(2)}, u32[]{:S(2)}) async-start(bf16[8,64,1024]{2,1,0:T(8,128)(2,1)} %bitcast.54), calls=%async_computation.1 | async-start | bytes 2097152 | tf_op jit(solution)/shard_map/all_to_all | solution.py:360
  64.0 4.6 %copy-start.22 = (bf16[256,1024]{1,0:T(8,128)(2,1)S(1)}, bf16[256,1024]{1,0:T(8,128)(2,1)}, u32[]{:S(2)}) copy-start(bf16[256,1024]{1,0:T(8,128)(2,1)} %copy-done.21) | copy-start | bytes 1572868
  79.2 1.0 copy-start.14
  80.2 13.3 %copy-start.20 = (f32[256]{0:T(256)S(1)}, f32[256]{0:T(256)}, u32[]{:S(2)}) copy-start(f32[256]{0:T(256)} %convert_element_type.125) | copy-start | bytes 3076
  83.3 11.1 %copy-start.18 = (bf16[256,1024]{1,0:T(8,128)(2,1)S(1)}, bf16[256,1024]{1,0:T(8,128)(2,1)}, u32[]{:S(2)}) copy-start(bf16[256,1024]{1,0:T(8,128)(2,1)} %copy-done.17) | copy-start | bytes 1572868
  83.3 1.5 collective-permute-start.6
  83.3 4.5 %collective-permute-start.7 = (f32[40,256]{1,0:T(8,128)}, f32[40,256]{1,0:T(8,128)S(1)}, u32[]{:S(2)}, u32[]{:S(2)}) collective-permute-start(f32[40,256]{1,0:T(8,128)} %get-tuple-element.87.mine), channel_id=1, source_target_pairs={{0,17},{1,16},{2,19},{3,18},{4,21},{5,20},{6,23},{7,22},{8,25},{9,... | collective-permute-start | bytes 122888 | tf_op jit(solution)/shard_map/ppermute | solution.py:357
  88.8 15.6 %all-to-all-start.2 = ((f32[8,2,40,256]{3,2,1,0:T(8,128)}), f32[8,2,40,256]{3,2,1,0:T(8,128)S(1)}, u32[]{:S(2)}, u32[]{:S(2)}) async-start(f32[8,2,40,256]{3,2,1,0:T(8,128)} %broadcast_in_dim.41), calls=%async_computation.2 | async-start | bytes 1310720 | tf_op jit(solution)/shard_map/all_to_all | solution.py:360
  94.3 2.7 %copy-start.19 = (bf16[256,1024]{1,0:T(8,128)(2,1)S(1)}, bf16[256,1024]{1,0:T(8,128)(2,1)}, u32[]{:S(2)}) copy-start(bf16[256,1024]{1,0:T(8,128)(2,1)} %copy-done.17) | copy-start | bytes 1572868
  94.3 2.7 %copy-start.23 = (bf16[256,1024]{1,0:T(8,128)(2,1)S(1)}, bf16[256,1024]{1,0:T(8,128)(2,1)}, u32[]{:S(2)}) copy-start(bf16[256,1024]{1,0:T(8,128)(2,1)} %copy-done.21) | copy-start | bytes 1572868
  104.3 0.8 copy-start.15
  105.2 13.0 %copy-start.12 = (bf16[1024,1024]{1,0:T(8,128)(2,1)S(1)}, bf16[1024,1024]{1,0:T(8,128)(2,1)}, u32[]{:S(2)}) copy-start(bf16[1024,1024]{1,0:T(8,128)(2,1)} %param.13) | copy-start | bytes 6291460
  116.3 2.0 %copy-start.1 = (bf16[2,512,1024]{2,1,0:T(8,128)(2,1)S(1)}, bf16[2,512,1024]{2,1,0:T(8,128)(2,1)}, u32[]{:S(2)}) copy-start(bf16[2,512,1024]{2,1,0:T(8,128)(2,1)} %backward.1.grads) | copy-start | bytes 6291460
  118.2 1.0 copy-start.24
  120.7 2.7 %collective-permute-start.10 = (bf16[512,1024]{1,0:T(8,128)(2,1)S(1)}, bf16[512,1024]{1,0:T(8,128)(2,1)S(1)}, u32[]{:S(2)}, u32[]{:S(2)}) collective-permute-start(bf16[512,1024]{1,0:T(8,128)(2,1)S(1)} %convolution_convert_fusion), channel_id=1, source_target_pairs={{0,1},{1,0},{2,3},{3,2},{4,5},{5,4},{6,7},{7,6},{8,9},{9,8},{10,11... | collective-permute-start | bytes 3145736 | tf_op jit(solution)/shard_map/ppermute | solution.py:357
  120.8 4.1 %collective-permute-start.9 = (bf16[512,1024]{1,0:T(8,128)(2,1)S(1)}, bf16[512,1024]{1,0:T(8,128)(2,1)S(1)}, u32[]{:S(2)}, u32[]{:S(2)}) collective-permute-start(bf16[512,1024]{1,0:T(8,128)(2,1)S(1)} %convolution_convert_fusion.1), channel_id=1, source_target_pairs={{0,1},{1,0},{2,3},{3,2},{4,5},{5,4},{6,7},{7,6},{8,9},{9,8},{10,11... | collective-permute-start | bytes 3145736 | tf_op jit(solution)/shard_map/ppermute | solution.py:357
  121.3 9.2 %collective-permute-start.8 = (bf16[256,1024]{1,0:T(8,128)(2,1)S(1)}, bf16[256,1024]{1,0:T(8,128)(2,1)S(1)}, u32[]{:S(2)}, u32[]{:S(2)}) collective-permute-start(bf16[256,1024]{1,0:T(8,128)(2,1)S(1)} %fusion.5), channel_id=1, source_target_pairs={{8,0},{5,1},{16,8},{13,5},{24,16},{21,13},{26,24},{29,21},{18,26},... | collective-permute-start | bytes 1572872 | tf_op jit(solution)/shard_map/ppermute | solution.py:357
  126.2 8.7 %copy-start.4 = (bf16[256,512]{1,0:T(8,128)(2,1)}, bf16[256,512]{1,0:T(8,128)(2,1)S(1)}, u32[]{:S(2)}) copy-start(bf16[256,512]{1,0:T(8,128)(2,1)S(1)} %get-tuple-element.114.refs_4_) | copy-start | bytes 786436
  130.5 10.4 %collective-permute-start.11 = (bf16[256,768]{1,0:T(8,128)(2,1)S(1)}, bf16[256,768]{1,0:T(8,128)(2,1)S(1)}, u32[]{:S(2)}, u32[]{:S(2)}) collective-permute-start(bf16[256,768]{1,0:T(8,128)(2,1)S(1)} %get-tuple-element.104), channel_id=1, source_target_pairs={{0,2},{1,3},{2,0},{3,1},{4,6},{5,7},{6,4},{7,5},{8,10},{9,11},{10,... | collective-permute-start | bytes 1179656 | tf_op jit(solution)/shard_map/ppermute | solution.py:357
  131.0 10.0 %collective-permute-start.12 = (bf16[256,768]{1,0:T(8,128)(2,1)S(1)}, bf16[256,768]{1,0:T(8,128)(2,1)S(1)}, u32[]{:S(2)}, u32[]{:S(2)}) collective-permute-start(bf16[256,768]{1,0:T(8,128)(2,1)S(1)} %get-tuple-element.106), channel_id=1, source_target_pairs={{0,4},{1,5},{2,6},{3,7},{4,0},{5,1},{6,2},{7,3},{8,12},{9,13},{10,... | collective-permute-start | bytes 1179656 | tf_op jit(solution)/shard_map/ppermute | solution.py:357
  133.3 6.9 %collective-permute-start.13 = (bf16[256,512]{1,0:T(8,128)(2,1)S(1)}, bf16[256,512]{1,0:T(8,128)(2,1)S(1)}, u32[]{:S(2)}, u32[]{:S(2)}) collective-permute-start(bf16[256,512]{1,0:T(8,128)(2,1)S(1)} %get-tuple-element.108), channel_id=1, source_target_pairs={{0,8},{1,9},{2,10},{3,11},{4,12},{5,13},{6,14},{7,15},{8,0},{9,1},... | collective-permute-start | bytes 786440 | tf_op jit(solution)/shard_map/ppermute | solution.py:357
  140.2 0.7 copy-start.6
  141.0 0.8 copy-start.2
  141.8 21.4 %all-to-all-start.3 = ((bf16[8,64,1024]{2,1,0:T(8,128)(2,1)}), bf16[8,64,1024]{2,1,0:T(8,128)(2,1)}, u32[]{:S(2)}, u32[]{:S(2)}) async-start(bf16[8,64,1024]{2,1,0:T(8,128)(2,1)} %bitcast.18), calls=%async_computation.3 | async-start | bytes 2097152 | tf_op jit(solution)/shard_map/all_to_all | solution.py:360
  146.0 1.0 copy-start.3
  147.0 0.9 copy-start.5
  148.0 0.9 copy-start.7
  149.8 0.7 copy-start.8
  150.5 0.7 copy-start.10
  151.2 11.9 %collective-permute-start.14 = (bf16[128,768]{1,0:T(8,128)(2,1)}, bf16[128,768]{1,0:T(8,128)(2,1)S(1)}, u32[]{:S(2)}, u32[]{:S(2)}) collective-permute-start(bf16[128,768]{1,0:T(8,128)(2,1)} %get-tuple-element.117), channel_id=1, source_target_pairs={{0,4},{1,5},{2,6},{3,7},{4,0},{5,1},{6,2},{7,3},{8,12},{9,13},{10,... | collective-permute-start | bytes 589832 | tf_op jit(solution)/shard_map/ppermute | solution.py:357
  153.1 10.0 %collective-permute-start.15 = (bf16[128,768]{1,0:T(8,128)(2,1)}, bf16[128,768]{1,0:T(8,128)(2,1)S(1)}, u32[]{:S(2)}, u32[]{:S(2)}) collective-permute-start(bf16[128,768]{1,0:T(8,128)(2,1)} %get-tuple-element.119), channel_id=1, source_target_pairs={{0,8},{1,9},{2,10},{3,11},{4,12},{5,13},{6,14},{7,15},{8,0},{9,1},... | collective-permute-start | bytes 589832 | tf_op jit(solution)/shard_map/ppermute | solution.py:357
  154.6 6.2 %collective-permute-start.16 = (bf16[128,512]{1,0:T(8,128)(2,1)S(1)}, bf16[128,512]{1,0:T(8,128)(2,1)S(1)}, u32[]{:S(2)}, u32[]{:S(2)}) collective-permute-start(bf16[128,512]{1,0:T(8,128)(2,1)S(1)} %get-tuple-element.121), channel_id=1, source_target_pairs={{0,2},{1,3},{2,0},{3,1},{4,6},{5,7},{6,4},{7,5},{8,10},{9,11},{10,... | collective-permute-start | bytes 393224 | tf_op jit(solution)/shard_map/ppermute | solution.py:357
  166.6 4.5 %copy-start.9 = (bf16[128,768]{1,0:T(8,128)(2,1)S(1)}, bf16[128,768]{1,0:T(8,128)(2,1)}, u32[]{:S(2)}) copy-start(bf16[128,768]{1,0:T(8,128)(2,1)} %copy-done.8) | copy-start | bytes 589828
  166.7 4.5 %copy-start.11 = (bf16[128,768]{1,0:T(8,128)(2,1)S(1)}, bf16[128,768]{1,0:T(8,128)(2,1)}, u32[]{:S(2)}) copy-start(bf16[128,768]{1,0:T(8,128)(2,1)} %copy-done.10) | copy-start | bytes 589828
  166.7 2.0 %collective-permute-start.17 = (bf16[256,1024]{1,0:T(8,128)(2,1)S(1)}, bf16[256,1024]{1,0:T(8,128)(2,1)S(1)}, u32[]{:S(2)}, u32[]{:S(2)}) collective-permute-start(bf16[256,1024]{1,0:T(8,128)(2,1)S(1)} %pad_maximum_fusion.3), channel_id=1, source_target_pairs={{0,1},{1,0},{2,3},{3,2},{4,5},{5,4},{6,7},{7,6},{8,9},{9,8},{10,11... | collective-permute-start | bytes 1572872 | tf_op jit(solution)/shard_map/ppermute | solution.py:357
  168.9 14.9 %collective-permute-start.21 = (bf16[128,1024]{1,0:T(8,128)(2,1)S(1)}, bf16[128,1024]{1,0:T(8,128)(2,1)S(1)}, u32[]{:S(2)}, u32[]{:S(2)}) collective-permute-start(bf16[128,1024]{1,0:T(8,128)(2,1)S(1)} %fusion.8), channel_id=1, source_target_pairs={{0,16},{1,17},{2,18},{3,19},{4,20},{5,21},{6,22},{7,23},{8,24},{9,... | collective-permute-start | bytes 786440 | tf_op jit(solution)/shard_map/ppermute | solution.py:357
  171.3 13.3 %collective-permute-start.18 = (bf16[64,768]{1,0:T(8,128)(2,1)S(1)}, bf16[64,768]{1,0:T(8,128)(2,1)S(1)}, u32[]{:S(2)}, u32[]{:S(2)}) collective-permute-start(bf16[64,768]{1,0:T(8,128)(2,1)S(1)} %get-tuple-element.136), channel_id=1, source_target_pairs={{0,8},{1,9},{2,10},{3,11},{4,12},{5,13},{6,14},{7,15},{8,0},{9,1},... | collective-permute-start | bytes 294920 | tf_op jit(solution)/shard_map/ppermute | solution.py:357
  172.2 12.5 %collective-permute-start.19 = (bf16[64,768]{1,0:T(8,128)(2,1)S(1)}, bf16[64,768]{1,0:T(8,128)(2,1)S(1)}, u32[]{:S(2)}, u32[]{:S(2)}) collective-permute-start(bf16[64,768]{1,0:T(8,128)(2,1)S(1)} %get-tuple-element.138), channel_id=1, source_target_pairs={{0,2},{1,3},{2,0},{3,1},{4,6},{5,7},{6,4},{7,5},{8,10},{9,11},{10,... | collective-permute-start | bytes 294920 | tf_op jit(solution)/shard_map/ppermute | solution.py:357
  173.3 11.3 %collective-permute-start.20 = (bf16[64,512]{1,0:T(8,128)(2,1)S(1)}, bf16[64,512]{1,0:T(8,128)(2,1)S(1)}, u32[]{:S(2)}, u32[]{:S(2)}) collective-permute-start(bf16[64,512]{1,0:T(8,128)(2,1)S(1)} %get-tuple-element.140), channel_id=1, source_target_pairs={{0,4},{1,5},{2,6},{3,7},{4,0},{5,1},{6,2},{7,3},{8,12},{9,13},{10,... | collective-permute-start | bytes 196616 | tf_op jit(solution)/shard_map/ppermute | solution.py:357
  184.8 8.4 %collective-permute-start.22 = (bf16[32,2048]{1,0:T(8,128)(2,1)S(1)}, bf16[32,2048]{1,0:T(8,128)(2,1)S(1)}, u32[]{:S(2)}, u32[]{:S(2)}) collective-permute-start(bf16[32,2048]{1,0:T(8,128)(2,1)S(1)} %slice.104), channel_id=1, source_target_pairs={{0,16},{1,17},{2,18},{3,19},{4,20},{5,21},{6,22},{7,23},{8,24},{9,... | collective-permute-start | bytes 393224 | tf_op jit(solution)/shard_map/ppermute | solution.py:357

commit v4 on v3

--- a/solution.py
+++ b/solution.py
@@ -388,7 +388,6 @@
     far_index = send_index(far_spans) + cap
     rolled = jnp.where(hround == 0, far_index, jnp.roll(far_index, part_rows, axis=0))
     send = one_hot(near_index, slots)
-    send_far = one_hot(far_index, slots)
     send_far_rolled = one_hot(rolled, slots)
     sources = move(source_pos[0], fetch)
     group = sources // tdev
@@ -440,6 +439,8 @@
     y_prev = (mm(grads[0, :SPAN], w_qk, NT) + mm(grads[1, :SPAN], w_v, NT)).astype(bf16)
     y_next = move(y_prev, backward_way)
 
+    mine_hot = one_hot(jnp.concatenate([my_part(far_index), my_part(near_index)]), slots)
+    theirs_hot = one_hot(jnp.concatenate([their_part(far_index), their_part(near_index)]), slots)
     x_theirs, _ = lax.optimization_barrier((x_theirs, y_prev))
     theirs = [move(mm(x_theirs, grads[k]).astype(bf16), swap) for k in range(2)]
     y_own = (mm(grads[0, SPAN:], w_qk, NT) + mm(grads[1, SPAN:], w_v, NT)).astype(bf16)
@@ -461,7 +462,6 @@
             operands = [array for pair in pairs for array in pair]
         cuts = call_fold(kernel, operands, (width // 2) >> (turn + 1), widths, "fold")
         if turn == 0:
-            y_next, cuts = lax.optimization_barrier((y_next, cuts))
             sent_y = place_rows(jnp.transpose(pick), y_own, y_next)
         pairs = []
         for k, (leave, keep) in enumerate(cuts):
@@ -473,15 +473,12 @@
             got_y = exchange(sent_y.reshape(near, 2 * cap, width)).reshape(slots, width)
         if turn == 1:
             got_y, pairs = lax.optimization_barrier((got_y, pairs))
-            rows_far = mm(send_far, got_y)
-            rows_near = mm(send, got_y)
-            from_core = jnp.concatenate([their_part(rows_far), their_part(rows_near)], axis=0)
-            from_core = move(from_core.astype(bf16), swap)
+            from_core = move(mm(theirs_hot, got_y).astype(bf16), swap)
+            my_rows = mm(mine_hot, got_y)
             pairs, from_core = lax.optimization_barrier((pairs, from_core))
-            from_core = from_core.astype(f32)
-            crossing = move((my_part(rows_far) + from_core[:part_rows]).astype(bf16), mirror)
-            grad_x = my_part(rows_near) + from_core[part_rows:] + crossing.astype(f32)
-            grad_x = grad_x.astype(bf16)
+            my_rows = my_rows + from_core.astype(f32)
+            crossing = move(my_rows[:part_rows].astype(bf16), mirror)
+            grad_x = (my_rows[part_rows:] + crossing.astype(f32)).astype(bf16)
 
     pairs, grad_x = lax.optimization_barrier((pairs, grad_x))
     summed = jnp.concatenate([a.astype(f32) + b.astype(f32) for a, b in pairs], axis=1)

time: 195 us -> 193 us (0.990)
    unnamed x50 -> x52, local copies, waits for them, and re-layouts: 8.77 us -> 8.77 us
  transfers between devices with their start and end apart: 27 -> 27, of which waited for: 17 -> 16; matrix products, arithmetic and copies ran while one was open for 15% -> 16% of each run, Pallas kernels for 6% -> 6%
where the time goes in v4:
time: 193 us; the launch traced here: 192 us
  waiting for transfers between devices  73.3 us (38%)
  starting transfers between devices  42.1 us (22%)
  matrix products  30.1 us (16%)
  Pallas kernels  24.9 us (13%)
  local copies, waits for them, and re-layouts  14.5 us (8%)
  other arithmetic  5.76 us (3%)
    ppermute x23, waiting for transfers between devices, move(): return lax.ppermute(rows, both, route)  53 us
    dot_general x19, matrix products, mm(): return lax.dot_general(a, b, dims, preferred_element_type=f32)  30.1 us
    ppermute x23, starting transfers between devices, move(): return lax.ppermute(rows, both, route)  24.7 us
    all_to_all x4, waiting for transfers between devices, exchange(): lax.all_to_all(blocks, 'ctx', 0, 0, axis_index_groups=halves, tiled=True)  20.2 us
    all_to_all x4, starting transfers between devices, exchange(): lax.all_to_all(blocks, 'ctx', 0, 0, axis_index_groups=halves, tiled=True)  17.4 us
    pallas_call x1, Pallas kernels, backward(): pl.pallas_call(functools.partial(backward_kernel, scale), grid=(width //...  11.1 us
    unnamed x52, local copies, waits for them, and re-layouts  8.77 us
    pallas_call x1, Pallas kernels, forward(): pl.pallas_call(functools.partial(forward_kernel, scale), grid=(width // B...  7.64 us
  transfers between devices with their start and end apart: 27, of which 16 were waited for; matrix products, arithmetic and copies ran while one was open for 16% of the time, Pallas kernels for 6%

profile of v4, /device:TPU:0, one launch (start us, length us, event | category | flops | bytes accessed | tf_op | source)
XLA Modules:
  0.0 191.6 jit_solution(13149347825122677127)
XLA Ops:
  0.7 1.1 constant_dynamic-slice_fusion.1
  2.6 4.1 %collective-permute-start.1 = (bf16[144,1024]{1,0:T(8,128)(2,1)S(1)}, bf16[144,1024]{1,0:T(8,128)(2,1)}, u32[]{:S(2)}, u32[]{:S(2)}) collective-permute-start(bf16[144,1024]{1,0:T(8,128)(2,1)S(1)} %pad_maximum_fusion.4), channel_id=1, source_target_pairs={{0,16},{1,17},{2,18},{3,19},{4,20},{5,21},{6,22},{7,23},{8,24},{9,... | collective-permute-start | bytes 884744 | tf_op jit(solution)/shard_map/ppermute | solution.py:357
  6.7 1.3 collective-permute-start
  8.7 1.0 constant_dynamic-slice_fusion
  9.6 10.5 %collective-permute-done.1 = bf16[144,1024]{1,0:T(8,128)(2,1)} collective-permute-done((bf16[144,1024]{1,0:T(8,128)(2,1)S(1)}, bf16[144,1024]{1,0:T(8,128)(2,1)}, u32[]{:S(2)}, u32[]{:S(2)}) %collective-permute-start.1) | collective-permute-done | bytes 294944 | tf_op jit(solution)/shard_map/ppermute | solution.py:357
  20.8 1.0 slice.55
  23.0 0.8 collective-permute-done.2
  23.8 1.5 add_convert_fusion.1
  25.3 3.8 %all-to-all-start = ((bf16[8,64,1024]{2,1,0:T(8,128)(2,1)}), bf16[8,64,1024]{2,1,0:T(8,128)(2,1)S(1)}, u32[]{:S(2)}, u32[]{:S(2)}) async-start(bf16[8,64,1024]{2,1,0:T(8,128)(2,1)} %bitcast.53), calls=%async_computation | async-start | bytes 2097152 | tf_op jit(solution)/shard_map/all_to_all | solution.py:360
  29.4 3.6 %collective-permute-start.4 = (bf16[128,1024]{1,0:T(8,128)(2,1)S(1)}, bf16[128,1024]{1,0:T(8,128)(2,1)}, u32[]{:S(2)}, u32[]{:S(2)}) collective-permute-start(bf16[128,1024]{1,0:T(8,128)(2,1)S(1)} %constant_dynamic-slice_fusion), channel_id=1, source_target_pairs={{0,16},{1,17},{2,18},{3,19},{4,20},{5,21},{6,22},{7,23},{8,24},{9,... | collective-permute-start | bytes 786440 | tf_op jit(solution)/shard_map/ppermute | solution.py:357
  32.9 2.9 %fusion.17 = f32[512,1024]{1,0:T(8,128)} fusion(bf16[256,1024]{1,0:T(8,128)(2,1)} %param.11, s32[256]{0:T(256)S(1)} %get-tuple-element.148), kind=kOutput, calls=%fused_computation.46 | convolution fusion | flops 268566528 | bytes 2622464 | tf_op jit(solution)/shard_map/dot_general | solution.py:54
  35.9 12.9 %all-to-all-done = bf16[8,64,1024]{2,1,0:T(8,128)(2,1)S(1)} async-done(((bf16[8,64,1024]{2,1,0:T(8,128)(2,1)}), bf16[8,64,1024]{2,1,0:T(8,128)(2,1)S(1)}, u32[]{:S(2)}, u32[]{:S(2)}) %all-to-all-start) | async-done | bytes 1048608 | tf_op jit(solution)/shard_map/all_to_all | solution.py:360
  49.5 3.2 %convolution_convert_fusion.6.v_own = bf16[256,1024]{1,0:T(8,128)(2,1)} fusion(bf16[256,1024]{1,0:T(8,128)(2,1)S(1)} %convolution_convert_fusion.3, bf16[1024,1024]{1,0:T(8,128)(2,1)} %param.13), kind=kOutput, calls=%fused_computation.17 | convolution fusion | flops 537133056 | bytes 3145728 | tf_op jit(solution)/shard_map/dot_general | solution.py:54
  52.7 1.5 convolution_convert_fusion.7.k_own
  54.2 2.5 %add_convert_fusion = bf16[512,1024]{1,0:T(8,128)(2,1)} fusion(f32[512,1024]{1,0:T(8,128)S(1)} %copy-done.13, bf16[128,1024]{1,0:T(8,128)(2,1)S(1)} %collective-permute-done.5, bf16[128,1024]{1,0:T(8,128)(2,1)} %collective-permute-done.4, s32[256]{0:T(256)S(1)} %add_select_fusion.1), kind=kOutput, calls=%fused_computation.2 | convolution fusion | flops 270663680 | bytes 3671040 | tf_op jit(solution)/shard_map/dot_general | solution.py:54
  56.8 1.7 collective-permute-done.3
  58.5 0.8 copy-done.22
  59.3 4.6 %all-to-all-start.1 = ((bf16[8,64,1024]{2,1,0:T(8,128)(2,1)}), bf16[8,64,1024]{2,1,0:T(8,128)(2,1)S(1)}, u32[]{:S(2)}, u32[]{:S(2)}) async-start(bf16[8,64,1024]{2,1,0:T(8,128)(2,1)} %bitcast.54), calls=%async_computation.1 | async-start | bytes 2097152 | tf_op jit(solution)/shard_map/all_to_all | solution.py:360
  63.9 0.8 fusion.19.pick
  65.3 3.3 %convolution_convert_fusion.4.v_prev = bf16[256,1024]{1,0:T(8,128)(2,1)} fusion(bf16[256,1024]{1,0:T(8,128)(2,1)} %copy-done.22, bf16[1024,1024]{1,0:T(8,128)(2,1)} %param.13), kind=kOutput, calls=%fused_computation.15 | convolution fusion | flops 537133056 | bytes 3145728 | tf_op jit(solution)/shard_map/dot_general | solution.py:54
  68.6 1.6 convolution_convert_fusion.5.k_prev
  70.2 7.6 %forward.1 = (f32[16,256]{1,0:T(8,128)}, f32[16,256]{1,0:T(8,128)}, f32[1024,256]{1,0:T(8,128)}, bf16[16,512,256]{2,1,0:T(8,128)(2,1)}) custom-call(bf16[256,1024]{1,0:T(8,128)(2,1)} %convolution_convert_fusion.7.k_own, bf16[256,1024]{1,0:T(8,128)(2,1)} %convolution_convert_fusion.6.v_own, bf16[256,1024]{1,0:T(8,128)(2,1)} %convolution_convert_fusion.5.k_prev, ...), custom_call_target="tpu_custom_call" | custom-call | tf_op jit(solution)/shard_map/forward/pallas_call | solution.py:121
  77.8 1.4 all-to-all-done.1
  79.2 1.0 copy-done.14
  80.2 3.1 %cotangent.1 = (bf16[256,1024]{1,0:T(8,128)(2,1)}, bf16[1024,256]{1,0:T(8,128)(2,1)}, f32[40,256]{1,0:T(8,128)}) custom-call(bf16[512,1024]{1,0:T(8,128)(2,1)} %bitcast.51, bf16[256,512]{1,0:T(8,128)(2,1)} %fusion.19.pick, f32[1024,256]{1,0:T(8,128)} %get-tuple-element.77.out_t, f32[16,256]{1,0:T(8,128)} %get-tuple-element.78.lse, f32[1,256]{1,0:T(1,128)} %bitcast.58), custom_call_target="tpu_custom_call" | custom-call | tf_op jit(solution)/shard_map/cotangent/pallas_call | solution.py:157
  83.3 1.5 collective-permute-start.7
  84.8 3.0 %collective-permute-done.7 = f32[40,256]{1,0:T(8,128)S(1)} collective-permute-done((f32[40,256]{1,0:T(8,128)}, f32[40,256]{1,0:T(8,128)S(1)}, u32[]{:S(2)}, u32[]{:S(2)}) %collective-permute-start.7) | collective-permute-done | bytes 40992 | tf_op jit(solution)/shard_map/ppermute | solution.py:357
  87.8 0.9 broadcast_in_dim.41
  88.7 4.7 %all-to-all-start.2 = ((f32[8,2,40,256]{3,2,1,0:T(8,128)}), f32[8,2,40,256]{3,2,1,0:T(8,128)S(1)}, u32[]{:S(2)}, u32[]{:S(2)}) async-start(f32[8,2,40,256]{3,2,1,0:T(8,128)} %broadcast_in_dim.41), calls=%async_computation.2 | async-start | bytes 1310720 | tf_op jit(solution)/shard_map/all_to_all | solution.py:360
  94.0 0.8 copy.14.wanted
  94.9 2.7 %fusion.2 = bf16[512,512]{1,0:T(8,128)(2,1)} fusion(s32[512]{0:T(512)S(1)} %get-tuple-element.149, bf16[256,1024]{1,0:T(8,128)(2,1)S(1)} %copy-done.18, bf16[256,1024]{1,0:T(8,128)(2,1)} %copy-done.22), kind=kOutput, calls=%fused_computation.11 | convolution fusion | flops 539754496 | bytes 1574912 | tf_op jit(solution)/shard_map/dot_general | solution.py:54
  97.5 0.8 fusion.3.x_t
  98.3 6.0 %all-to-all-done.2 = f32[8,2,40,256]{3,2,1,0:T(8,128)S(1)} async-done(((f32[8,2,40,256]{3,2,1,0:T(8,128)}), f32[8,2,40,256]{3,2,1,0:T(8,128)S(1)}, u32[]{:S(2)}, u32[]{:S(2)}) %all-to-all-start.2) | async-done | bytes 655392 | tf_op jit(solution)/shard_map/all_to_all | solution.py:360
  104.3 0.8 copy-done.15
  105.1 11.1 %backward.1.grads = bf16[2,512,1024]{2,1,0:T(8,128)(2,1)} custom-call(f32[16,40,256]{2,1,0:T(8,128)} %bitcast.55, f32[256,1]{1,0:T(8,128)} %copy.14.wanted, f32[40,256]{1,0:T(8,128)} %get-tuple-element.80.mine, f32[16,256]{1,0:T(8,128)} %get-tuple-element.82.inverse, bf16[16,512,256]{2,1,0:T(8,128)(2,1)} %get-tuple-element.83.probs, ...), custom_call_target="tpu_custom_call" | custom-call | tf_op jit(solution)/shard_map/backward/pallas_call | solution.py:241
  116.2 1.9 %fusion.9 = f32[256,1024]{1,0:T(8,128)S(1)} fusion(bf16[1024,1024]{1,0:T(8,128)(2,1)S(1)} %copy-done, bf16[2,512,1024]{2,1,0:T(8,128)(2,1)} %backward.1.grads), kind=kOutput, calls=%fused_computation.31 | convolution fusion | flops 536870912 | bytes 3670016 | tf_op jit(solution)/shard_map/dot_general | solution.py:54
  118.2 0.7 fusion.5
  122.0 1.4 collective-permute-done.10.other_v
  123.4 1.5 collective-permute-done.9.other_k
  124.9 1.3 fold.3
  126.8 1.5 collective-permute-start.12
  129.1 0.9 collective-permute-start.13
  129.9 0.8 fusion.4.y_own
  130.7 1.5 place_rows.1
  132.2 4.8 %collective-permute-done.13.refs_5_ = bf16[256,512]{1,0:T(8,128)(2,1)S(1)} collective-permute-done((bf16[256,512]{1,0:T(8,128)(2,1)S(1)}, bf16[256,512]{1,0:T(8,128)(2,1)S(1)}, u32[]{:S(2)}, u32[]{:S(2)}) %collective-permute-start.13) | collective-permute-done | bytes 262176 | tf_op jit(solution)/shard_map/ppermute | solution.py:357
  138.1 0.8 copy-done.2
  138.8 4.2 %all-to-all-start.3 = ((bf16[8,64,1024]{2,1,0:T(8,128)(2,1)}), bf16[8,64,1024]{2,1,0:T(8,128)(2,1)}, u32[]{:S(2)}, u32[]{:S(2)}) async-start(bf16[8,64,1024]{2,1,0:T(8,128)(2,1)} %bitcast.18), calls=%async_computation.3 | async-start | bytes 2097152 | tf_op jit(solution)/shard_map/all_to_all | solution.py:360
  143.1 1.0 copy-done.3
  144.1 0.9 copy-done.5
  145.0 0.9 copy-done.7
  147.6 1.9 collective-permute-start.14
  149.5 1.5 collective-permute-start.15
  151.0 1.5 collective-permute-start.16
  152.6 6.8 %collective-permute-done.16.refs_5_ = bf16[128,512]{1,0:T(8,128)(2,1)S(1)} collective-permute-done((bf16[128,512]{1,0:T(8,128)(2,1)S(1)}, bf16[128,512]{1,0:T(8,128)(2,1)S(1)}, u32[]{:S(2)}, u32[]{:S(2)}) %collective-permute-start.16) | collective-permute-done | bytes 131104 | tf_op jit(solution)/shard_map/ppermute | solution.py:357
  159.3 1.7 collective-permute-done.14.refs_1_
  161.0 1.8 convolution_convert_fusion.2
  162.9 1.9 collective-permute-done.17
  164.8 1.7 convolution_add_fusion
  166.5 1.9 collective-permute-start.21
  168.5 1.4 collective-permute-start.18
  169.9 0.9 collective-permute-start.19
  171.4 10.1 %collective-permute-done.21 = bf16[128,1024]{1,0:T(8,128)(2,1)S(1)} collective-permute-done((bf16[128,1024]{1,0:T(8,128)(2,1)S(1)}, bf16[128,1024]{1,0:T(8,128)(2,1)S(1)}, u32[]{:S(2)}, u32[]{:S(2)}) %collective-permute-start.21) | collective-permute-done | bytes 262176 | tf_op jit(solution)/shard_map/ppermute | solution.py:357
  181.4 0.8 fusion.8
  182.4 8.4 %collective-permute-done.22 = bf16[32,2048]{1,0:T(8,128)(2,1)S(1)} collective-permute-done((bf16[32,2048]{1,0:T(8,128)(2,1)S(1)}, bf16[32,2048]{1,0:T(8,128)(2,1)S(1)}, u32[]{:S(2)}, u32[]{:S(2)}) %collective-permute-start.22) | collective-permute-done | bytes 131104 | tf_op jit(solution)/shard_map/ppermute | solution.py:357
  (106 shorter events, 14.5 us)
Async XLA Ops:
  0.6 52.0 %copy-start = (bf16[1024,1024]{1,0:T(8,128)(2,1)S(1)}, bf16[1024,1024]{1,0:T(8,128)(2,1)}, u32[]{:S(2)}) copy-start(bf16[1024,1024]{1,0:T(8,128)(2,1)} %param.12) | copy-start | bytes 6291460
  0.6 21.8 %copy-start.16 = (bf16[256,1024]{1,0:T(8,128)(2,1)S(1)}, bf16[256,1024]{1,0:T(8,128)(2,1)}, u32[]{:S(2)}) copy-start(bf16[256,1024]{1,0:T(8,128)(2,1)} %param.10) | copy-start | bytes 1572868
  2.6 17.5 %collective-permute-start.1 = (bf16[144,1024]{1,0:T(8,128)(2,1)S(1)}, bf16[144,1024]{1,0:T(8,128)(2,1)}, u32[]{:S(2)}, u32[]{:S(2)}) collective-permute-start(bf16[144,1024]{1,0:T(8,128)(2,1)S(1)} %pad_maximum_fusion.4), channel_id=1, source_target_pairs={{0,16},{1,17},{2,18},{3,19},{4,20},{5,21},{6,22},{7,23},{8,24},{9,... | collective-permute-start | bytes 884744 | tf_op jit(solution)/shard_map/ppermute | solution.py:357
  6.7 18.7 %collective-permute-start = (s32[256]{0:T(256)}, s32[256]{0:T(256)S(1)}, u32[]{:S(2)}, u32[]{:S(2)}) collective-permute-start(s32[256]{0:T(256)} %bitcast.62), channel_id=1, source_target_pairs={{0,0},{1,1},{14,2},{19,3},{30,4},{3,5},{16,6},{17,7},{2,8},{31,9},... | collective-permute-start | bytes 3080 | tf_op jit(solution)/shard_map/ppermute | solution.py:357
  22.2 1.6 collective-permute-start.2
  25.3 23.4 %all-to-all-start = ((bf16[8,64,1024]{2,1,0:T(8,128)(2,1)}), bf16[8,64,1024]{2,1,0:T(8,128)(2,1)S(1)}, u32[]{:S(2)}, u32[]{:S(2)}) async-start(bf16[8,64,1024]{2,1,0:T(8,128)(2,1)} %bitcast.53), calls=%async_computation | async-start | bytes 2097152 | tf_op jit(solution)/shard_map/all_to_all | solution.py:360
  29.4 19.9 %collective-permute-start.4 = (bf16[128,1024]{1,0:T(8,128)(2,1)S(1)}, bf16[128,1024]{1,0:T(8,128)(2,1)}, u32[]{:S(2)}, u32[]{:S(2)}) collective-permute-start(bf16[128,1024]{1,0:T(8,128)(2,1)S(1)} %constant_dynamic-slice_fusion), channel_id=1, source_target_pairs={{0,16},{1,17},{2,18},{3,19},{4,20},{5,21},{6,22},{7,23},{8,24},{9,... | collective-permute-start | bytes 786440 | tf_op jit(solution)/shard_map/ppermute | solution.py:357
  49.2 5.0 %copy-start.17 = (bf16[256,1024]{1,0:T(8,128)(2,1)}, bf16[256,1024]{1,0:T(8,128)(2,1)S(1)}, u32[]{:S(2)}) copy-start(bf16[256,1024]{1,0:T(8,128)(2,1)S(1)} %convolution_convert_fusion.3) | copy-start | bytes 1572868
  49.2 9.2 %collective-permute-start.3 = (bf16[256,1024]{1,0:T(8,128)(2,1)S(1)}, bf16[256,1024]{1,0:T(8,128)(2,1)S(1)}, u32[]{:S(2)}, u32[]{:S(2)}) collective-permute-start(bf16[256,1024]{1,0:T(8,128)(2,1)S(1)} %convolution_convert_fusion.3), channel_id=1, source_target_pairs={{0,8},{1,5},{8,16},{5,13},{16,24},{13,21},{24,26},{21,29},{26,18},... | collective-permute-start | bytes 1572872 | tf_op jit(solution)/shard_map/ppermute | solution.py:357
  49.3 4.9 %collective-permute-start.5 = (bf16[128,1024]{1,0:T(8,128)(2,1)}, bf16[128,1024]{1,0:T(8,128)(2,1)S(1)}, u32[]{:S(2)}, u32[]{:S(2)}) collective-permute-start(bf16[128,1024]{1,0:T(8,128)(2,1)} %collective-permute-done.4), channel_id=1, source_target_pairs={{0,1},{1,0},{2,3},{3,2},{4,5},{5,4},{6,7},{7,6},{8,9},{9,8},{10,11... | collective-permute-start | bytes 786440 | tf_op jit(solution)/shard_map/ppermute | solution.py:357
  52.7 1.6 copy-start.13
  58.5 0.8 copy-start.22
  59.3 19.9 %all-to-all-start.1 = ((bf16[8,64,1024]{2,1,0:T(8,128)(2,1)}), bf16[8,64,1024]{2,1,0:T(8,128)(2,1)S(1)}, u32[]{:S(2)}, u32[]{:S(2)}) async-start(bf16[8,64,1024]{2,1,0:T(8,128)(2,1)} %bitcast.54), calls=%async_computation.1 | async-start | bytes 2097152 | tf_op jit(solution)/shard_map/all_to_all | solution.py:360
  63.9 4.7 %copy-start.23 = (bf16[256,1024]{1,0:T(8,128)(2,1)S(1)}, bf16[256,1024]{1,0:T(8,128)(2,1)}, u32[]{:S(2)}) copy-start(bf16[256,1024]{1,0:T(8,128)(2,1)} %copy-done.22) | copy-start | bytes 1572868
  79.2 1.0 copy-start.14
  80.2 13.9 %copy-start.20 = (f32[256]{0:T(256)S(1)}, f32[256]{0:T(256)}, u32[]{:S(2)}) copy-start(f32[256]{0:T(256)} %convert_element_type.126) | copy-start | bytes 3076
  83.3 11.6 %copy-start.18 = (bf16[256,1024]{1,0:T(8,128)(2,1)S(1)}, bf16[256,1024]{1,0:T(8,128)(2,1)}, u32[]{:S(2)}) copy-start(bf16[256,1024]{1,0:T(8,128)(2,1)} %copy-done.17) | copy-start | bytes 1572868
  83.3 1.5 collective-permute-start.6
  83.3 4.5 %collective-permute-start.7 = (f32[40,256]{1,0:T(8,128)}, f32[40,256]{1,0:T(8,128)S(1)}, u32[]{:S(2)}, u32[]{:S(2)}) collective-permute-start(f32[40,256]{1,0:T(8,128)} %get-tuple-element.80.mine), channel_id=1, source_target_pairs={{0,17},{1,16},{2,19},{3,18},{4,21},{5,20},{6,23},{7,22},{8,25},{9,... | collective-permute-start | bytes 122888 | tf_op jit(solution)/shard_map/ppermute | solution.py:357
  88.7 15.6 %all-to-all-start.2 = ((f32[8,2,40,256]{3,2,1,0:T(8,128)}), f32[8,2,40,256]{3,2,1,0:T(8,128)S(1)}, u32[]{:S(2)}, u32[]{:S(2)}) async-start(f32[8,2,40,256]{3,2,1,0:T(8,128)} %broadcast_in_dim.41), calls=%async_computation.2 | async-start | bytes 1310720 | tf_op jit(solution)/shard_map/all_to_all | solution.py:360
  94.8 2.7 %copy-start.19 = (bf16[256,1024]{1,0:T(8,128)(2,1)S(1)}, bf16[256,1024]{1,0:T(8,128)(2,1)}, u32[]{:S(2)}) copy-start(bf16[256,1024]{1,0:T(8,128)(2,1)} %copy-done.17) | copy-start | bytes 1572868
  94.8 2.7 %copy-start.21 = (s32[512]{0:T(512)S(1)}, s32[512]{0:T(512)}, u32[]{:S(2)}) copy-start(s32[512]{0:T(512)} %get-tuple-element.150) | copy-start | bytes 6148
  94.8 2.7 %copy-start.24 = (bf16[256,1024]{1,0:T(8,128)(2,1)S(1)}, bf16[256,1024]{1,0:T(8,128)(2,1)}, u32[]{:S(2)}) copy-start(bf16[256,1024]{1,0:T(8,128)(2,1)} %copy-done.22) | copy-start | bytes 1572868
  104.3 0.8 copy-start.15
  105.1 13.0 %copy-start.12 = (bf16[1024,1024]{1,0:T(8,128)(2,1)S(1)}, bf16[1024,1024]{1,0:T(8,128)(2,1)}, u32[]{:S(2)}) copy-start(bf16[1024,1024]{1,0:T(8,128)(2,1)} %param.13) | copy-start | bytes 6291460
  116.2 2.0 %copy-start.1 = (bf16[2,512,1024]{2,1,0:T(8,128)(2,1)S(1)}, bf16[2,512,1024]{2,1,0:T(8,128)(2,1)}, u32[]{:S(2)}) copy-start(bf16[2,512,1024]{2,1,0:T(8,128)(2,1)} %backward.1.grads) | copy-start | bytes 6291460
  118.2 1.0 copy-start.25
  120.7 2.7 %collective-permute-start.10 = (bf16[512,1024]{1,0:T(8,128)(2,1)S(1)}, bf16[512,1024]{1,0:T(8,128)(2,1)S(1)}, u32[]{:S(2)}, u32[]{:S(2)}) collective-permute-start(bf16[512,1024]{1,0:T(8,128)(2,1)S(1)} %convolution_convert_fusion), channel_id=1, source_target_pairs={{0,1},{1,0},{2,3},{3,2},{4,5},{5,4},{6,7},{7,6},{8,9},{9,8},{10,11... | collective-permute-start | bytes 3145736 | tf_op jit(solution)/shard_map/ppermute | solution.py:357
  120.7 4.1 %collective-permute-start.9 = (bf16[512,1024]{1,0:T(8,128)(2,1)S(1)}, bf16[512,1024]{1,0:T(8,128)(2,1)S(1)}, u32[]{:S(2)}, u32[]{:S(2)}) collective-permute-start(bf16[512,1024]{1,0:T(8,128)(2,1)S(1)} %convolution_convert_fusion.1), channel_id=1, source_target_pairs={{0,1},{1,0},{2,3},{3,2},{4,5},{5,4},{6,7},{7,6},{8,9},{9,8},{10,11... | collective-permute-start | bytes 3145736 | tf_op jit(solution)/shard_map/ppermute | solution.py:357
  121.3 9.4 %collective-permute-start.8 = (bf16[256,1024]{1,0:T(8,128)(2,1)S(1)}, bf16[256,1024]{1,0:T(8,128)(2,1)S(1)}, u32[]{:S(2)}, u32[]{:S(2)}) collective-permute-start(bf16[256,1024]{1,0:T(8,128)(2,1)S(1)} %fusion.5), channel_id=1, source_target_pairs={{8,0},{5,1},{16,8},{13,5},{24,16},{21,13},{26,24},{29,21},{18,26},... | collective-permute-start | bytes 1572872 | tf_op jit(solution)/shard_map/ppermute | solution.py:357
  126.2 4.5 %copy-start.4 = (bf16[256,512]{1,0:T(8,128)(2,1)}, bf16[256,512]{1,0:T(8,128)(2,1)S(1)}, u32[]{:S(2)}) copy-start(bf16[256,512]{1,0:T(8,128)(2,1)S(1)} %get-tuple-element.100.refs_4_) | copy-start | bytes 786436
  126.2 11.5 %collective-permute-start.11 = (bf16[256,768]{1,0:T(8,128)(2,1)S(1)}, bf16[256,768]{1,0:T(8,128)(2,1)S(1)}, u32[]{:S(2)}, u32[]{:S(2)}) collective-permute-start(bf16[256,768]{1,0:T(8,128)(2,1)S(1)} %get-tuple-element.90), channel_id=1, source_target_pairs={{0,2},{1,3},{2,0},{3,1},{4,6},{5,7},{6,4},{7,5},{8,10},{9,11},{10,... | collective-permute-start | bytes 1179656 | tf_op jit(solution)/shard_map/ppermute | solution.py:357
  126.8 11.3 %collective-permute-start.12 = (bf16[256,768]{1,0:T(8,128)(2,1)S(1)}, bf16[256,768]{1,0:T(8,128)(2,1)S(1)}, u32[]{:S(2)}, u32[]{:S(2)}) collective-permute-start(bf16[256,768]{1,0:T(8,128)(2,1)S(1)} %get-tuple-element.92), channel_id=1, source_target_pairs={{0,4},{1,5},{2,6},{3,7},{4,0},{5,1},{6,2},{7,3},{8,12},{9,13},{10,... | collective-permute-start | bytes 1179656 | tf_op jit(solution)/shard_map/ppermute | solution.py:357
  129.1 7.9 %collective-permute-start.13 = (bf16[256,512]{1,0:T(8,128)(2,1)S(1)}, bf16[256,512]{1,0:T(8,128)(2,1)S(1)}, u32[]{:S(2)}, u32[]{:S(2)}) collective-permute-start(bf16[256,512]{1,0:T(8,128)(2,1)S(1)} %get-tuple-element.94), channel_id=1, source_target_pairs={{0,8},{1,9},{2,10},{3,11},{4,12},{5,13},{6,14},{7,15},{8,0},{9,1},... | collective-permute-start | bytes 786440 | tf_op jit(solution)/shard_map/ppermute | solution.py:357
  136.9 0.7 copy-start.6
  138.1 0.8 copy-start.2
  138.8 22.2 %all-to-all-start.3 = ((bf16[8,64,1024]{2,1,0:T(8,128)(2,1)}), bf16[8,64,1024]{2,1,0:T(8,128)(2,1)}, u32[]{:S(2)}, u32[]{:S(2)}) async-start(bf16[8,64,1024]{2,1,0:T(8,128)(2,1)} %bitcast.18), calls=%async_computation.3 | async-start | bytes 2097152 | tf_op jit(solution)/shard_map/all_to_all | solution.py:360
  143.1 1.0 copy-start.3
  144.1 0.9 copy-start.5
  145.0 0.9 copy-start.7
  146.2 0.7 copy-start.8
  146.9 0.7 copy-start.10
  147.6 13.4 %collective-permute-start.14 = (bf16[128,768]{1,0:T(8,128)(2,1)S(1)}, bf16[128,768]{1,0:T(8,128)(2,1)S(1)}, u32[]{:S(2)}, u32[]{:S(2)}) collective-permute-start(bf16[128,768]{1,0:T(8,128)(2,1)S(1)} %get-tuple-element.103), channel_id=1, source_target_pairs={{0,4},{1,5},{2,6},{3,7},{4,0},{5,1},{6,2},{7,3},{8,12},{9,13},{10,... | collective-permute-start | bytes 589832 | tf_op jit(solution)/shard_map/ppermute | solution.py:357
  149.5 11.5 %collective-permute-start.15 = (bf16[128,768]{1,0:T(8,128)(2,1)S(1)}, bf16[128,768]{1,0:T(8,128)(2,1)S(1)}, u32[]{:S(2)}, u32[]{:S(2)}) collective-permute-start(bf16[128,768]{1,0:T(8,128)(2,1)S(1)} %get-tuple-element.105), channel_id=1, source_target_pairs={{0,8},{1,9},{2,10},{3,11},{4,12},{5,13},{6,14},{7,15},{8,0},{9,1},... | collective-permute-start | bytes 589832 | tf_op jit(solution)/shard_map/ppermute | solution.py:357
  151.0 8.3 %collective-permute-start.16 = (bf16[128,512]{1,0:T(8,128)(2,1)S(1)}, bf16[128,512]{1,0:T(8,128)(2,1)S(1)}, u32[]{:S(2)}, u32[]{:S(2)}) collective-permute-start(bf16[128,512]{1,0:T(8,128)(2,1)S(1)} %get-tuple-element.107), channel_id=1, source_target_pairs={{0,2},{1,3},{2,0},{3,1},{4,6},{5,7},{6,4},{7,5},{8,10},{9,11},{10,... | collective-permute-start | bytes 393224 | tf_op jit(solution)/shard_map/ppermute | solution.py:357
  161.0 7.4 %copy-start.9 = (bf16[128,768]{1,0:T(8,128)(2,1)S(1)}, bf16[128,768]{1,0:T(8,128)(2,1)}, u32[]{:S(2)}) copy-start(bf16[128,768]{1,0:T(8,128)(2,1)} %copy-done.8) | copy-start | bytes 589828
  161.0 7.4 %copy-start.11 = (bf16[128,768]{1,0:T(8,128)(2,1)S(1)}, bf16[128,768]{1,0:T(8,128)(2,1)}, u32[]{:S(2)}) copy-start(bf16[128,768]{1,0:T(8,128)(2,1)} %copy-done.10) | copy-start | bytes 589828
  162.8 2.0 %collective-permute-start.17 = (bf16[256,1024]{1,0:T(8,128)(2,1)S(1)}, bf16[256,1024]{1,0:T(8,128)(2,1)S(1)}, u32[]{:S(2)}, u32[]{:S(2)}) collective-permute-start(bf16[256,1024]{1,0:T(8,128)(2,1)S(1)} %convolution_convert_fusion.2), channel_id=1, source_target_pairs={{0,1},{1,0},{2,3},{3,2},{4,5},{5,4},{6,7},{7,6},{8,9},{9,8},{10,11... | collective-permute-start | bytes 1572872 | tf_op jit(solution)/shard_map/ppermute | solution.py:357
  166.5 14.9 %collective-permute-start.21 = (bf16[128,1024]{1,0:T(8,128)(2,1)S(1)}, bf16[128,1024]{1,0:T(8,128)(2,1)S(1)}, u32[]{:S(2)}, u32[]{:S(2)}) collective-permute-start(bf16[128,1024]{1,0:T(8,128)(2,1)S(1)} %slice.101), channel_id=1, source_target_pairs={{0,16},{1,17},{2,18},{3,19},{4,20},{5,21},{6,22},{7,23},{8,24},{9,... | collective-permute-start | bytes 786440 | tf_op jit(solution)/shard_map/ppermute | solution.py:357
  168.5 13.7 %collective-permute-start.18 = (bf16[64,768]{1,0:T(8,128)(2,1)S(1)}, bf16[64,768]{1,0:T(8,128)(2,1)S(1)}, u32[]{:S(2)}, u32[]{:S(2)}) collective-permute-start(bf16[64,768]{1,0:T(8,128)(2,1)S(1)} %get-tuple-element.122), channel_id=1, source_target_pairs={{0,8},{1,9},{2,10},{3,11},{4,12},{5,13},{6,14},{7,15},{8,0},{9,1},... | collective-permute-start | bytes 294920 | tf_op jit(solution)/shard_map/ppermute | solution.py:357
  169.9 12.3 %collective-permute-start.19 = (bf16[64,768]{1,0:T(8,128)(2,1)S(1)}, bf16[64,768]{1,0:T(8,128)(2,1)S(1)}, u32[]{:S(2)}, u32[]{:S(2)}) collective-permute-start(bf16[64,768]{1,0:T(8,128)(2,1)S(1)} %get-tuple-element.124), channel_id=1, source_target_pairs={{0,2},{1,3},{2,0},{3,1},{4,6},{5,7},{6,4},{7,5},{8,10},{9,11},{10,... | collective-permute-start | bytes 294920 | tf_op jit(solution)/shard_map/ppermute | solution.py:357
  170.8 11.4 %collective-permute-start.20 = (bf16[64,512]{1,0:T(8,128)(2,1)S(1)}, bf16[64,512]{1,0:T(8,128)(2,1)S(1)}, u32[]{:S(2)}, u32[]{:S(2)}) collective-permute-start(bf16[64,512]{1,0:T(8,128)(2,1)S(1)} %get-tuple-element.126), channel_id=1, source_target_pairs={{0,4},{1,5},{2,6},{3,7},{4,0},{5,1},{6,2},{7,3},{8,12},{9,13},{10,... | collective-permute-start | bytes 196616 | tf_op jit(solution)/shard_map/ppermute | solution.py:357
  182.4 8.5 %collective-permute-start.22 = (bf16[32,2048]{1,0:T(8,128)(2,1)S(1)}, bf16[32,2048]{1,0:T(8,128)(2,1)S(1)}, u32[]{:S(2)}, u32[]{:S(2)}) collective-permute-start(bf16[32,2048]{1,0:T(8,128)(2,1)S(1)} %slice.102), channel_id=1, source_target_pairs={{0,16},{1,17},{2,18},{3,19},{4,20},{5,21},{6,22},{7,23},{8,24},{9,... | collective-permute-start | bytes 393224 | tf_op jit(solution)/shard_map/ppermute | solution.py:357

commit v5 on v4

--- a/solution.py
+++ b/solution.py
@@ -445,11 +445,11 @@
     theirs = [move(mm(x_theirs, grads[k]).astype(bf16), swap) for k in range(2)]
     y_own = (mm(grads[0, SPAN:], w_qk, NT) + mm(grads[1, SPAN:], w_v, NT)).astype(bf16)
 
-    bits = near.bit_length() - 1
+    bits = peers.bit_length() - 1
     blocks = 2 * width // BLOCK
     edges = [BLOCK * ((blocks * k + 2) // 3) for k in range(4)]
     widths = [edges[k + 1] - edges[k] for k in range(3)]
-    left = [list(range(bits + 1)) for _ in range(3)]
+    left = [list(range(bits)) for _ in range(3)]
     pairs = None
     for turn in range(bits):
         turn_bits = [(k * bits // 3 + turn) % bits for k in range(3)]
@@ -481,9 +481,8 @@
             grad_x = (my_rows[part_rows:] + crossing.astype(f32)).astype(bf16)
 
     pairs, grad_x = lax.optimization_barrier((pairs, grad_x))
-    summed = jnp.concatenate([a.astype(f32) + b.astype(f32) for a, b in pairs], axis=1)
-    leaving = move(summed[each:].astype(bf16), mirror).astype(f32)
-    weight_grads = (summed[:each] + leaving) * (tdev * peers) ** (-0.5)
+    weight_grads = jnp.concatenate([a.astype(f32) + b.astype(f32) for a, b in pairs], axis=1)
+    weight_grads = weight_grads * (tdev * peers) ** (-0.5)
     return (grad_x, weight_grads[:, :width], weight_grads[:, width:])
 
 

time: 193 us -> 196 us (1.016)
  starting transfers between devices: 42.1 us -> 47.2 us
  waiting for transfers between devices: 73.3 us -> 71.1 us
    ppermute x23 -> x25, starting transfers between devices: 24.7 us -> 29.8 us  [move(): return lax.ppermute(rows, both, route)]
    ppermute x23 -> x25, waiting for transfers between devices: 53 us -> 50.9 us  [move(): return lax.ppermute(rows, both, route)]
  transfers between devices with their start and end apart: 27 -> 29, of which waited for: 16 -> 18; matrix products, arithmetic and copies ran while one was open for 16% -> 16% of each run, Pallas kernels for 6% -> 6%
where the time goes in v5:
time: 196 us; the launch traced here: 194 us
  waiting for transfers between devices  71.1 us (36%)
  starting transfers between devices  47.2 us (24%)
  matrix products  30.1 us (15%)
  Pallas kernels  24.9 us (13%)
  local copies, waits for them, and re-layouts  14.4 us (7%)
  other arithmetic  5.71 us (3%)
    ppermute x25, waiting for transfers between devices, move(): return lax.ppermute(rows, both, route)  50.9 us
    dot_general x19, matrix products, mm(): return lax.dot_general(a, b, dims, preferred_element_type=f32)  30.1 us
    ppermute x25, starting transfers between devices, move(): return lax.ppermute(rows, both, route)  29.8 us
    all_to_all x4, waiting for transfers between devices, exchange(): lax.all_to_all(blocks, 'ctx', 0, 0, axis_index_groups=halves, tiled=True)  20.2 us
    all_to_all x4, starting transfers between devices, exchange(): lax.all_to_all(blocks, 'ctx', 0, 0, axis_index_groups=halves, tiled=True)  17.4 us
    pallas_call x1, Pallas kernels, backward(): pl.pallas_call(functools.partial(backward_kernel, scale), grid=(width //...  11.1 us
    unnamed x52, local copies, waits for them, and re-layouts  8.72 us
    pallas_call x1, Pallas kernels, forward(): pl.pallas_call(functools.partial(forward_kernel, scale), grid=(width // B...  7.62 us
  transfers between devices with their start and end apart: 29, of which 18 were waited for; matrix products, arithmetic and copies ran while one was open for 16% of the time, Pallas kernels for 6%

profile of v5, /device:TPU:0, one launch (start us, length us, event | category | flops | bytes accessed | tf_op | source)
XLA Modules:
  0.0 194.5 jit_solution(16031488926994421896)
XLA Ops:
  0.7 1.1 constant_dynamic-slice_fusion.1
  2.6 4.1 %collective-permute-start.1 = (bf16[144,1024]{1,0:T(8,128)(2,1)S(1)}, bf16[144,1024]{1,0:T(8,128)(2,1)}, u32[]{:S(2)}, u32[]{:S(2)}) collective-permute-start(bf16[144,1024]{1,0:T(8,128)(2,1)S(1)} %pad_maximum_fusion.3), channel_id=1, source_target_pairs={{0,16},{1,17},{2,18},{3,19},{4,20},{5,21},{6,22},{7,23},{8,24},{9,... | collective-permute-start | bytes 884744 | tf_op jit(solution)/shard_map/ppermute | solution.py:357
  6.7 1.3 collective-permute-start
  8.7 1.0 constant_dynamic-slice_fusion
  9.6 10.5 %collective-permute-done.1 = bf16[144,1024]{1,0:T(8,128)(2,1)} collective-permute-done((bf16[144,1024]{1,0:T(8,128)(2,1)S(1)}, bf16[144,1024]{1,0:T(8,128)(2,1)}, u32[]{:S(2)}, u32[]{:S(2)}) %collective-permute-start.1) | collective-permute-done | bytes 294944 | tf_op jit(solution)/shard_map/ppermute | solution.py:357
  20.8 1.0 slice.48
  23.0 0.8 collective-permute-done.2
  23.8 1.5 add_convert_fusion.1
  25.3 3.8 %all-to-all-start = ((bf16[8,64,1024]{2,1,0:T(8,128)(2,1)}), bf16[8,64,1024]{2,1,0:T(8,128)(2,1)S(1)}, u32[]{:S(2)}, u32[]{:S(2)}) async-start(bf16[8,64,1024]{2,1,0:T(8,128)(2,1)} %bitcast.53), calls=%async_computation | async-start | bytes 2097152 | tf_op jit(solution)/shard_map/all_to_all | solution.py:360
  29.4 3.6 %collective-permute-start.4 = (bf16[128,1024]{1,0:T(8,128)(2,1)S(1)}, bf16[128,1024]{1,0:T(8,128)(2,1)}, u32[]{:S(2)}, u32[]{:S(2)}) collective-permute-start(bf16[128,1024]{1,0:T(8,128)(2,1)S(1)} %constant_dynamic-slice_fusion), channel_id=1, source_target_pairs={{0,16},{1,17},{2,18},{3,19},{4,20},{5,21},{6,22},{7,23},{8,24},{9,... | collective-permute-start | bytes 786440 | tf_op jit(solution)/shard_map/ppermute | solution.py:357
  32.9 2.9 %fusion.17 = f32[512,1024]{1,0:T(8,128)} fusion(bf16[256,1024]{1,0:T(8,128)(2,1)} %param.11, s32[256]{0:T(256)S(1)} %get-tuple-element.160), kind=kOutput, calls=%fused_computation.45 | convolution fusion | flops 268566528 | bytes 2622464 | tf_op jit(solution)/shard_map/dot_general | solution.py:54
  35.9 12.9 %all-to-all-done = bf16[8,64,1024]{2,1,0:T(8,128)(2,1)S(1)} async-done(((bf16[8,64,1024]{2,1,0:T(8,128)(2,1)}), bf16[8,64,1024]{2,1,0:T(8,128)(2,1)S(1)}, u32[]{:S(2)}, u32[]{:S(2)}) %all-to-all-start) | async-done | bytes 1048608 | tf_op jit(solution)/shard_map/all_to_all | solution.py:360
  49.5 3.2 %convolution_convert_fusion.6.v_own = bf16[256,1024]{1,0:T(8,128)(2,1)} fusion(bf16[256,1024]{1,0:T(8,128)(2,1)S(1)} %convolution_convert_fusion.3, bf16[1024,1024]{1,0:T(8,128)(2,1)} %param.13), kind=kOutput, calls=%fused_computation.17 | convolution fusion | flops 537133056 | bytes 3145728 | tf_op jit(solution)/shard_map/dot_general | solution.py:54
  52.7 1.6 convolution_convert_fusion.7.k_own
  54.3 2.5 %add_convert_fusion = bf16[512,1024]{1,0:T(8,128)(2,1)} fusion(f32[512,1024]{1,0:T(8,128)S(1)} %copy-done.13, bf16[128,1024]{1,0:T(8,128)(2,1)S(1)} %collective-permute-done.5, bf16[128,1024]{1,0:T(8,128)(2,1)} %collective-permute-done.4, s32[256]{0:T(256)S(1)} %add_select_fusion.1), kind=kOutput, calls=%fused_computation.2 | convolution fusion | flops 270663680 | bytes 3671040 | tf_op jit(solution)/shard_map/dot_general | solution.py:54
  56.8 1.7 collective-permute-done.3
  58.5 0.8 copy-done.22
  59.3 4.6 %all-to-all-start.1 = ((bf16[8,64,1024]{2,1,0:T(8,128)(2,1)}), bf16[8,64,1024]{2,1,0:T(8,128)(2,1)S(1)}, u32[]{:S(2)}, u32[]{:S(2)}) async-start(bf16[8,64,1024]{2,1,0:T(8,128)(2,1)} %bitcast.54), calls=%async_computation.1 | async-start | bytes 2097152 | tf_op jit(solution)/shard_map/all_to_all | solution.py:360
  63.9 0.8 fusion.19.pick
  65.3 3.3 %convolution_convert_fusion.4.v_prev = bf16[256,1024]{1,0:T(8,128)(2,1)} fusion(bf16[256,1024]{1,0:T(8,128)(2,1)} %copy-done.22, bf16[1024,1024]{1,0:T(8,128)(2,1)} %param.13), kind=kOutput, calls=%fused_computation.15 | convolution fusion | flops 537133056 | bytes 3145728 | tf_op jit(solution)/shard_map/dot_general | solution.py:54
  68.6 1.6 convolution_convert_fusion.5.k_prev
  70.2 7.6 %forward.1 = (f32[16,256]{1,0:T(8,128)}, f32[16,256]{1,0:T(8,128)}, f32[1024,256]{1,0:T(8,128)}, bf16[16,512,256]{2,1,0:T(8,128)(2,1)}) custom-call(bf16[256,1024]{1,0:T(8,128)(2,1)} %convolution_convert_fusion.7.k_own, bf16[256,1024]{1,0:T(8,128)(2,1)} %convolution_convert_fusion.6.v_own, bf16[256,1024]{1,0:T(8,128)(2,1)} %convolution_convert_fusion.5.k_prev, ...), custom_call_target="tpu_custom_call" | custom-call | tf_op jit(solution)/shard_map/forward/pallas_call | solution.py:121
  77.8 1.4 all-to-all-done.1
  79.2 1.0 copy-done.14
  80.2 3.1 %cotangent.1 = (bf16[256,1024]{1,0:T(8,128)(2,1)}, bf16[1024,256]{1,0:T(8,128)(2,1)}, f32[40,256]{1,0:T(8,128)}) custom-call(bf16[512,1024]{1,0:T(8,128)(2,1)} %bitcast.51, bf16[256,512]{1,0:T(8,128)(2,1)} %fusion.19.pick, f32[1024,256]{1,0:T(8,128)} %get-tuple-element.83.out_t, f32[16,256]{1,0:T(8,128)} %get-tuple-element.84.lse, f32[1,256]{1,0:T(1,128)} %bitcast.58), custom_call_target="tpu_custom_call" | custom-call | tf_op jit(solution)/shard_map/cotangent/pallas_call | solution.py:157
  83.3 1.5 collective-permute-start.7
  84.8 3.0 %collective-permute-done.7 = f32[40,256]{1,0:T(8,128)S(1)} collective-permute-done((f32[40,256]{1,0:T(8,128)}, f32[40,256]{1,0:T(8,128)S(1)}, u32[]{:S(2)}, u32[]{:S(2)}) %collective-permute-start.7) | collective-permute-done | bytes 40992 | tf_op jit(solution)/shard_map/ppermute | solution.py:357
  87.8 0.9 broadcast_in_dim.41
  88.7 4.7 %all-to-all-start.2 = ((f32[8,2,40,256]{3,2,1,0:T(8,128)}), f32[8,2,40,256]{3,2,1,0:T(8,128)S(1)}, u32[]{:S(2)}, u32[]{:S(2)}) async-start(f32[8,2,40,256]{3,2,1,0:T(8,128)} %broadcast_in_dim.41), calls=%async_computation.2 | async-start | bytes 1310720 | tf_op jit(solution)/shard_map/all_to_all | solution.py:360
  94.1 0.8 copy.14.wanted
  94.9 2.7 %fusion.2 = bf16[512,512]{1,0:T(8,128)(2,1)} fusion(s32[512]{0:T(512)S(1)} %get-tuple-element.161, bf16[256,1024]{1,0:T(8,128)(2,1)S(1)} %copy-done.18, bf16[256,1024]{1,0:T(8,128)(2,1)} %copy-done.22), kind=kOutput, calls=%fused_computation.11 | convolution fusion | flops 539754496 | bytes 1574912 | tf_op jit(solution)/shard_map/dot_general | solution.py:54
  98.3 6.0 %all-to-all-done.2 = f32[8,2,40,256]{3,2,1,0:T(8,128)S(1)} async-done(((f32[8,2,40,256]{3,2,1,0:T(8,128)}), f32[8,2,40,256]{3,2,1,0:T(8,128)S(1)}, u32[]{:S(2)}, u32[]{:S(2)}) %all-to-all-start.2) | async-done | bytes 655392 | tf_op jit(solution)/shard_map/all_to_all | solution.py:360
  104.3 0.8 copy-done.15
  105.1 11.1 %backward.1.grads = bf16[2,512,1024]{2,1,0:T(8,128)(2,1)} custom-call(f32[16,40,256]{2,1,0:T(8,128)} %bitcast.55, f32[256,1]{1,0:T(8,128)} %copy.14.wanted, f32[40,256]{1,0:T(8,128)} %get-tuple-element.86.mine, f32[16,256]{1,0:T(8,128)} %get-tuple-element.88.inverse, bf16[16,512,256]{2,1,0:T(8,128)(2,1)} %get-tuple-element.89.probs, ...), custom_call_target="tpu_custom_call" | custom-call | tf_op jit(solution)/shard_map/backward/pallas_call | solution.py:241
  116.2 1.9 fusion.9
  121.9 1.4 collective-permute-done.10.other_v
  123.4 1.5 collective-permute-done.9.other_k
  124.9 1.3 fold.4
  126.8 1.5 collective-permute-start.12
  129.0 0.9 collective-permute-start.13
  130.7 1.5 place_rows.1
  132.2 4.7 %collective-permute-done.13.refs_5_ = bf16[256,512]{1,0:T(8,128)(2,1)S(1)} collective-permute-done((bf16[256,512]{1,0:T(8,128)(2,1)S(1)}, bf16[256,512]{1,0:T(8,128)(2,1)S(1)}, u32[]{:S(2)}, u32[]{:S(2)}) %collective-permute-start.13) | collective-permute-done | bytes 262176 | tf_op jit(solution)/shard_map/ppermute | solution.py:357
  138.8 4.3 %all-to-all-start.3 = ((bf16[8,64,1024]{2,1,0:T(8,128)(2,1)}), bf16[8,64,1024]{2,1,0:T(8,128)(2,1)}, u32[]{:S(2)}, u32[]{:S(2)}) async-start(bf16[8,64,1024]{2,1,0:T(8,128)(2,1)} %bitcast.18), calls=%async_computation.3 | async-start | bytes 2097152 | tf_op jit(solution)/shard_map/all_to_all | solution.py:360
  143.1 1.0 copy-done.3
  144.1 0.9 copy-done.5
  145.1 0.9 copy-done.7
  147.6 1.9 collective-permute-start.14
  149.5 1.5 collective-permute-start.15
  151.0 2.0 %collective-permute-start.16 = (bf16[128,512]{1,0:T(8,128)(2,1)S(1)}, bf16[128,512]{1,0:T(8,128)(2,1)S(1)}, u32[]{:S(2)}, u32[]{:S(2)}) collective-permute-start(bf16[128,512]{1,0:T(8,128)(2,1)S(1)} %get-tuple-element.113), channel_id=1, source_target_pairs={{0,16},{1,17},{2,18},{3,19},{4,20},{5,21},{6,22},{7,23},{8,24},{9,... | collective-permute-start | bytes 393224 | tf_op jit(solution)/shard_map/ppermute | solution.py:357
  153.1 8.1 %collective-permute-done.16.refs_5_ = bf16[128,512]{1,0:T(8,128)(2,1)S(1)} collective-permute-done((bf16[128,512]{1,0:T(8,128)(2,1)S(1)}, bf16[128,512]{1,0:T(8,128)(2,1)S(1)}, u32[]{:S(2)}, u32[]{:S(2)}) %collective-permute-start.16) | collective-permute-done | bytes 131104 | tf_op jit(solution)/shard_map/ppermute | solution.py:357
  161.2 2.2 %collective-permute-done.15.refs_3_ = bf16[128,768]{1,0:T(8,128)(2,1)S(1)} collective-permute-done((bf16[128,768]{1,0:T(8,128)(2,1)S(1)}, bf16[128,768]{1,0:T(8,128)(2,1)S(1)}, u32[]{:S(2)}, u32[]{:S(2)}) %collective-permute-start.15) | collective-permute-done | bytes 196640 | tf_op jit(solution)/shard_map/ppermute | solution.py:357
  163.4 1.8 convolution_convert_fusion.2
  165.3 1.9 collective-permute-done.17
  167.2 1.7 convolution_add_fusion
  168.9 1.3 collective-permute-start.24
  170.3 1.1 collective-permute-start.18
  171.4 2.9 %collective-permute-start.19 = (bf16[64,768]{1,0:T(8,128)(2,1)S(1)}, bf16[64,768]{1,0:T(8,128)(2,1)S(1)}, u32[]{:S(2)}, u32[]{:S(2)}) collective-permute-start(bf16[64,768]{1,0:T(8,128)(2,1)S(1)} %get-tuple-element.130), channel_id=1, source_target_pairs={{0,16},{1,17},{2,18},{3,19},{4,20},{5,21},{6,22},{7,23},{8,24},{9,... | collective-permute-start | bytes 294920 | tf_op jit(solution)/shard_map/ppermute | solution.py:357
  174.3 0.9 collective-permute-start.20
  175.3 3.3 %collective-permute-done.20.refs_5_ = bf16[64,512]{1,0:T(8,128)(2,1)S(1)} collective-permute-done((bf16[64,512]{1,0:T(8,128)(2,1)S(1)}, bf16[64,512]{1,0:T(8,128)(2,1)S(1)}, u32[]{:S(2)}, u32[]{:S(2)}) %collective-permute-start.20) | collective-permute-done | bytes 65568 | tf_op jit(solution)/shard_map/ppermute | solution.py:357
  179.0 9.1 %collective-permute-done.19.refs_3_ = bf16[64,768]{1,0:T(8,128)(2,1)S(1)} collective-permute-done((bf16[64,768]{1,0:T(8,128)(2,1)S(1)}, bf16[64,768]{1,0:T(8,128)(2,1)S(1)}, u32[]{:S(2)}, u32[]{:S(2)}) %collective-permute-start.19) | collective-permute-done | bytes 98336 | tf_op jit(solution)/shard_map/ppermute | solution.py:357
  188.2 1.5 collective-permute-start.22
  189.7 1.5 collective-permute-start.23
  191.2 0.8 fusion.8
  192.0 1.7 collective-permute-done.23
  (109 shorter events, 17.3 us)
Async XLA Ops:
  0.6 52.0 %copy-start = (bf16[1024,1024]{1,0:T(8,128)(2,1)S(1)}, bf16[1024,1024]{1,0:T(8,128)(2,1)}, u32[]{:S(2)}) copy-start(bf16[1024,1024]{1,0:T(8,128)(2,1)} %param.12) | copy-start | bytes 6291460
  0.6 21.8 %copy-start.16 = (bf16[256,1024]{1,0:T(8,128)(2,1)S(1)}, bf16[256,1024]{1,0:T(8,128)(2,1)}, u32[]{:S(2)}) copy-start(bf16[256,1024]{1,0:T(8,128)(2,1)} %param.10) | copy-start | bytes 1572868
  2.6 17.5 %collective-permute-start.1 = (bf16[144,1024]{1,0:T(8,128)(2,1)S(1)}, bf16[144,1024]{1,0:T(8,128)(2,1)}, u32[]{:S(2)}, u32[]{:S(2)}) collective-permute-start(bf16[144,1024]{1,0:T(8,128)(2,1)S(1)} %pad_maximum_fusion.3), channel_id=1, source_target_pairs={{0,16},{1,17},{2,18},{3,19},{4,20},{5,21},{6,22},{7,23},{8,24},{9,... | collective-permute-start | bytes 884744 | tf_op jit(solution)/shard_map/ppermute | solution.py:357
  6.7 18.7 %collective-permute-start = (s32[256]{0:T(256)}, s32[256]{0:T(256)S(1)}, u32[]{:S(2)}, u32[]{:S(2)}) collective-permute-start(s32[256]{0:T(256)} %bitcast.62), channel_id=1, source_target_pairs={{0,0},{1,1},{14,2},{19,3},{30,4},{3,5},{16,6},{17,7},{2,8},{31,9},... | collective-permute-start | bytes 3080 | tf_op jit(solution)/shard_map/ppermute | solution.py:357
  22.2 1.6 collective-permute-start.2
  25.3 23.4 %all-to-all-start = ((bf16[8,64,1024]{2,1,0:T(8,128)(2,1)}), bf16[8,64,1024]{2,1,0:T(8,128)(2,1)S(1)}, u32[]{:S(2)}, u32[]{:S(2)}) async-start(bf16[8,64,1024]{2,1,0:T(8,128)(2,1)} %bitcast.53), calls=%async_computation | async-start | bytes 2097152 | tf_op jit(solution)/shard_map/all_to_all | solution.py:360
  29.4 19.9 %collective-permute-start.4 = (bf16[128,1024]{1,0:T(8,128)(2,1)S(1)}, bf16[128,1024]{1,0:T(8,128)(2,1)}, u32[]{:S(2)}, u32[]{:S(2)}) collective-permute-start(bf16[128,1024]{1,0:T(8,128)(2,1)S(1)} %constant_dynamic-slice_fusion), channel_id=1, source_target_pairs={{0,16},{1,17},{2,18},{3,19},{4,20},{5,21},{6,22},{7,23},{8,24},{9,... | collective-permute-start | bytes 786440 | tf_op jit(solution)/shard_map/ppermute | solution.py:357
  49.2 5.0 %copy-start.17 = (bf16[256,1024]{1,0:T(8,128)(2,1)}, bf16[256,1024]{1,0:T(8,128)(2,1)S(1)}, u32[]{:S(2)}) copy-start(bf16[256,1024]{1,0:T(8,128)(2,1)S(1)} %convolution_convert_fusion.3) | copy-start | bytes 1572868
  49.3 9.2 %collective-permute-start.3 = (bf16[256,1024]{1,0:T(8,128)(2,1)S(1)}, bf16[256,1024]{1,0:T(8,128)(2,1)S(1)}, u32[]{:S(2)}, u32[]{:S(2)}) collective-permute-start(bf16[256,1024]{1,0:T(8,128)(2,1)S(1)} %convolution_convert_fusion.3), channel_id=1, source_target_pairs={{0,8},{1,5},{8,16},{5,13},{16,24},{13,21},{24,26},{21,29},{26,18},... | collective-permute-start | bytes 1572872 | tf_op jit(solution)/shard_map/ppermute | solution.py:357
  49.3 4.9 %collective-permute-start.5 = (bf16[128,1024]{1,0:T(8,128)(2,1)}, bf16[128,1024]{1,0:T(8,128)(2,1)S(1)}, u32[]{:S(2)}, u32[]{:S(2)}) collective-permute-start(bf16[128,1024]{1,0:T(8,128)(2,1)} %collective-permute-done.4), channel_id=1, source_target_pairs={{0,1},{1,0},{2,3},{3,2},{4,5},{5,4},{6,7},{7,6},{8,9},{9,8},{10,11... | collective-permute-start | bytes 786440 | tf_op jit(solution)/shard_map/ppermute | solution.py:357
  52.7 1.6 copy-start.13
  58.5 0.8 copy-start.22
  59.3 19.9 %all-to-all-start.1 = ((bf16[8,64,1024]{2,1,0:T(8,128)(2,1)}), bf16[8,64,1024]{2,1,0:T(8,128)(2,1)S(1)}, u32[]{:S(2)}, u32[]{:S(2)}) async-start(bf16[8,64,1024]{2,1,0:T(8,128)(2,1)} %bitcast.54), calls=%async_computation.1 | async-start | bytes 2097152 | tf_op jit(solution)/shard_map/all_to_all | solution.py:360
  63.9 4.7 %copy-start.23 = (bf16[256,1024]{1,0:T(8,128)(2,1)S(1)}, bf16[256,1024]{1,0:T(8,128)(2,1)}, u32[]{:S(2)}) copy-start(bf16[256,1024]{1,0:T(8,128)(2,1)} %copy-done.22) | copy-start | bytes 1572868
  79.2 1.0 copy-start.14
  80.2 13.9 %copy-start.20 = (f32[256]{0:T(256)S(1)}, f32[256]{0:T(256)}, u32[]{:S(2)}) copy-start(f32[256]{0:T(256)} %convert_element_type.122) | copy-start | bytes 3076
  83.3 11.6 %copy-start.18 = (bf16[256,1024]{1,0:T(8,128)(2,1)S(1)}, bf16[256,1024]{1,0:T(8,128)(2,1)}, u32[]{:S(2)}) copy-start(bf16[256,1024]{1,0:T(8,128)(2,1)} %copy-done.17) | copy-start | bytes 1572868
  83.3 1.5 collective-permute-start.6
  83.3 4.5 %collective-permute-start.7 = (f32[40,256]{1,0:T(8,128)}, f32[40,256]{1,0:T(8,128)S(1)}, u32[]{:S(2)}, u32[]{:S(2)}) collective-permute-start(f32[40,256]{1,0:T(8,128)} %get-tuple-element.86.mine), channel_id=1, source_target_pairs={{0,17},{1,16},{2,19},{3,18},{4,21},{5,20},{6,23},{7,22},{8,25},{9,... | collective-permute-start | bytes 122888 | tf_op jit(solution)/shard_map/ppermute | solution.py:357
  88.7 15.6 %all-to-all-start.2 = ((f32[8,2,40,256]{3,2,1,0:T(8,128)}), f32[8,2,40,256]{3,2,1,0:T(8,128)S(1)}, u32[]{:S(2)}, u32[]{:S(2)}) async-start(f32[8,2,40,256]{3,2,1,0:T(8,128)} %broadcast_in_dim.41), calls=%async_computation.2 | async-start | bytes 1310720 | tf_op jit(solution)/shard_map/all_to_all | solution.py:360
  94.9 2.7 %copy-start.19 = (bf16[256,1024]{1,0:T(8,128)(2,1)S(1)}, bf16[256,1024]{1,0:T(8,128)(2,1)}, u32[]{:S(2)}) copy-start(bf16[256,1024]{1,0:T(8,128)(2,1)} %copy-done.17) | copy-start | bytes 1572868
  94.9 2.7 %copy-start.21 = (s32[512]{0:T(512)S(1)}, s32[512]{0:T(512)}, u32[]{:S(2)}) copy-start(s32[512]{0:T(512)} %get-tuple-element.162) | copy-start | bytes 6148
  94.9 2.7 %copy-start.24 = (bf16[256,1024]{1,0:T(8,128)(2,1)S(1)}, bf16[256,1024]{1,0:T(8,128)(2,1)}, u32[]{:S(2)}) copy-start(bf16[256,1024]{1,0:T(8,128)(2,1)} %copy-done.22) | copy-start | bytes 1572868
  104.3 0.8 copy-start.15
  105.1 13.0 %copy-start.12 = (bf16[1024,1024]{1,0:T(8,128)(2,1)S(1)}, bf16[1024,1024]{1,0:T(8,128)(2,1)}, u32[]{:S(2)}) copy-start(bf16[1024,1024]{1,0:T(8,128)(2,1)} %param.13) | copy-start | bytes 6291460
  116.2 2.0 %copy-start.1 = (bf16[2,512,1024]{2,1,0:T(8,128)(2,1)S(1)}, bf16[2,512,1024]{2,1,0:T(8,128)(2,1)}, u32[]{:S(2)}) copy-start(bf16[2,512,1024]{2,1,0:T(8,128)(2,1)} %backward.1.grads) | copy-start | bytes 6291460
  118.2 1.0 copy-start.25
  120.7 2.7 %collective-permute-start.10 = (bf16[512,1024]{1,0:T(8,128)(2,1)S(1)}, bf16[512,1024]{1,0:T(8,128)(2,1)S(1)}, u32[]{:S(2)}, u32[]{:S(2)}) collective-permute-start(bf16[512,1024]{1,0:T(8,128)(2,1)S(1)} %convolution_convert_fusion), channel_id=1, source_target_pairs={{0,1},{1,0},{2,3},{3,2},{4,5},{5,4},{6,7},{7,6},{8,9},{9,8},{10,11... | collective-permute-start | bytes 3145736 | tf_op jit(solution)/shard_map/ppermute | solution.py:357
  120.7 4.1 %collective-permute-start.9 = (bf16[512,1024]{1,0:T(8,128)(2,1)S(1)}, bf16[512,1024]{1,0:T(8,128)(2,1)S(1)}, u32[]{:S(2)}, u32[]{:S(2)}) collective-permute-start(bf16[512,1024]{1,0:T(8,128)(2,1)S(1)} %convolution_convert_fusion.1), channel_id=1, source_target_pairs={{0,1},{1,0},{2,3},{3,2},{4,5},{5,4},{6,7},{7,6},{8,9},{9,8},{10,11... | collective-permute-start | bytes 3145736 | tf_op jit(solution)/shard_map/ppermute | solution.py:357
  121.3 9.4 %collective-permute-start.8 = (bf16[256,1024]{1,0:T(8,128)(2,1)S(1)}, bf16[256,1024]{1,0:T(8,128)(2,1)S(1)}, u32[]{:S(2)}, u32[]{:S(2)}) collective-permute-start(bf16[256,1024]{1,0:T(8,128)(2,1)S(1)} %fusion.5), channel_id=1, source_target_pairs={{8,0},{5,1},{16,8},{13,5},{24,16},{21,13},{26,24},{29,21},{18,26},... | collective-permute-start | bytes 1572872 | tf_op jit(solution)/shard_map/ppermute | solution.py:357
  126.1 4.5 %copy-start.4 = (bf16[256,512]{1,0:T(8,128)(2,1)}, bf16[256,512]{1,0:T(8,128)(2,1)S(1)}, u32[]{:S(2)}) copy-start(bf16[256,512]{1,0:T(8,128)(2,1)S(1)} %get-tuple-element.106.refs_4_) | copy-start | bytes 786436
  126.2 11.4 %collective-permute-start.11 = (bf16[256,768]{1,0:T(8,128)(2,1)S(1)}, bf16[256,768]{1,0:T(8,128)(2,1)S(1)}, u32[]{:S(2)}, u32[]{:S(2)}) collective-permute-start(bf16[256,768]{1,0:T(8,128)(2,1)S(1)} %get-tuple-element.96), channel_id=1, source_target_pairs={{0,2},{1,3},{2,0},{3,1},{4,6},{5,7},{6,4},{7,5},{8,10},{9,11},{10,... | collective-permute-start | bytes 1179656 | tf_op jit(solution)/shard_map/ppermute | solution.py:357
  126.8 11.3 %collective-permute-start.12 = (bf16[256,768]{1,0:T(8,128)(2,1)S(1)}, bf16[256,768]{1,0:T(8,128)(2,1)S(1)}, u32[]{:S(2)}, u32[]{:S(2)}) collective-permute-start(bf16[256,768]{1,0:T(8,128)(2,1)S(1)} %get-tuple-element.98), channel_id=1, source_target_pairs={{0,4},{1,5},{2,6},{3,7},{4,0},{5,1},{6,2},{7,3},{8,12},{9,13},{10,... | collective-permute-start | bytes 1179656 | tf_op jit(solution)/shard_map/ppermute | solution.py:357
  129.0 7.9 %collective-permute-start.13 = (bf16[256,512]{1,0:T(8,128)(2,1)S(1)}, bf16[256,512]{1,0:T(8,128)(2,1)S(1)}, u32[]{:S(2)}, u32[]{:S(2)}) collective-permute-start(bf16[256,512]{1,0:T(8,128)(2,1)S(1)} %get-tuple-element.100), channel_id=1, source_target_pairs={{0,8},{1,9},{2,10},{3,11},{4,12},{5,13},{6,14},{7,15},{8,0},{9,1},... | collective-permute-start | bytes 786440 | tf_op jit(solution)/shard_map/ppermute | solution.py:357
  136.9 0.7 copy-start.6
  138.1 0.8 copy-start.2
  138.8 24.6 %all-to-all-start.3 = ((bf16[8,64,1024]{2,1,0:T(8,128)(2,1)}), bf16[8,64,1024]{2,1,0:T(8,128)(2,1)}, u32[]{:S(2)}, u32[]{:S(2)}) async-start(bf16[8,64,1024]{2,1,0:T(8,128)(2,1)} %bitcast.18), calls=%async_computation.3 | async-start | bytes 2097152 | tf_op jit(solution)/shard_map/all_to_all | solution.py:360
  143.1 1.0 copy-start.3
  144.1 0.9 copy-start.5
  145.1 0.9 copy-start.7
  146.2 0.7 copy-start.8
  146.9 0.7 copy-start.10
  147.6 13.6 %collective-permute-start.14 = (bf16[128,768]{1,0:T(8,128)(2,1)S(1)}, bf16[128,768]{1,0:T(8,128)(2,1)S(1)}, u32[]{:S(2)}, u32[]{:S(2)}) collective-permute-start(bf16[128,768]{1,0:T(8,128)(2,1)S(1)} %get-tuple-element.109), channel_id=1, source_target_pairs={{0,4},{1,5},{2,6},{3,7},{4,0},{5,1},{6,2},{7,3},{8,12},{9,13},{10,... | collective-permute-start | bytes 589832 | tf_op jit(solution)/shard_map/ppermute | solution.py:357
  149.5 13.9 %collective-permute-start.15 = (bf16[128,768]{1,0:T(8,128)(2,1)S(1)}, bf16[128,768]{1,0:T(8,128)(2,1)S(1)}, u32[]{:S(2)}, u32[]{:S(2)}) collective-permute-start(bf16[128,768]{1,0:T(8,128)(2,1)S(1)} %get-tuple-element.111), channel_id=1, source_target_pairs={{0,8},{1,9},{2,10},{3,11},{4,12},{5,13},{6,14},{7,15},{8,0},{9,1},... | collective-permute-start | bytes 589832 | tf_op jit(solution)/shard_map/ppermute | solution.py:357
  151.0 10.2 %collective-permute-start.16 = (bf16[128,512]{1,0:T(8,128)(2,1)S(1)}, bf16[128,512]{1,0:T(8,128)(2,1)S(1)}, u32[]{:S(2)}, u32[]{:S(2)}) collective-permute-start(bf16[128,512]{1,0:T(8,128)(2,1)S(1)} %get-tuple-element.113), channel_id=1, source_target_pairs={{0,16},{1,17},{2,18},{3,19},{4,20},{5,21},{6,22},{7,23},{8,24},{9,... | collective-permute-start | bytes 393224 | tf_op jit(solution)/shard_map/ppermute | solution.py:357
  163.4 6.8 %copy-start.9 = (bf16[128,768]{1,0:T(8,128)(2,1)S(1)}, bf16[128,768]{1,0:T(8,128)(2,1)}, u32[]{:S(2)}) copy-start(bf16[128,768]{1,0:T(8,128)(2,1)} %copy-done.8) | copy-start | bytes 589828
  163.4 6.8 %copy-start.11 = (bf16[128,768]{1,0:T(8,128)(2,1)S(1)}, bf16[128,768]{1,0:T(8,128)(2,1)}, u32[]{:S(2)}) copy-start(bf16[128,768]{1,0:T(8,128)(2,1)} %copy-done.10) | copy-start | bytes 589828
  165.2 2.0 %collective-permute-start.17 = (bf16[256,1024]{1,0:T(8,128)(2,1)S(1)}, bf16[256,1024]{1,0:T(8,128)(2,1)S(1)}, u32[]{:S(2)}, u32[]{:S(2)}) collective-permute-start(bf16[256,1024]{1,0:T(8,128)(2,1)S(1)} %convolution_convert_fusion.2), channel_id=1, source_target_pairs={{0,1},{1,0},{2,3},{3,2},{4,5},{5,4},{6,7},{7,6},{8,9},{9,8},{10,11... | collective-permute-start | bytes 1572872 | tf_op jit(solution)/shard_map/ppermute | solution.py:357
  168.9 22.3 %collective-permute-start.24 = (bf16[128,1024]{1,0:T(8,128)(2,1)S(1)}, bf16[128,1024]{1,0:T(8,128)(2,1)S(1)}, u32[]{:S(2)}, u32[]{:S(2)}) collective-permute-start(bf16[128,1024]{1,0:T(8,128)(2,1)S(1)} %slice.86), channel_id=1, source_target_pairs={{0,16},{1,17},{2,18},{3,19},{4,20},{5,21},{6,22},{7,23},{8,24},{9,... | collective-permute-start | bytes 786440 | tf_op jit(solution)/shard_map/ppermute | solution.py:357
  170.3 8.7 %collective-permute-start.18 = (bf16[64,768]{1,0:T(8,128)(2,1)S(1)}, bf16[64,768]{1,0:T(8,128)(2,1)S(1)}, u32[]{:S(2)}, u32[]{:S(2)}) collective-permute-start(bf16[64,768]{1,0:T(8,128)(2,1)S(1)} %get-tuple-element.128), channel_id=1, source_target_pairs={{0,8},{1,9},{2,10},{3,11},{4,12},{5,13},{6,14},{7,15},{8,0},{9,1},... | collective-permute-start | bytes 294920 | tf_op jit(solution)/shard_map/ppermute | solution.py:357
  171.4 16.6 %collective-permute-start.19 = (bf16[64,768]{1,0:T(8,128)(2,1)S(1)}, bf16[64,768]{1,0:T(8,128)(2,1)S(1)}, u32[]{:S(2)}, u32[]{:S(2)}) collective-permute-start(bf16[64,768]{1,0:T(8,128)(2,1)S(1)} %get-tuple-element.130), channel_id=1, source_target_pairs={{0,16},{1,17},{2,18},{3,19},{4,20},{5,21},{6,22},{7,23},{8,24},{9,... | collective-permute-start | bytes 294920 | tf_op jit(solution)/shard_map/ppermute | solution.py:357
  174.3 4.3 %collective-permute-start.20 = (bf16[64,512]{1,0:T(8,128)(2,1)S(1)}, bf16[64,512]{1,0:T(8,128)(2,1)S(1)}, u32[]{:S(2)}, u32[]{:S(2)}) collective-permute-start(bf16[64,512]{1,0:T(8,128)(2,1)S(1)} %get-tuple-element.132), channel_id=1, source_target_pairs={{0,2},{1,3},{2,0},{3,1},{4,6},{5,7},{6,4},{7,5},{8,10},{9,11},{10,... | collective-permute-start | bytes 196616 | tf_op jit(solution)/shard_map/ppermute | solution.py:357
  188.1 5.5 %collective-permute-start.21 = (bf16[32,768]{1,0:T(8,128)(2,1)S(1)}, bf16[32,768]{1,0:T(8,128)(2,1)S(1)}, u32[]{:S(2)}, u32[]{:S(2)}) collective-permute-start(bf16[32,768]{1,0:T(8,128)(2,1)S(1)} %get-tuple-element.134), channel_id=1, source_target_pairs={{0,16},{1,17},{2,18},{3,19},{4,20},{5,21},{6,22},{7,23},{8,24},{9,... | collective-permute-start | bytes 147464 | tf_op jit(solution)/shard_map/ppermute | solution.py:357
  188.2 5.5 %collective-permute-start.22 = (bf16[32,768]{1,0:T(8,128)(2,1)S(1)}, bf16[32,768]{1,0:T(8,128)(2,1)S(1)}, u32[]{:S(2)}, u32[]{:S(2)}) collective-permute-start(bf16[32,768]{1,0:T(8,128)(2,1)S(1)} %get-tuple-element.136), channel_id=1, source_target_pairs={{0,2},{1,3},{2,0},{3,1},{4,6},{5,7},{6,4},{7,5},{8,10},{9,11},{10,... | collective-permute-start | bytes 147464 | tf_op jit(solution)/shard_map/ppermute | solution.py:357
  189.7 3.9 %collective-permute-start.23 = (bf16[32,512]{1,0:T(8,128)(2,1)S(1)}, bf16[32,512]{1,0:T(8,128)(2,1)S(1)}, u32[]{:S(2)}, u32[]{:S(2)}) collective-permute-start(bf16[32,512]{1,0:T(8,128)(2,1)S(1)} %get-tuple-element.138), channel_id=1, source_target_pairs={{0,4},{1,5},{2,6},{3,7},{4,0},{5,1},{6,2},{7,3},{8,12},{9,13},{10,... | collective-permute-start | bytes 98312 | tf_op jit(solution)/shard_map/ppermute | solution.py:357
